TPU v7x, 32 devices: a whole 2x2x4 slice. The times are simulated.
32 devices in a mesh: dp: 8 (over z, x), expert: 4 (over y, core).
Axes of the slice: x: 2, y: 2, z: 4, core: 2. Of those that a mesh axis runs over, the one named last changes fastest.
Arguments:
- out_grad: bfloat16 [4096, 4096], P(('dp', 'expert')), may hold values from -6 to 6
- expert_ids: int32 [4096, 4], P(('dp', 'expert')), may hold values from 0 to 15, all different within a row; in each aligned block of 128 rows (0 to 127, 128 to 255, ...) at most 48 rows name the same one
- gate_weights: bfloat16 [4096, 4], P(('dp', 'expert')), may hold values from 0.019897461 to 0.5
- saved_acts: bfloat16 [8, 4, 16, 48, 1536], P('dp', None, 'expert'), may hold values from -8 to 8
- down_weight: bfloat16 [16, 4096, 768], P('expert', 'dp'), may hold values from -0.09375 to 0.09375
Outputs:
- pre_grads: bfloat16 [8, 4, 16, 48, 1536], P('dp', None, 'expert')
- down_grad: bfloat16 [16, 4096, 768], P('expert', 'dp')
- gate_grad: float32 [4096, 4], P(('dp', 'expert'))
Inputs may be any that keep to these rules, and one draw needn't show every extreme that they name: `expert_ids`: each token names 4 different experts; among the 128 tokens of one device no expert is named by more than 48 tokens, a bound that some block reaches.
All inputs are finite; a program needn't handle non-finite values.
Results may differ from a plain program's by a relative error of at most 0.0057.
Values may be sent and summed in bfloat16 or wider, within the bound.
No kernel may reach another device: no remote copies, remote signals or barrier semaphores. Data moves between devices by JAX's collectives and lax.ppermute only.
A program may use at most 192 MiB of HBM per device.

v0:
```python
import jax
import jax.numpy as jnp
from jax import lax
from jax.sharding import PartitionSpec as P

EXPERTS = 16
CAP = 48


def slot_numbers(choice_rows):
    hits = jnp.sum(
        (choice_rows[:, :, None] == jnp.arange(EXPERTS, dtype=jnp.int32)[None, None, :]).astype(
            jnp.int32
        ),
        axis=1,
    )
    before = jnp.cumsum(hits, axis=0) - hits
    return jnp.take_along_axis(before, choice_rows, axis=1)


def shards(out_grad, expert_ids, gate_weights, saved_acts, down_weight):
    sources = lax.axis_size("expert")
    local_count = down_weight.shape[0]
    hidden_width = down_weight.shape[2]
    width = out_grad.shape[1]
    tok_rows = out_grad.shape[0]
    top_count = expert_ids.shape[1]
    own_slots = slot_numbers(expert_ids)
    own_target = expert_ids * CAP + own_slots
    total_slots = sources * local_count * CAP
    flat_target = own_target.reshape(-1)
    copies = jnp.broadcast_to(out_grad[:, None, :], (tok_rows, top_count, width)).reshape(-1, width)
    outgoing = jnp.zeros((total_slots, width), jnp.bfloat16).at[flat_target].set(copies)
    outgoing = outgoing.reshape(sources, local_count, CAP, width)
    gate_out = jnp.zeros((total_slots,), jnp.bfloat16).at[flat_target].set(gate_weights.reshape(-1))
    gate_out = gate_out.reshape(sources, local_count, CAP)
    routed, gate_slot = (
        lax.all_to_all(outgoing, "expert", split_axis=0, concat_axis=0, tiled=True),
        lax.all_to_all(gate_out, "expert", split_axis=0, concat_axis=0, tiled=True),
    )
    saved = saved_acts[0]
    gate_pre = saved[..., :hidden_width].astype(jnp.float32)
    up_pre = saved[..., hidden_width:].astype(jnp.float32)
    sigma = jax.nn.sigmoid(gate_pre)
    silu_val = gate_pre * sigma
    act = silu_val * up_pre
    act_low = act.astype(jnp.bfloat16)
    back = jnp.einsum(
        "slcd,ldf->slcf",
        routed,
        lax.all_gather(down_weight, "dp", axis=1, tiled=True),
        preferred_element_type=jnp.float32,
    )
    score = jnp.sum(back * act, axis=3)
    gate_f = gate_slot.astype(jnp.float32)[..., None]
    grad_act = gate_f * back
    d_gate = grad_act * up_pre * sigma * (1.0 + gate_pre * (1.0 - sigma))
    d_up = grad_act * silu_val
    pre_grads = jnp.concatenate([d_gate, d_up], axis=3).astype(jnp.bfloat16)[None]
    weighted = (gate_f * routed.astype(jnp.float32)).astype(jnp.bfloat16)
    summed = lax.psum_scatter(
        jnp.einsum("slcd,slcf->dlf", weighted, act_low, preferred_element_type=jnp.float32),
        "dp",
        scatter_dimension=0,
        tiled=True,
    )
    down_grad = jnp.transpose(summed, (1, 0, 2)).astype(jnp.bfloat16)
    returned = lax.all_to_all(score, "expert", split_axis=0, concat_axis=0, tiled=True)
    gate_grad = jnp.take(returned.reshape(-1), own_target.reshape(-1)).reshape(tok_rows, top_count)
    return (pre_grads, down_grad, gate_grad)


def solution(mesh):
    placed = (
        P(("dp", "expert"), None),
        P(("dp", "expert"), None),
        P(("dp", "expert"), None),
        P("dp", None, "expert", None, None),
        P("expert", "dp", None),
    )
    return jax.shard_map(
        shards,
        mesh=mesh,
        in_specs=placed,
        out_specs=(
            P("dp", None, "expert", None, None),
            P("expert", "dp", None),
            P(("dp", "expert"), None),
        ),
        check_vma=False,
    )
```

profile of v0, /device:TPU:0, one launch (start us, length us, event | category | flops | bytes accessed | tf_op | source)
XLA Modules:
  0.0 1299.8 jit_solution(16462456834012310413)
XLA Ops:
  7.2 0.7 all-gather.2.cloned.1.call-update
  8.7 3.8 gather_fusion.1
  13.0 3.8 scatter_custom_fusion
  16.7 0.7 reshape.107
  17.4 4.2 all-to-all-start
  21.7 4.0 broadcast_in_dim.31
  25.7 6.9 reshape.137
  32.6 11.4 scatter_custom_fusion.1
  44.1 5.4 all-to-all-start.1
  49.8 1.6 copy.119
  51.4 68.8 %all-to-all-done.1 = bf16[4,4,48,4096]{3,2,1,0:T(8,128)(2,1)} async-done(((bf16[4,4,48,4096]{3,2,1,0:T(8,128)(2,1)}), bf16[4,4,48,4096]{3,2,1,0:T(8,128)(2,1)}, u32[]{:S(2)}, u32[]{:S(2)}) %all-to-all-start.1) | async-done | bytes 6291488 | tf_op jit(solution)/shard_map/all_to_all | solution.py:38
  120.2 21.7 %convolution_bitcast_fusion = f32[4096,4,768]{0,2,1:T(8,128)} fusion(bf16[4,4,48,1536]{3,2,0,1:T(8,128)(2,1)} %bitcast.43, bf16[4,4,48,4096]{3,2,1,0:T(8,128)(2,1)} %all-to-all-done.1, f32[4,4,48]{2,1,0:T(4,128)S(1)} %convert_element_type.36), kind=kOutput, calls=%fused_computation.6 | convolution fusion | flops 4845993984 | bytes 58985472 | tf_op jit(solution)/shard_map/slcd,slcf->dlf/dot_general | solution.py:62
  142.0 350.7 %all-gather.2.cloned.1.call-done = bf16[4,4096,768]{2,1,0:T(8,128)(2,1)} async-done(((bf16[4,512,768]{2,1,0:T(8,128)(2,1)}), bf16[4,4096,768]{2,1,0:T(8,128)(2,1)}) %all-gather.2.cloned.1.call-update) | async-done | bytes 25165840 | tf_op jit(solution)/shard_map/all_gather | solution.py:51
  492.7 15.7 %fusion.17 = (bf16[1,4,4,48,768]{4,3,1,2,0:T(8,128)(2,1)S(1)}, bf16[1,4,4,48,768]{4,3,1,2,0:T(8,128)(2,1)}, f32[4,4,48]{2,0,1:T(4,128)}) fusion(f32[4,4,48]{2,0,1:T(4,128)S(1)} %copy.102, bf16[4,4,48,1536]{3,2,0,1:T(8,128)(2,1)S(1)} %bitcast.44, bf16[4,4096,768]{2,1,0:T(8,128)(2,1)} %all-gather.2.cloned.1.call-done, bf16[4,4,48,4096]{3,2,1,0:T(8,128)(2,1)} %all-to-all-done.1), kind=kOutput, calls=%fused_computation.33 | convolution fusion | flops 4843043840 | bytes 36182016 | tf_op jit(solution)/shard_map/slcd,ldf->slcf/dot_general | solution.py:48
  508.4 0.7 copy.106
  509.1 0.7 reshape.152
  509.8 3.2 all-to-all-start.2
  513.0 1.5 pad_maximum_fusion
  514.5 1.6 copy.108
  517.3 0.7 reduce
  518.1 2.3 gather_fusion
  521.2 765.8 %reduce-scatter.2.cloned.1.call-done = f32[512,4,768]{0,2,1:T(8,128)} async-done(((f32[4096,4,768]{0,2,1:T(8,128)}), f32[512,4,768]{0,2,1:T(8,128)}) %reduce-scatter.2.cloned.1.call-update) | async-done | bytes 6291472 | tf_op jit(solution)/shard_map/reduce_scatter | solution.py:61
  1287.0 3.2 convert_bitcast_fusion
  1290.2 2.8 copy.109
  (39 shorter events, 3.6 us)
Async XLA Ops:
  7.2 0.8 copy-start.4
  7.2 1.0 copy-start.3
  7.2 485.5 %all-gather.2.cloned.1.call-start = ((), (), s32[]{:S(2)}) async-start(), calls=%async_computation.4 | async-start | bytes 28311552 | tf_op jit(solution)/shard_map/all_gather | solution.py:51
  8.7 12.9 copy-start.2
  17.4 26.7 %all-to-all-start = ((bf16[4,4,48]{2,1,0:T(4,128)(2,1)}), bf16[4,4,48]{2,1,0:T(4,128)(2,1)S(1)}, u32[]{:S(2)}, u32[]{:S(2)}) async-start(bf16[4,4,48]{2,1,0:T(4,128)(2,1)} %reshape.107), calls=%async_computation | async-start | bytes 8192 | tf_op jit(solution)/shard_map/all_to_all | solution.py:39
  44.1 5.7 copy-start
  44.1 76.1 %all-to-all-start.1 = ((bf16[4,4,48,4096]{3,2,1,0:T(8,128)(2,1)}), bf16[4,4,48,4096]{3,2,1,0:T(8,128)(2,1)}, u32[]{:S(2)}, u32[]{:S(2)}) async-start(bf16[4,4,48,4096]{3,2,1,0:T(8,128)(2,1)} %bitcast.42), calls=%async_computation.1 | async-start | bytes 12582912 | tf_op jit(solution)/shard_map/all_to_all | solution.py:38
  49.5 1237.5 %reduce-scatter.2.cloned.1.call-start = ((), (), s32[]{:S(2)}) async-start(), calls=%async_computation.5 | async-start | bytes 56623104 | tf_op jit(solution)/shard_map/reduce_scatter | solution.py:61
  141.9 350.8 %copy-start.1 = (bf16[1,4,4,48,1536]{4,3,1,2,0:T(8,128)(2,1)S(1)}, bf16[1,4,4,48,1536]{4,3,1,2,0:T(8,128)(2,1)}, u32[]{:S(2)}) copy-start(bf16[1,4,4,48,1536]{4,3,1,2,0:T(8,128)(2,1)} %copy.119) | copy-start | bytes 7077892
  509.8 7.0 all-to-all-start.2
Sparse Core Ops, SparseCore 0:
  9.6 483.1 all-gather.1
  496.6 790.3 reduce-scatter.1
where the time goes:
time: 1300 us
  waiting for transfers between devices  1190 us (92%)
  local copies, waits for them, and re-layouts  42.1 us (3%)
  matrix products  37.4 us (3%)
  between operations  14.2 us (1%)
  starting transfers between devices  13.2 us (1%)
    reduce_scatter x1, waiting for transfers between devices, shards(): lax.psum_scatter(jnp.einsum('slcd,slcf->dlf', weighted, act_low, preferre...  766 us
    all_gather x1, waiting for transfers between devices, shards(): lax.all_gather(down_weight, 'dp', axis=1, tiled=True)  351 us
    all_to_all x1, waiting for transfers between devices, shards(): lax.all_to_all(outgoing, 'expert', split_axis=0, concat_axis=0, tiled=True)  68.8 us
  transfers between devices with their start and end apart: 5, of which 4 were waited for; matrix products, arithmetic and copies ran while one was open for 6% of the time, Pallas kernels for 0%

commit v1 on v0

v1 whole, which is shorter than its diff:
```python
import functools

import jax
import jax.numpy as jnp
from jax import lax
from jax.experimental import pallas as pl
from jax.experimental.pallas import tpu as pltpu
from jax.sharding import PartitionSpec as P

EXPERTS = 16
CAP = 48
META = 16
NONE = 255.0
BF = jnp.bfloat16
F32 = jnp.float32


def params(mib):
    return pltpu.CompilerParams(vmem_limit_bytes=mib * 1024 * 1024)


def dot(a, b):
    return jnp.dot(a, b, preferred_element_type=F32)


def dot_t(a, b):
    return lax.dot_general(a, b, (((0,), (0,)), ((), ())), preferred_element_type=F32)


def named(ids, rows):
    experts = lax.broadcasted_iota(jnp.int32, (rows, EXPERTS), 1)
    return [(ids[:, k : k + 1] == experts).astype(F32) for k in range(ids.shape[1])]


def pack_kernel(rows, part, idx, grad_ref, ids_ref, gates_ref, *outs):
    cols = named(ids_ref[...], rows)
    gates = gates_ref[...].astype(F32)
    hit = sum(cols)
    gate = sum(c * gates[:, k : k + 1] for k, c in enumerate(cols))
    r = lax.broadcasted_iota(jnp.int32, (rows, rows), 0)
    c = lax.broadcasted_iota(jnp.int32, (rows, rows), 1)
    earlier, eye = (r < c).astype(BF), (r == c).astype(BF)
    before = dot_t(hit.astype(BF), earlier)
    hit_t = dot_t(hit.astype(BF), eye)
    gate_t = dot_t(gate.astype(BF), eye)
    slots = jnp.where(hit_t > 0.5, before, NONE)
    z = idx[0]
    for k, out in enumerate(outs):
        at = pl.multiple_of((z ^ k) * part, 128)
        out[0:rows, :] = grad_ref[:, pl.ds(at, part)]
        out[rows : rows + META, :] = jnp.zeros((META, part), BF)
        out[rows : rows + META, 0:rows] = slots.astype(BF)
        out[rows : rows + META, rows : 2 * rows] = gate_t.astype(BF)


def act_kernel(half, idx, saved_ref, keep_ref, send_ref):
    x = idx[1]
    width = 2 * half
    for out, side in ((send_ref, 1 - x), (keep_ref, x)):
        at = pl.multiple_of(side * half, 128)
        for e in range(saved_ref.shape[2]):
            g = saved_ref[0, 0, e, :, pl.ds(at, half)].astype(F32)
            u = saved_ref[0, 0, e, :, pl.ds(pl.multiple_of(width + at, 128), half)].astype(F32)
            out[e] = (g * lax.logistic(g) * u).astype(BF)


def pick(meta, row):
    rows = lax.broadcasted_iota(jnp.int32, meta.shape, 0)
    return jnp.sum(jnp.where(rows == row, meta, 0.0), axis=0, keepdims=True)


def spread(meta, expert, rows):
    line = pick(meta, expert)
    slots = lax.broadcasted_iota(jnp.int32, (CAP, rows), 0).astype(F32)
    hot = slots == line[:, 0:rows]
    return hot, jnp.where(hot, line[:, rows : 2 * rows], 0.0)


def route_kernel(rows, places, idx, a_ref, b_ref, own_ref, other_ref, part_ref, weighted_ref, routed):
    x, m = idx[1], idx[2]
    expert = m * pl.num_programs(0) + pl.program_id(0)
    near = a_ref.shape[0]
    sources = len(places) // 2
    for at, (jx, jm) in enumerate(places):
        ref, i = (a_ref, at) if at < near else (b_ref, at - near)
        meta = ref[i, rows : rows + META, 0 : 2 * rows].astype(F32)
        hot, gated = spread(meta, expert, rows)
        both = jnp.concatenate([hot.astype(BF), gated.astype(BF)], axis=0)
        got = dot(both, ref[i, 0:rows, :]).astype(BF)
        row = (jx * sources + jm) * CAP
        routed[row : row + CAP, :] = got[0:CAP]
        weighted_ref[0, row : row + CAP, :] = got[CAP:]
    depth = own_ref.shape[1]
    mine = pl.ds(pl.multiple_of(x * depth, 128), depth)
    theirs = pl.ds(pl.multiple_of((1 - x) * depth, 128), depth)
    back = dot(routed[:, mine], own_ref[0]) + dot(routed[:, theirs], other_ref[0])
    size = sources * CAP
    part_ref[0, 0] = back[0:size].astype(part_ref.dtype)
    part_ref[1, 0] = back[size:].astype(part_ref.dtype)


def grad_kernel(rows_of, idx, *refs):
    total = refs[-1]
    keep_ref, send_ref = refs[-3], refs[-2]
    refs = list(refs[:-3])
    z, x = idx[0], idx[1]
    nz = len(rows_of)
    outer = (z == 0) | (z == nz - 1)
    size = refs[0].shape[1] // 2
    acc = None
    for k, count in enumerate(rows_of):
        weighted = refs.pop(0)
        acts = [refs.pop(0) for _ in range(count)]
        for jx in range(2):
            act = acts[0][jx, 0]
            if count == 2:
                act = jnp.where(outer, act, acts[1][jx, 0])
            term = dot_t(weighted[0, jx * size : (jx + 1) * size, :], act)
            acc = term if acc is None else acc + term
    total[...] = acc
    depth = total.shape[0] // 2
    keep_ref[0] = total[pl.ds(pl.multiple_of(x * depth, 8), depth), :].astype(BF)
    send_ref[0] = total[pl.ds(pl.multiple_of((1 - x) * depth, 8), depth), :].astype(BF)


def last_kernel(rows, half, n_own, idx, saved_ref, meta_ref, *refs):
    owns, (other_ref, pre_ref, score_ref) = refs[:n_own], refs[n_own:]
    x, m = idx[1], idx[2]
    count = saved_ref.shape[2]
    width = 2 * half
    meta = meta_ref[0].astype(F32)
    r = lax.broadcasted_iota(jnp.int32, (CAP, 128), 0)
    c = lax.broadcasted_iota(jnp.int32, (CAP, 128), 1)
    for e in range(count):
        _, gated = spread(meta, m * count + e, rows)
        gate = jnp.sum(gated, axis=1, keepdims=True)
        score = jnp.zeros((CAP, 1), F32)
        for mine in (True, False):
            at = pl.multiple_of((x if mine else 1 - x) * half, 128)
            up_at = pl.multiple_of(width + at, 128)
            if mine:
                back = sum(o[0, e].astype(F32) for o in owns)
            else:
                back = other_ref[e].astype(F32)
            g = saved_ref[0, 0, e, :, pl.ds(at, half)].astype(F32)
            u = saved_ref[0, 0, e, :, pl.ds(up_at, half)].astype(F32)
            sig = lax.logistic(g)
            silu = g * sig
            score = score + jnp.sum(back * (silu * u), axis=1, keepdims=True)
            grad = gate * back
            pre_ref[0, 0, e, :, pl.ds(at, half)] = (grad * u * sig * (1.0 + g * (1.0 - sig))).astype(BF)
            pre_ref[0, 0, e, :, pl.ds(up_at, half)] = (grad * silu).astype(BF)
        score_ref[0, e : e + 1, :] = jnp.sum(jnp.where(r == c, score, 0.0), axis=0, keepdims=True)


def gate_kernel(rows, idx, ids_ref, *refs):
    out_ref = refs[-1]
    m = idx[2]
    cols = named(ids_ref[...], rows)
    r = lax.broadcasted_iota(jnp.int32, (rows, rows), 0)
    c = lax.broadcasted_iota(jnp.int32, (rows, rows), 1)
    before = dot((c < r).astype(BF), sum(cols).astype(BF))
    lanes = lax.broadcasted_iota(jnp.int32, (rows, 128), 1).astype(F32)
    at = lax.broadcasted_iota(jnp.int32, (rows, EXPERTS), 1)
    slots = [jnp.sum(col * before, axis=1, keepdims=True) for col in cols]
    names = [jnp.sum(jnp.where(col > 0.5, at, 0), axis=1, keepdims=True) for col in cols]
    outs = [jnp.zeros((rows, 1), F32) for _ in cols]
    for jm, ref in enumerate(refs[:-1]):
        for e in range(ref.shape[0]):
            expert = (m ^ jm) * ref.shape[0] + e
            line = ref[e : e + 1, :]
            for k in range(len(cols)):
                hit = (lanes == slots[k]) & (names[k] == expert)
                outs[k] = outs[k] + jnp.sum(jnp.where(hit, line, 0.0), axis=1, keepdims=True)
    for k, o in enumerate(outs):
        out_ref[:, k : k + 1] = o


def call(kernel, grid, in_specs, out_specs, out_shape, scratch=(), mib=32, cost=None):
    return pl.pallas_call(
        kernel,
        grid_spec=pltpu.PrefetchScalarGridSpec(
            num_scalar_prefetch=1,
            grid=grid,
            in_specs=in_specs,
            out_specs=out_specs,
            scratch_shapes=list(scratch),
        ),
        out_shape=out_shape,
        compiler_params=params(mib),
        cost_estimate=cost,
    )


def whole(shape):
    return pl.BlockSpec(shape, lambda *_: (0,) * len(shape))


def shards(out_grad, expert_ids, gate_weights, saved_acts, down_weight):
    sources = lax.axis_size("expert")
    n_dp = lax.axis_size("dp")
    nz = n_dp // 2
    line = nz == 4
    count, depth, width = down_weight.shape
    half = width // 2
    rows, model = out_grad.shape
    part = model // nz
    top = expert_ids.shape[1]
    size = sources * CAP
    dp, m = lax.axis_index("dp"), lax.axis_index("expert")
    z, x = dp // 2, dp % 2
    idx = jnp.stack([z, x, m]).astype(jnp.int32)

    def move_z(v, pairs):
        return lax.ppermute(v, "dp", [(2 * a + i, 2 * b + i) for a, b in pairs for i in range(2)])

    def flip_z(v, k):
        return move_z(v, [(a, a ^ k) for a in range(nz)])

    def flip_x(v):
        return lax.ppermute(v, "dp", [(i, i ^ 1) for i in range(n_dp)])

    def flip_m(v, k):
        return lax.ppermute(v, "expert", [(i, i ^ k) for i in range(sources)])

    pieces = call(
        functools.partial(pack_kernel, rows, part),
        (1,),
        [whole((rows, model)), whole((rows, top)), whole((rows, top))],
        [whole((rows + META, part))] * nz,
        [jax.ShapeDtypeStruct((rows + META, part), BF)] * nz,
    )(idx, out_grad, expert_ids, gate_weights)

    other_half = lax.dynamic_slice_in_dim(down_weight, (1 - x) * half, half, 2)
    own_w = lax.dynamic_slice_in_dim(down_weight, x * half, half, 2)
    other_w = flip_x(other_half)

    bits = []
    bit = sources // 2
    while bit:
        bits.append(bit)
        bit //= 2
    places = [(0, 0), (1, 0)]
    for bit in bits:
        places = places + [(jx, jm ^ bit) for jx, jm in places]

    near, far = {}, {}
    for k in sorted(range(nz), reverse=True):
        v = pieces[k] if k == 0 else flip_z(pieces[k], k)
        v = v[None]
        got = flip_x(v)
        for bit in bits:
            v = jnp.concatenate([v, got], axis=0)
            got = flip_m(v, bit)
        near[k], far[k] = v, got

    act_shape = jax.ShapeDtypeStruct((count, size, half), BF)
    act_spec = pl.BlockSpec((count, CAP, half), lambda j, idx: (0, j, 0))
    saved_spec = pl.BlockSpec((1, 1, count, CAP, 2 * width), lambda j, idx: (0, idx[2] ^ j, 0, 0, 0))
    keep, send = call(
        functools.partial(act_kernel, half),
        (sources,),
        [saved_spec],
        [act_spec, act_spec],
        [act_shape, act_shape],
    )(idx, saved_acts)
    own_act = jnp.stack([keep, flip_x(send)])

    inner = [(1, 2), (2, 1)]
    inward = [(0, 1), (3, 2)]
    outward = [(1, 0), (2, 3)]
    if line:
        r1 = flip_z(own_act, 1)
        i3 = move_z(own_act, inner)
        o2 = move_z(i3, outward)
        i2 = move_z(r1, inner)
        o3 = move_z(i2, outward)
        acts = [[own_act], [r1], [o2, i2], [o3, i3]]
    else:
        acts = [[own_act]] + [[flip_z(own_act, k)] for k in range(1, nz)]

    nb = len(places)
    blocks = pl.BlockSpec((nb // 2, rows + META, part), lambda e, idx: (0, 0, 0))
    w_spec = pl.BlockSpec((1, depth, half), lambda e, idx: (e, 0, 0))
    parts, weighted = {}, {}
    for k in sorted(range(nz), reverse=True):
        wire = k == nz - 1 or not line
        parts[k], weighted[k] = call(
            functools.partial(route_kernel, rows, places),
            (count,),
            [blocks, blocks, w_spec, w_spec],
            [
                pl.BlockSpec((2, 1, size, half), lambda e, idx: (0, e, 0, 0)),
                pl.BlockSpec((1, 2 * size, part), lambda e, idx: (e, 0, 0)),
            ],
            [
                jax.ShapeDtypeStruct((2, count, size, half), BF if wire and k else F32),
                jax.ShapeDtypeStruct((count, 2 * size, part), BF),
            ],
            [pltpu.VMEM((2 * size, part), BF)],
        )(idx, near[k], far[k], own_w, other_w)

    def plus(v, got):
        return (v + got.astype(F32)).astype(BF)

    if line:
        s1 = move_z(parts[3], inward)
        v2 = plus(parts[2], s1)
        s2_in = move_z(v2, inward)
        s2_mid = move_z(v2, inner)
        v3 = plus(parts[1], s2_mid)
        v4 = plus(parts[3].astype(F32), s2_in)
        got = [flip_z(v3, 1), move_z(v4, inner)]
    else:
        got = [flip_z(parts[k], k) for k in range(1, nz)]
    owns = [parts[0]] + got
    outgoing = sum(o[1].astype(F32) for o in owns).astype(BF)
    other = flip_x(outgoing)

    flat = []
    specs = []
    for k in range(nz):
        flat.append(weighted[k])
        specs.append(pl.BlockSpec((1, 2 * size, part), lambda e, idx: (e, 0, 0)))
        for a in acts[k]:
            flat.append(a)
            specs.append(pl.BlockSpec((2, 1, size, half), lambda e, idx: (0, e, 0, 0)))
    g_spec = pl.BlockSpec((1, depth, half), lambda e, idx: (e, 0, 0))
    g_shape = jax.ShapeDtypeStruct((count, depth, half), BF)
    g_keep, g_send = call(
        functools.partial(grad_kernel, [len(a) for a in acts]),
        (count,),
        specs,
        [g_spec, g_spec],
        [g_shape, g_shape],
        [pltpu.VMEM((part, half), F32)],
        mib=60,
    )(idx, *flat)
    g_got = flip_x(g_send)
    down_grad = jnp.where(
        x == 0,
        jnp.concatenate([g_keep, g_got], axis=2),
        jnp.concatenate([g_got, g_keep], axis=2),
    )

    order = {jm: at for at, (jx, jm) in enumerate(places) if jx == 0}
    n_near = near[0].shape[0]

    def meta_of(jm):
        at = order[jm]
        ref, i = (near[0], at) if at < n_near else (far[0], at - n_near)
        return ref[i, rows:, 0 : 2 * rows]

    meta = jnp.stack([meta_of(jm) for jm in range(sources)])
    own_spec = pl.BlockSpec((1, count, CAP, half), lambda j, idx: (0, 0, j, 0))
    pre_grads, scores = call(
        functools.partial(last_kernel, rows, half, len(owns)),
        (sources,),
        [saved_spec, pl.BlockSpec((1, META, 2 * rows), lambda j, idx: (j, 0, 0))]
        + [own_spec] * len(owns)
        + [act_spec],
        [saved_spec, pl.BlockSpec((1, count, 128), lambda j, idx: (j, 0, 0))],
        [
            jax.ShapeDtypeStruct(saved_acts.shape, BF),
            jax.ShapeDtypeStruct((sources, count, 128), F32),
        ],
    )(idx, saved_acts, meta, *owns, other)
    returned = [scores[0]] + [flip_m(scores[j], j) for j in range(1, sources)]
    gate_grad = call(
        functools.partial(gate_kernel, rows),
        (1,),
        [whole((rows, top))] + [whole((count, 128))] * sources,
        whole((rows, top)),
        jax.ShapeDtypeStruct((rows, top), F32),
    )(idx, expert_ids, *returned)
    return (pre_grads, down_grad, gate_grad)


def solution(mesh):
    placed = (
        P(("dp", "expert"), None),
        P(("dp", "expert"), None),
        P(("dp", "expert"), None),
        P("dp", None, "expert", None, None),
        P("expert", "dp", None),
    )
    return jax.shard_map(
        shards,
        mesh=mesh,
        in_specs=placed,
        out_specs=(
            P("dp", None, "expert", None, None),
            P("expert", "dp", None),
            P(("dp", "expert"), None),
        ),
        check_vma=False,
    )
```

time: 1300 us -> 288 us (0.22)
  waiting for transfers between devices: 1190 us -> 121 us
  starting transfers between devices: 13.2 us -> 92.7 us
  Pallas kernels: 0 us -> 44 us
  matrix products: 37.4 us -> 0 us
  local copies, waits for them, and re-layouts: 42.1 us -> 16.4 us
  between operations: 14.2 us -> 1.12 us
    reduce_scatter x1 -> x0, waiting for transfers between devices: 766 us -> none  [shards(): lax.psum_scatter(jnp.einsum('slcd,slcf->dlf', weighted, act_low, preferre...]
    all_gather x1 -> x0, waiting for transfers between devices: 351 us -> none  [shards(): lax.all_gather(down_weight, 'dp', axis=1, tiled=True)]
    ppermute x0 -> x32, waiting for transfers between devices: none -> 121 us  [the longest x8 78.2 us: flip_x(): return lax.ppermute(v, 'dp', [(i, i ^ 1) for i in range(n_dp)])]
    ppermute x0 -> x32, starting transfers between devices: none -> 92.7 us  [the longest x13 75.2 us: move_z(): lax.ppermute(v, 'dp', [(2 * a + i, 2 * b + i) for a, b in pairs for i in...]
    all_to_all x3 -> x0, waiting for transfers between devices: 69.5 us -> none  [the longest x1 68.8 us: shards(): lax.all_to_all(outgoing, 'expert', split_axis=0, concat_axis=0, tiled=True)]
    pallas_call x0 -> x9, Pallas kernels: none -> 44 us  [the longest x4 20.4 us: shards(): call(functools.partial(route_kernel, rows, places), (count,), [blocks, bl...]
    dot_general x2 -> x0, matrix products: 37.4 us -> none  [the longest x1 21.7 us: shards(): jnp.einsum('slcd,slcf->dlf', weighted, act_low, preferred_element_type=jn...]
    scatter x2 -> x0, local copies, waits for them, and re-layouts: 15.2 us -> none  [the longest x1 11.4 us: shards(): jnp.zeros((total_slots, width), jnp.bfloat16).at[flat_target].set(copies)]
  transfers between devices with their start and end apart: 5 -> 32, of which waited for: 4 -> 13; matrix products, arithmetic and copies ran while one was open for 6% -> 5% of each run, Pallas kernels for 0% -> 14%
where the time goes in v1:
time: 288 us
  waiting for transfers between devices  121 us (42%)
  starting transfers between devices  92.7 us (32%)
  Pallas kernels  44 us (15%)
  local copies, waits for them, and re-layouts  16.4 us (6%)
  other arithmetic  12.3 us (4%)
    ppermute x8, waiting for transfers between devices, flip_x(): return lax.ppermute(v, 'dp', [(i, i ^ 1) for i in range(n_dp)])  78.2 us
    ppermute x13, starting transfers between devices, move_z(): lax.ppermute(v, 'dp', [(2 * a + i, 2 * b + i) for a, b in pairs for i in...  75.2 us
    ppermute x13, waiting for transfers between devices, move_z(): lax.ppermute(v, 'dp', [(2 * a + i, 2 * b + i) for a, b in pairs for i in...  35.1 us
    pallas_call x4, Pallas kernels, shards(): call(functools.partial(route_kernel, rows, places), (count,), [blocks, bl...  20.4 us
    pallas_call x1, Pallas kernels, shards(): call(functools.partial(grad_kernel, [len(a) for a in acts]), (count,), sp...  14.1 us
    unnamed x49, local copies, waits for them, and re-layouts  12.1 us
    ppermute x8, starting transfers between devices, flip_x(): return lax.ppermute(v, 'dp', [(i, i ^ 1) for i in range(n_dp)])  11.1 us
    ppermute x11, waiting for transfers between devices, flip_m(): return lax.ppermute(v, 'expert', [(i, i ^ k) for i in range(sources)])  8 us
  transfers between devices with their start and end apart: 32, of which 13 were waited for; matrix products, arithmetic and copies ran while one was open for 5% of the time, Pallas kernels for 14%

profile of v1, /device:TPU:0, one launch (start us, length us, event | category | flops | bytes accessed | tf_op | source)
XLA Modules:
  0.0 287.8 jit_solution(3134778046359956326)
XLA Ops:
  4.5 5.1 %collective-permute-start.12 = (bf16[144,1024]{1,0:T(8,128)(2,1)S(1)}, bf16[144,1024]{1,0:T(8,128)(2,1)S(1)}, u32[]{:S(2)}, u32[]{:S(2)}) collective-permute-start(bf16[144,1024]{1,0:T(8,128)(2,1)S(1)} %get-tuple-element.27), channel_id=1, source_target_pairs={{0,24},{4,28},{8,16},{12,20},{16,8},{20,12},{24,0},{28,4},{1,25},{... | collective-permute-start | bytes 884744 | tf_op jit(solution)/shard_map/ppermute | solution.py:215
  9.6 7.1 %collective-permute-done.12 = bf16[144,1024]{1,0:T(8,128)(2,1)S(1)} collective-permute-done((bf16[144,1024]{1,0:T(8,128)(2,1)S(1)}, bf16[144,1024]{1,0:T(8,128)(2,1)S(1)}, u32[]{:S(2)}, u32[]{:S(2)}) %collective-permute-start.12) | collective-permute-done | bytes 294944 | tf_op jit(solution)/shard_map/ppermute | solution.py:215
  18.2 6.6 %collective-permute-done.13 = bf16[1,144,1024]{2,1,0:T(8,128)(2,1)S(1)} collective-permute-done((bf16[1,144,1024]{2,1,0:T(8,128)(2,1)S(1)}, bf16[1,144,1024]{2,1,0:T(8,128)(2,1)S(1)}, u32[]{:S(2)}, u32[]{:S(2)}) %collective-permute-start.13) | collective-permute-done | bytes 294944 | tf_op jit(solution)/shard_map/ppermute | solution.py:221
  30.8 6.9 %collective-permute-start.8 = (bf16[144,1024]{1,0:T(8,128)(2,1)S(1)}, bf16[144,1024]{1,0:T(8,128)(2,1)S(1)}, u32[]{:S(2)}, u32[]{:S(2)}) collective-permute-start(bf16[144,1024]{1,0:T(8,128)(2,1)S(1)} %get-tuple-element.25), channel_id=1, source_target_pairs={{0,16},{4,20},{8,24},{12,28},{16,0},{20,4},{24,8},{28,12},{1,17},{... | collective-permute-start | bytes 884744 | tf_op jit(solution)/shard_map/ppermute | solution.py:215
  40.9 7.8 %collective-permute-done.8 = bf16[144,1024]{1,0:T(8,128)(2,1)S(1)} collective-permute-done((bf16[144,1024]{1,0:T(8,128)(2,1)S(1)}, bf16[144,1024]{1,0:T(8,128)(2,1)S(1)}, u32[]{:S(2)}, u32[]{:S(2)}) %collective-permute-start.8) | collective-permute-done | bytes 294944 | tf_op jit(solution)/shard_map/ppermute | solution.py:215
  52.0 20.9 %collective-permute-done.9 = bf16[1,144,1024]{2,1,0:T(8,128)(2,1)S(1)} collective-permute-done((bf16[1,144,1024]{2,1,0:T(8,128)(2,1)S(1)}, bf16[1,144,1024]{2,1,0:T(8,128)(2,1)S(1)}, u32[]{:S(2)}, u32[]{:S(2)}) %collective-permute-start.9) | collective-permute-done | bytes 294944 | tf_op jit(solution)/shard_map/ppermute | solution.py:221
  73.8 5.9 %collective-permute-start.4 = (bf16[144,1024]{1,0:T(8,128)(2,1)S(1)}, bf16[144,1024]{1,0:T(8,128)(2,1)S(1)}, u32[]{:S(2)}, u32[]{:S(2)}) collective-permute-start(bf16[144,1024]{1,0:T(8,128)(2,1)S(1)} %get-tuple-element.23), channel_id=1, source_target_pairs={{0,8},{4,12},{8,0},{12,4},{16,24},{20,28},{24,16},{28,20},{1,9},{5... | collective-permute-start | bytes 884744 | tf_op jit(solution)/shard_map/ppermute | solution.py:215
  79.7 2.7 collective-permute-done.22
  82.5 6.3 %collective-permute-start.23 = (bf16[2,4,192,384]{3,2,1,0:T(8,128)(2,1)S(1)}, bf16[2,4,192,384]{3,2,1,0:T(8,128)(2,1)S(1)}, u32[]{:S(2)}, u32[]{:S(2)}) collective-permute-start(bf16[2,4,192,384]{3,2,1,0:T(8,128)(2,1)S(1)} %pad_maximum_fusion.4.refs_1_), channel_id=1, source_target_pairs={{0,8},{4,12},{8,0},{12,4},{16,24},{20,28},{24,16},{28,20},{1,9},{5... | collective-permute-start | bytes 3538952 | tf_op jit(solution)/shard_map/ppermute | solution.py:215
  89.0 5.1 %shard_map.80 = (bf16[2,4,192,384]{3,2,1,0:T(8,128)(2,1)S(1)}, bf16[4,384,1024]{2,1,0:T(8,128)(2,1)S(1)}) custom-call(s32[3]{0:T(128)S(1)} %pad_add_fusion.idx, bf16[4,144,1024]{2,1,0:T(8,128)(2,1)S(1)} %pad_maximum_fusion.3.a_ref, bf16[4,144,1024]{2,1,0:T(8,128)(2,1)S(1)} %collective-permute-done.15.b_ref, ...), custom_call_target="tpu_custom_call" | custom-call | tf_op jit(solution)/shard_map/pallas_call | solution.py:288
  99.6 7.6 %collective-permute-done.5 = bf16[1,144,1024]{2,1,0:T(8,128)(2,1)S(1)} collective-permute-done((bf16[1,144,1024]{2,1,0:T(8,128)(2,1)S(1)}, bf16[1,144,1024]{2,1,0:T(8,128)(2,1)S(1)}, u32[]{:S(2)}, u32[]{:S(2)}) %collective-permute-start.5) | collective-permute-done | bytes 294944 | tf_op jit(solution)/shard_map/ppermute | solution.py:221
  109.3 6.6 %collective-permute-done = bf16[1,144,1024]{2,1,0:T(8,128)(2,1)S(1)} collective-permute-done((bf16[1,144,1024]{2,1,0:T(8,128)(2,1)S(1)}, bf16[1,144,1024]{2,1,0:T(8,128)(2,1)S(1)}, u32[]{:S(2)}, u32[]{:S(2)}) %collective-permute-start) | collective-permute-done | bytes 294944 | tf_op jit(solution)/shard_map/ppermute | solution.py:221
  117.5 6.1 %collective-permute-done.6 = bf16[2,144,1024]{2,1,0:T(8,128)(2,1)S(1)} collective-permute-done((bf16[2,144,1024]{2,1,0:T(8,128)(2,1)S(1)}, bf16[2,144,1024]{2,1,0:T(8,128)(2,1)S(1)}, u32[]{:S(2)}, u32[]{:S(2)}) %collective-permute-start.6) | collective-permute-done | bytes 589856 | tf_op jit(solution)/shard_map/ppermute | solution.py:224
  125.3 5.1 %shard_map.79 = (f32[2,4,192,384]{3,2,1,0:T(8,128)S(1)}, bf16[4,384,1024]{2,1,0:T(8,128)(2,1)S(1)}) custom-call(s32[3]{0:T(128)S(1)} %pad_add_fusion.idx, bf16[4,144,1024]{2,1,0:T(8,128)(2,1)S(1)} %pad_maximum_fusion.2.a_ref, bf16[4,144,1024]{2,1,0:T(8,128)(2,1)S(1)} %collective-permute-done.11.b_ref, bf16[4,512,384]{2,1,0:T(8,128)(2,1)S(1)} %get-tuple-element.43.own_ref, ...), custom_call_target="tpu_custom_call" | custom-call | tf_op jit(solution)/shard_map/pallas_call | solution.py:288
  130.4 6.1 %collective-permute-done.16 = bf16[2,4,192,384]{3,2,1,0:T(8,128)(2,1)S(1)} collective-permute-done((bf16[2,4,192,384]{3,2,1,0:T(8,128)(2,1)S(1)}, bf16[2,4,192,384]{3,2,1,0:T(8,128)(2,1)S(1)}, u32[]{:S(2)}, u32[]{:S(2)}) %collective-permute-start.16) | collective-permute-done | bytes 1179680 | tf_op jit(solution)/shard_map/ppermute | solution.py:215
  136.8 4.5 %collective-permute-start.19 = (bf16[2,4,192,384]{3,2,1,0:T(8,128)(2,1)S(1)}, bf16[2,4,192,384]{3,2,1,0:T(8,128)(2,1)S(1)}, u32[]{:S(2)}, u32[]{:S(2)}) collective-permute-start(bf16[2,4,192,384]{3,2,1,0:T(8,128)(2,1)S(1)} %add_convert_fusion.2), channel_id=1, source_target_pairs={{0,8},{4,12},{24,16},{28,20},{1,9},{5,13},{25,17},{29,21},{2,10},{... | collective-permute-start | bytes 3538952 | tf_op jit(solution)/shard_map/ppermute | solution.py:215
  143.6 5.1 %shard_map.78 = (f32[2,4,192,384]{3,2,1,0:T(8,128)S(1)}, bf16[4,384,1024]{2,1,0:T(8,128)(2,1)S(1)}) custom-call(s32[3]{0:T(128)S(1)} %pad_add_fusion.idx, bf16[4,144,1024]{2,1,0:T(8,128)(2,1)S(1)} %pad_maximum_fusion.1.a_ref, bf16[4,144,1024]{2,1,0:T(8,128)(2,1)S(1)} %collective-permute-done.7.b_ref, bf16[4,512,384]{2,1,0:T(8,128)(2,1)S(1)} %get-tuple-element.43.own_ref, ...), custom_call_target="tpu_custom_call" | custom-call | tf_op jit(solution)/shard_map/pallas_call | solution.py:288
  150.0 13.4 %collective-permute-done.19 = bf16[2,4,192,384]{3,2,1,0:T(8,128)(2,1)S(1)} collective-permute-done((bf16[2,4,192,384]{3,2,1,0:T(8,128)(2,1)S(1)}, bf16[2,4,192,384]{3,2,1,0:T(8,128)(2,1)S(1)}, u32[]{:S(2)}, u32[]{:S(2)}) %collective-permute-start.19) | collective-permute-done | bytes 1179680 | tf_op jit(solution)/shard_map/ppermute | solution.py:215
  167.0 38.8 %collective-permute-start.18 = (bf16[2,4,192,384]{3,2,1,0:T(8,128)(2,1)}, bf16[2,4,192,384]{3,2,1,0:T(8,128)(2,1)}, u32[]{:S(2)}, u32[]{:S(2)}) collective-permute-start(bf16[2,4,192,384]{3,2,1,0:T(8,128)(2,1)} %add_convert_fusion.1), channel_id=1, source_target_pairs={{0,8},{4,12},{8,0},{12,4},{16,24},{20,28},{24,16},{28,20},{1,9},{5... | collective-permute-start | bytes 3538952 | tf_op jit(solution)/shard_map/ppermute | solution.py:215
  205.8 5.1 %shard_map.77 = (f32[2,4,192,384]{3,2,1,0:T(8,128)S(1)}, bf16[4,384,1024]{2,1,0:T(8,128)(2,1)S(1)}) custom-call(s32[3]{0:T(128)S(1)} %pad_add_fusion.idx, bf16[4,144,1024]{2,1,0:T(8,128)(2,1)S(1)} %pad_maximum_fusion.a_ref, bf16[4,144,1024]{2,1,0:T(8,128)(2,1)S(1)} %collective-permute-done.2.b_ref, bf16[4,512,384]{2,1,0:T(8,128)(2,1)S(1)} %get-tuple-element.43.own_ref, ...), custom_call_target="tpu_custom_call" | custom-call | tf_op jit(solution)/shard_map/pallas_call | solution.py:288
  216.1 14.1 %shard_map.83 = (bf16[4,512,384]{2,1,0:T(8,128)(2,1)}, bf16[4,512,384]{2,1,0:T(8,128)(2,1)}) custom-call(s32[3]{0:T(128)} %copy-done.12, bf16[4,384,1024]{2,1,0:T(8,128)(2,1)} %copy-done.6, bf16[2,4,192,384]{3,2,1,0:T(8,128)(2,1)} %copy-done.14, bf16[4,384,1024]{2,1,0:T(8,128)(2,1)} %copy-done.5, bf16[2,4,192,384]{3,2,1,0:T(8,128)(2,1)} %copy-done.16, ...), custom_call_target="tpu_custom_call" | custom-call | tf_op jit(solution)/shard_map/pallas_call | solution.py:330
  238.6 33.7 %collective-permute-done.21.refs_3_ = bf16[4,192,384]{2,1,0:T(8,128)(2,1)} collective-permute-done((bf16[4,192,384]{2,1,0:T(8,128)(2,1)}, bf16[4,192,384]{2,1,0:T(8,128)(2,1)}, u32[]{:S(2)}, u32[]{:S(2)}) %collective-permute-start.21) | collective-permute-done | bytes 589856 | tf_op jit(solution)/shard_map/ppermute | solution.py:221
  274.0 5.2 %shard_map.81 = (bf16[1,4,4,48,1536]{4,3,2,1,0:T(8,128)(2,1)}, f32[4,4,128]{2,1,0:T(4,128)S(1)}) custom-call(s32[3]{0:T(128)S(1)} %copy-done.13, bf16[1,4,4,48,1536]{4,3,2,1,0:T(8,128)(2,1)S(1)} %copy-done, bf16[4,16,256]{2,1,0:T(8,128)(2,1)S(1)} %pad_maximum_fusion.9.meta_ref, f32[2,4,192,384]{3,2,1,0:T(8,128)S(1)} %copy-done.2, ...), custom_call_target="tpu_custom_call" | custom-call | tf_op jit(solution)/shard_map/pallas_call | solution.py:356
  281.1 3.9 %maximum_select_fusion = bf16[4,512,768]{2,1,0:T(8,128)(2,1)} fusion(bf16[4,512,384]{2,1,0:T(8,128)(2,1)} %collective-permute-done.28, bf16[4,512,384]{2,1,0:T(8,128)(2,1)S(1)} %copy-done.15, pred[]{:T(512)S(6)} %eq.5), kind=kLoop, calls=%fused_computation | loop fusion | flops 14155776 | bytes 6291457 | tf_op jit(solution)/shard_map/jit(_where)/select_n | solution.py:340
  (119 shorter events, 57.1 us)
Async XLA Ops:
  29.2 59.8 %collective-permute-start.3 = (bf16[4,512,384]{2,1,0:T(8,128)(2,1)S(1)}, bf16[4,512,384]{2,1,0:T(8,128)(2,1)S(1)}, u32[]{:S(2)}, u32[]{:S(2)}) collective-permute-start(bf16[4,512,384]{2,1,0:T(8,128)(2,1)S(1)} %get-tuple-element.42), channel_id=1, source_target_pairs={{0,4},{4,0},{8,12},{12,8},{16,20},{20,16},{24,28},{28,24},{1,5},{5... | collective-permute-start | bytes 4718600 | tf_op jit(solution)/shard_map/ppermute | solution.py:221
  30.8 17.9 %collective-permute-start.8 = (bf16[144,1024]{1,0:T(8,128)(2,1)S(1)}, bf16[144,1024]{1,0:T(8,128)(2,1)S(1)}, u32[]{:S(2)}, u32[]{:S(2)}) collective-permute-start(bf16[144,1024]{1,0:T(8,128)(2,1)S(1)} %get-tuple-element.25), channel_id=1, source_target_pairs={{0,16},{4,20},{8,24},{12,28},{16,0},{20,4},{24,8},{28,12},{1,17},{... | collective-permute-start | bytes 884744 | tf_op jit(solution)/shard_map/ppermute | solution.py:215
  40.8 48.2 %collective-permute-start.15 = (bf16[4,144,1024]{2,1,0:T(8,128)(2,1)S(1)}, bf16[4,144,1024]{2,1,0:T(8,128)(2,1)S(1)}, u32[]{:S(2)}, u32[]{:S(2)}) collective-permute-start(bf16[4,144,1024]{2,1,0:T(8,128)(2,1)S(1)} %pad_maximum_fusion.3.a_ref), channel_id=1, source_target_pairs={{0,1},{1,0},{2,3},{3,2},{4,5},{5,4},{6,7},{7,6},{8,9},{9,8},{10,11... | collective-permute-start | bytes 3538952 | tf_op jit(solution)/shard_map/ppermute | solution.py:224
  48.7 24.3 %collective-permute-start.9 = (bf16[1,144,1024]{2,1,0:T(8,128)(2,1)S(1)}, bf16[1,144,1024]{2,1,0:T(8,128)(2,1)S(1)}, u32[]{:S(2)}, u32[]{:S(2)}) collective-permute-start(bf16[1,144,1024]{2,1,0:T(8,128)(2,1)S(1)} %bitcast.27), channel_id=1, source_target_pairs={{0,4},{4,0},{8,12},{12,8},{16,20},{20,16},{24,28},{28,24},{1,5},{5... | collective-permute-start | bytes 884744 | tf_op jit(solution)/shard_map/ppermute | solution.py:221
  50.5 31.9 %collective-permute-start.22 = (bf16[4,192,384]{2,1,0:T(8,128)(2,1)S(1)}, bf16[4,192,384]{2,1,0:T(8,128)(2,1)S(1)}, u32[]{:S(2)}, u32[]{:S(2)}) collective-permute-start(bf16[4,192,384]{2,1,0:T(8,128)(2,1)S(1)} %get-tuple-element.32), channel_id=1, source_target_pairs={{0,4},{4,0},{8,12},{12,8},{16,20},{20,16},{24,28},{28,24},{1,5},{5... | collective-permute-start | bytes 1769480 | tf_op jit(solution)/shard_map/ppermute | solution.py:221
  73.0 15.8 %collective-permute-start.10 = (bf16[2,144,1024]{2,1,0:T(8,128)(2,1)S(1)}, bf16[2,144,1024]{2,1,0:T(8,128)(2,1)S(1)}, u32[]{:S(2)}, u32[]{:S(2)}) collective-permute-start(bf16[2,144,1024]{2,1,0:T(8,128)(2,1)S(1)} %pad_maximum_fusion.7), channel_id=1, source_target_pairs={{0,2},{1,3},{2,0},{3,1},{4,6},{5,7},{6,4},{7,5},{8,10},{9,11},{10,... | collective-permute-start | bytes 1769480 | tf_op jit(solution)/shard_map/ppermute | solution.py:224
  73.8 24.2 %collective-permute-start.4 = (bf16[144,1024]{1,0:T(8,128)(2,1)S(1)}, bf16[144,1024]{1,0:T(8,128)(2,1)S(1)}, u32[]{:S(2)}, u32[]{:S(2)}) collective-permute-start(bf16[144,1024]{1,0:T(8,128)(2,1)S(1)} %get-tuple-element.23), channel_id=1, source_target_pairs={{0,8},{4,12},{8,0},{12,4},{16,24},{20,28},{24,16},{28,20},{1,9},{5... | collective-permute-start | bytes 884744 | tf_op jit(solution)/shard_map/ppermute | solution.py:215
  82.5 41.9 %collective-permute-start.23 = (bf16[2,4,192,384]{3,2,1,0:T(8,128)(2,1)S(1)}, bf16[2,4,192,384]{3,2,1,0:T(8,128)(2,1)S(1)}, u32[]{:S(2)}, u32[]{:S(2)}) collective-permute-start(bf16[2,4,192,384]{3,2,1,0:T(8,128)(2,1)S(1)} %pad_maximum_fusion.4.refs_1_), channel_id=1, source_target_pairs={{0,8},{4,12},{8,0},{12,4},{16,24},{20,28},{24,16},{28,20},{1,9},{5... | collective-permute-start | bytes 3538952 | tf_op jit(solution)/shard_map/ppermute | solution.py:215
  88.9 35.6 %collective-permute-start.11 = (bf16[4,144,1024]{2,1,0:T(8,128)(2,1)S(1)}, bf16[4,144,1024]{2,1,0:T(8,128)(2,1)S(1)}, u32[]{:S(2)}, u32[]{:S(2)}) collective-permute-start(bf16[4,144,1024]{2,1,0:T(8,128)(2,1)S(1)} %pad_maximum_fusion.2.a_ref), channel_id=1, source_target_pairs={{0,1},{1,0},{2,3},{3,2},{4,5},{5,4},{6,7},{7,6},{8,9},{9,8},{10,11... | collective-permute-start | bytes 3538952 | tf_op jit(solution)/shard_map/ppermute | solution.py:224
  95.8 40.7 %collective-permute-start.16 = (bf16[2,4,192,384]{3,2,1,0:T(8,128)(2,1)S(1)}, bf16[2,4,192,384]{3,2,1,0:T(8,128)(2,1)S(1)}, u32[]{:S(2)}, u32[]{:S(2)}) collective-permute-start(bf16[2,4,192,384]{3,2,1,0:T(8,128)(2,1)S(1)} %get-tuple-element.28), channel_id=1, source_target_pairs={{0,8},{4,12},{24,16},{28,20},{1,9},{5,13},{25,17},{29,21},{2,10},{... | collective-permute-start | bytes 3538952 | tf_op jit(solution)/shard_map/ppermute | solution.py:215
  107.3 16.3 %collective-permute-start.6 = (bf16[2,144,1024]{2,1,0:T(8,128)(2,1)S(1)}, bf16[2,144,1024]{2,1,0:T(8,128)(2,1)S(1)}, u32[]{:S(2)}, u32[]{:S(2)}) collective-permute-start(bf16[2,144,1024]{2,1,0:T(8,128)(2,1)S(1)} %pad_maximum_fusion.6), channel_id=1, source_target_pairs={{0,2},{1,3},{2,0},{3,1},{4,6},{5,7},{6,4},{7,5},{8,10},{9,11},{10,... | collective-permute-start | bytes 1769480 | tf_op jit(solution)/shard_map/ppermute | solution.py:224
  115.9 25.4 %collective-permute-start.1 = (bf16[2,144,1024]{2,1,0:T(8,128)(2,1)S(1)}, bf16[2,144,1024]{2,1,0:T(8,128)(2,1)S(1)}, u32[]{:S(2)}, u32[]{:S(2)}) collective-permute-start(bf16[2,144,1024]{2,1,0:T(8,128)(2,1)S(1)} %pad_maximum_fusion.5), channel_id=1, source_target_pairs={{0,2},{1,3},{2,0},{3,1},{4,6},{5,7},{6,4},{7,5},{8,10},{9,11},{10,... | collective-permute-start | bytes 1769480 | tf_op jit(solution)/shard_map/ppermute | solution.py:224
  123.6 18.6 %collective-permute-start.24 = (bf16[2,4,192,384]{3,2,1,0:T(8,128)(2,1)S(1)}, bf16[2,4,192,384]{3,2,1,0:T(8,128)(2,1)S(1)}, u32[]{:S(2)}, u32[]{:S(2)}) collective-permute-start(bf16[2,4,192,384]{3,2,1,0:T(8,128)(2,1)S(1)} %pad_maximum_fusion.4.refs_1_), channel_id=1, source_target_pairs={{8,16},{12,20},{16,8},{20,12},{9,17},{13,21},{17,9},{21,13},{10,18... | collective-permute-start | bytes 3538952 | tf_op jit(solution)/shard_map/ppermute | solution.py:215
  124.5 17.8 %collective-permute-start.7 = (bf16[4,144,1024]{2,1,0:T(8,128)(2,1)S(1)}, bf16[4,144,1024]{2,1,0:T(8,128)(2,1)S(1)}, u32[]{:S(2)}, u32[]{:S(2)}) collective-permute-start(bf16[4,144,1024]{2,1,0:T(8,128)(2,1)S(1)} %pad_maximum_fusion.1.a_ref), channel_id=1, source_target_pairs={{0,1},{1,0},{2,3},{3,2},{4,5},{5,4},{6,7},{7,6},{8,9},{9,8},{10,11... | collective-permute-start | bytes 3538952 | tf_op jit(solution)/shard_map/ppermute | solution.py:224
  124.6 24.2 %collective-permute-start.26 = (bf16[2,4,192,384]{3,2,1,0:T(8,128)(2,1)S(1)}, bf16[2,4,192,384]{3,2,1,0:T(8,128)(2,1)S(1)}, u32[]{:S(2)}, u32[]{:S(2)}) collective-permute-start(bf16[2,4,192,384]{3,2,1,0:T(8,128)(2,1)S(1)} %collective-permute-done.23.refs_3_), channel_id=1, source_target_pairs={{8,16},{12,20},{16,8},{20,12},{9,17},{13,21},{17,9},{21,13},{10,18... | collective-permute-start | bytes 3538952 | tf_op jit(solution)/shard_map/ppermute | solution.py:215
  136.8 26.6 %collective-permute-start.19 = (bf16[2,4,192,384]{3,2,1,0:T(8,128)(2,1)S(1)}, bf16[2,4,192,384]{3,2,1,0:T(8,128)(2,1)S(1)}, u32[]{:S(2)}, u32[]{:S(2)}) collective-permute-start(bf16[2,4,192,384]{3,2,1,0:T(8,128)(2,1)S(1)} %add_convert_fusion.2), channel_id=1, source_target_pairs={{0,8},{4,12},{24,16},{28,20},{1,9},{5,13},{25,17},{29,21},{2,10},{... | collective-permute-start | bytes 3538952 | tf_op jit(solution)/shard_map/ppermute | solution.py:215
  141.3 24.4 %collective-permute-start.17 = (bf16[2,4,192,384]{3,2,1,0:T(8,128)(2,1)S(1)}, bf16[2,4,192,384]{3,2,1,0:T(8,128)(2,1)S(1)}, u32[]{:S(2)}, u32[]{:S(2)}) collective-permute-start(bf16[2,4,192,384]{3,2,1,0:T(8,128)(2,1)S(1)} %add_convert_fusion.2), channel_id=1, source_target_pairs={{8,16},{12,20},{16,8},{20,12},{9,17},{13,21},{17,9},{21,13},{10,18... | collective-permute-start | bytes 3538952 | tf_op jit(solution)/shard_map/ppermute | solution.py:215
  142.2 63.6 %collective-permute-start.2 = (bf16[4,144,1024]{2,1,0:T(8,128)(2,1)S(1)}, bf16[4,144,1024]{2,1,0:T(8,128)(2,1)S(1)}, u32[]{:S(2)}, u32[]{:S(2)}) collective-permute-start(bf16[4,144,1024]{2,1,0:T(8,128)(2,1)S(1)} %pad_maximum_fusion.a_ref), channel_id=1, source_target_pairs={{0,1},{1,0},{2,3},{3,2},{4,5},{5,4},{6,7},{7,6},{8,9},{9,8},{10,11... | collective-permute-start | bytes 3538952 | tf_op jit(solution)/shard_map/ppermute | solution.py:224
  142.3 71.7 %collective-permute-start.25 = (bf16[2,4,192,384]{3,2,1,0:T(8,128)(2,1)S(1)}, bf16[2,4,192,384]{3,2,1,0:T(8,128)(2,1)S(1)}, u32[]{:S(2)}, u32[]{:S(2)}) collective-permute-start(bf16[2,4,192,384]{3,2,1,0:T(8,128)(2,1)S(1)} %collective-permute-done.24.refs_9_), channel_id=1, source_target_pairs={{8,0},{12,4},{16,24},{20,28},{9,1},{13,5},{17,25},{21,29},{10,2},{... | collective-permute-start | bytes 3538952 | tf_op jit(solution)/shard_map/ppermute | solution.py:215
  148.7 65.3 %collective-permute-start.27 = (bf16[2,4,192,384]{3,2,1,0:T(8,128)(2,1)S(1)}, bf16[2,4,192,384]{3,2,1,0:T(8,128)(2,1)S(1)}, u32[]{:S(2)}, u32[]{:S(2)}) collective-permute-start(bf16[2,4,192,384]{3,2,1,0:T(8,128)(2,1)S(1)} %collective-permute-done.26.refs_6_), channel_id=1, source_target_pairs={{8,0},{12,4},{16,24},{20,28},{9,1},{13,5},{17,25},{21,29},{10,2},{... | collective-permute-start | bytes 3538952 | tf_op jit(solution)/shard_map/ppermute | solution.py:215
  164.8 66.9 %collective-permute-start.20 = (bf16[2,4,192,384]{3,2,1,0:T(8,128)(2,1)}, bf16[2,4,192,384]{3,2,1,0:T(8,128)(2,1)S(1)}, u32[]{:S(2)}, u32[]{:S(2)}) collective-permute-start(bf16[2,4,192,384]{3,2,1,0:T(8,128)(2,1)} %add_convert_fusion), channel_id=1, source_target_pairs={{8,16},{12,20},{16,8},{20,12},{9,17},{13,21},{17,9},{21,13},{10,18... | collective-permute-start | bytes 3538952 | tf_op jit(solution)/shard_map/ppermute | solution.py:215
  167.0 65.5 %collective-permute-start.18 = (bf16[2,4,192,384]{3,2,1,0:T(8,128)(2,1)}, bf16[2,4,192,384]{3,2,1,0:T(8,128)(2,1)}, u32[]{:S(2)}, u32[]{:S(2)}) collective-permute-start(bf16[2,4,192,384]{3,2,1,0:T(8,128)(2,1)} %add_convert_fusion.1), channel_id=1, source_target_pairs={{0,8},{4,12},{8,0},{12,4},{16,24},{20,28},{24,16},{28,20},{1,9},{5... | collective-permute-start | bytes 3538952 | tf_op jit(solution)/shard_map/ppermute | solution.py:215
  230.2 50.9 %collective-permute-start.28 = (bf16[4,512,384]{2,1,0:T(8,128)(2,1)}, bf16[4,512,384]{2,1,0:T(8,128)(2,1)}, u32[]{:S(2)}, u32[]{:S(2)}) collective-permute-start(bf16[4,512,384]{2,1,0:T(8,128)(2,1)} %get-tuple-element.37), channel_id=1, source_target_pairs={{0,4},{4,0},{8,12},{12,8},{16,20},{20,16},{24,28},{28,24},{1,5},{5... | collective-permute-start | bytes 4718600 | tf_op jit(solution)/shard_map/ppermute | solution.py:221
  235.0 37.3 %collective-permute-start.21 = (bf16[4,192,384]{2,1,0:T(8,128)(2,1)}, bf16[4,192,384]{2,1,0:T(8,128)(2,1)}, u32[]{:S(2)}, u32[]{:S(2)}) collective-permute-start(bf16[4,192,384]{2,1,0:T(8,128)(2,1)} %fusion), channel_id=1, source_target_pairs={{0,4},{4,0},{8,12},{12,8},{16,20},{20,16},{24,28},{28,24},{1,5},{5... | collective-permute-start | bytes 1769480 | tf_op jit(solution)/shard_map/ppermute | solution.py:221
  (31 other events, 615.9 us)

commit v2 on v1

v2 whole, which is shorter than its diff:
```python
import functools

import jax
import jax.numpy as jnp
from jax import lax
from jax.experimental import pallas as pl
from jax.experimental.pallas import tpu as pltpu
from jax.sharding import PartitionSpec as P

EXPERTS = 16
CAP = 48
META = 16
NONE = 255.0
BF = jnp.bfloat16
F32 = jnp.float32


def params(mib):
    return pltpu.CompilerParams(vmem_limit_bytes=mib * 1024 * 1024)


def dot(a, b):
    return jnp.dot(a, b, preferred_element_type=F32)


def dot_t(a, b):
    return lax.dot_general(a, b, (((0,), (0,)), ((), ())), preferred_element_type=F32)


def named(ids, rows):
    experts = lax.broadcasted_iota(jnp.int32, (rows, EXPERTS), 1)
    return [(ids[:, k : k + 1] == experts).astype(F32) for k in range(ids.shape[1])]


def pack_kernel(rows, part, idx, grad_ref, ids_ref, gates_ref, *outs):
    cols = named(ids_ref[...], rows)
    gates = gates_ref[...].astype(F32)
    hit = sum(cols)
    gate = sum(c * gates[:, k : k + 1] for k, c in enumerate(cols))
    r = lax.broadcasted_iota(jnp.int32, (rows, rows), 0)
    c = lax.broadcasted_iota(jnp.int32, (rows, rows), 1)
    earlier, eye = (r < c).astype(BF), (r == c).astype(BF)
    before = dot_t(hit.astype(BF), earlier)
    hit_t = dot_t(hit.astype(BF), eye)
    gate_t = dot_t(gate.astype(BF), eye)
    slots = jnp.where(hit_t > 0.5, before, NONE)
    z = idx[0]
    for k, out in enumerate(outs):
        at = pl.multiple_of((z ^ k) * part, 128)
        out[0:rows, :] = grad_ref[:, pl.ds(at, part)]
        out[rows : rows + META, :] = jnp.zeros((META, part), BF)
        out[rows : rows + META, 0:rows] = slots.astype(BF)
        out[rows : rows + META, rows : 2 * rows] = gate_t.astype(BF)


def act_kernel(half, idx, saved_ref, keep_ref, send_ref):
    x = idx[1]
    width = 2 * half
    for out, side in ((send_ref, 1 - x), (keep_ref, x)):
        at = pl.multiple_of(side * half, 128)
        for e in range(saved_ref.shape[2]):
            g = saved_ref[0, 0, e, :, pl.ds(at, half)].astype(F32)
            u = saved_ref[0, 0, e, :, pl.ds(pl.multiple_of(width + at, 128), half)].astype(F32)
            out[e] = (g * lax.logistic(g) * u).astype(BF)


def pair_kernel(keep_ref, got_ref, out_ref):
    both = jnp.concatenate([keep_ref[0], got_ref[0]], axis=0)
    out_ref[0] = both.astype(F32).T.astype(BF)


def pick(meta, row):
    rows = lax.broadcasted_iota(jnp.int32, meta.shape, 0)
    return jnp.sum(jnp.where(rows == row, meta, 0.0), axis=0, keepdims=True)


def spread(meta, expert, rows):
    line = pick(meta, expert)
    slots = lax.broadcasted_iota(jnp.int32, (CAP, rows), 0).astype(F32)
    hot = slots == line[:, 0:rows]
    return hot, jnp.where(hot, line[:, rows : 2 * rows], 0.0)


def route_kernel(
    rows, places, count, half, cut, idx, a_ref, b_ref, c_ref, own_ref, *refs
):
    others, (part_ref, weighted_ref, routed) = refs[:-3], refs[-3:]
    other = others[0][0]
    if len(others) == 2:
        other = jnp.where(pl.program_id(0) >= cut, others[1][0], other)
    x, m = idx[1], idx[2]
    expert = m * count + pl.program_id(0)
    lots = [(r, i) for r in (a_ref, b_ref, c_ref) for i in range(r.shape[0])]
    sources = len(places) // 2
    for at, (jx, jm) in enumerate(places):
        ref, i = lots[at]
        meta = ref[i, rows : rows + META, 0 : 2 * rows].astype(F32)
        hot, gated = spread(meta, expert, rows)
        both = jnp.concatenate([hot.astype(BF), gated.astype(BF)], axis=0)
        got = dot(both, ref[i, 0:rows, :]).astype(BF)
        row = (jx * sources + jm) * CAP
        routed[row : row + CAP, :] = got[0:CAP]
        weighted_ref[0, row : row + CAP, :] = got[CAP:]
    depth = own_ref.shape[1]
    mine = pl.ds(pl.multiple_of(x * depth, 128), depth)
    theirs = pl.ds(pl.multiple_of((1 - x) * depth, 128), depth)
    own = own_ref[0, :, pl.ds(pl.multiple_of(x * half, 128), half)]
    back = dot(routed[:, mine], own) + dot(routed[:, theirs], other)
    size = sources * CAP
    part_ref[0, 0] = back[0:size].astype(part_ref.dtype)
    part_ref[1, 0] = back[size:].astype(part_ref.dtype)


def grad_kernel(rows_of, idx, *refs):
    keep_ref, send_ref, total = refs[-3:]
    refs = list(refs[:-3])
    z, x = idx[0], idx[1]
    nz = len(rows_of)
    outer = (z == 0) | (z == nz - 1)
    weighted = [refs.pop(0) for _ in range(nz)]
    acts = []
    for count in rows_of:
        act = refs.pop(0)[0]
        acts.append(jnp.where(outer, act, refs.pop(0)[0]) if count == 2 else act)
    step = min(256, total.shape[0])
    for n in range(0, total.shape[0], step):
        acc = sum(dot(act, w[0, :, n : n + step]) for act, w in zip(acts, weighted))
        total[n : n + step, :] = acc.T.astype(BF)
    depth = total.shape[0] // 2
    keep_ref[0] = total[pl.ds(pl.multiple_of(x * depth, 16), depth), :]
    send_ref[0] = total[pl.ds(pl.multiple_of((1 - x) * depth, 16), depth), :]


def join_kernel(half, idx, keep_ref, got_ref, out_ref):
    x = idx[1]
    out_ref[0, :, pl.ds(pl.multiple_of(x * half, 128), half)] = keep_ref[0]
    out_ref[0, :, pl.ds(pl.multiple_of((1 - x) * half, 128), half)] = got_ref[0]


def last_kernel(rows, half, n_own, first, total, more, idx, saved_ref, meta_ref, *refs):
    owns, other_ref, (pre_ref, score_ref) = refs[:n_own], refs[n_own], refs[n_own + 1 + more :]
    x, m = idx[1], idx[2]
    count = saved_ref.shape[2]
    width = 2 * half
    meta = meta_ref[0].astype(F32)
    r = lax.broadcasted_iota(jnp.int32, (CAP, 128), 0)
    c = lax.broadcasted_iota(jnp.int32, (CAP, 128), 1)
    for e in range(count):
        _, gated = spread(meta, m * total + first + e, rows)
        gate = jnp.sum(gated, axis=1, keepdims=True)
        score = jnp.zeros((CAP, 1), F32)
        for mine in (True, False):
            at = pl.multiple_of((x if mine else 1 - x) * half, 128)
            up_at = pl.multiple_of(width + at, 128)
            if mine:
                back = sum(o[0, e].astype(F32) for o in owns)
            else:
                back = other_ref[e].astype(F32)
            g = saved_ref[0, 0, e, :, pl.ds(at, half)].astype(F32)
            u = saved_ref[0, 0, e, :, pl.ds(up_at, half)].astype(F32)
            sig = lax.logistic(g)
            silu = g * sig
            score = score + jnp.sum(back * (silu * u), axis=1, keepdims=True)
            grad = gate * back
            pre_ref[0, 0, e, :, pl.ds(at, half)] = (grad * u * sig * (1.0 + g * (1.0 - sig))).astype(BF)
            pre_ref[0, 0, e, :, pl.ds(up_at, half)] = (grad * silu).astype(BF)
        score_ref[0, e : e + 1, :] = jnp.sum(jnp.where(r == c, score, 0.0), axis=0, keepdims=True)


def gate_kernel(rows, idx, ids_ref, *refs):
    out_ref = refs[-1]
    m = idx[2]
    cols = named(ids_ref[...], rows)
    r = lax.broadcasted_iota(jnp.int32, (rows, rows), 0)
    c = lax.broadcasted_iota(jnp.int32, (rows, rows), 1)
    before = dot((c < r).astype(BF), sum(cols).astype(BF))
    lanes = lax.broadcasted_iota(jnp.int32, (rows, 128), 1).astype(F32)
    at = lax.broadcasted_iota(jnp.int32, (rows, EXPERTS), 1)
    slots = [jnp.sum(col * before, axis=1, keepdims=True) for col in cols]
    names = [jnp.sum(jnp.where(col > 0.5, at, 0), axis=1, keepdims=True) for col in cols]
    outs = [jnp.zeros((rows, 1), F32) for _ in cols]
    for jm, ref in enumerate(refs[:-1]):
        for e in range(ref.shape[0]):
            expert = (m ^ jm) * ref.shape[0] + e
            line = ref[e : e + 1, :]
            for k in range(len(cols)):
                hit = (lanes == slots[k]) & (names[k] == expert)
                outs[k] = outs[k] + jnp.sum(jnp.where(hit, line, 0.0), axis=1, keepdims=True)
    for k, o in enumerate(outs):
        out_ref[:, k : k + 1] = o


def call(name, kernel, grid, in_specs, out_specs, out_shape, scratch=(), mib=32, alias=None, flops=0, moved=0):
    return pl.pallas_call(
        kernel,
        name=name,
        grid_spec=pltpu.PrefetchScalarGridSpec(
            num_scalar_prefetch=1,
            grid=grid,
            in_specs=in_specs,
            out_specs=out_specs,
            scratch_shapes=list(scratch),
        ),
        out_shape=out_shape,
        compiler_params=params(mib),
        input_output_aliases=alias or {},
        cost_estimate=pl.CostEstimate(flops=flops, bytes_accessed=moved, transcendentals=0),
    )


def after(v, *deps):
    return lax.optimization_barrier((v, *deps))[0]


def whole(shape):
    return pl.BlockSpec(shape, lambda *_: (0,) * len(shape))


def shards(out_grad, expert_ids, gate_weights, saved_acts, down_weight):
    sources = lax.axis_size("expert")
    n_dp = lax.axis_size("dp")
    nz = n_dp // 2
    line = nz == 4
    count, depth, width = down_weight.shape
    half = width // 2
    rows, model = out_grad.shape
    part = model // nz
    top = expert_ids.shape[1]
    size = sources * CAP
    lots, per = 1, count
    cuts = 2 if count % 2 == 0 else 1
    cut = count // cuts
    dp, m = lax.axis_index("dp"), lax.axis_index("expert")
    z, x = dp // 2, dp % 2
    idx = jnp.stack([z, x, m]).astype(jnp.int32)

    def move_z(v, pairs, name):
        with jax.named_scope(name):
            return lax.ppermute(v, "dp", [(2 * a + i, 2 * b + i) for a, b in pairs for i in range(2)])

    def flip_z(v, k, name):
        return move_z(v, [(a, a ^ k) for a in range(nz)], name)

    def flip_x(v, name):
        with jax.named_scope(name):
            return lax.ppermute(v, "dp", [(i, i ^ 1) for i in range(n_dp)])

    def flip_m(v, k, name):
        with jax.named_scope(name):
            return lax.ppermute(v, "expert", [(i, i ^ k) for i in range(sources)])

    inner = [(1, 2), (2, 1)]
    inward = [(0, 1), (3, 2)]
    outward = [(1, 0), (2, 3)]

    act_shape = jax.ShapeDtypeStruct((count, size, half), BF)
    act_spec = pl.BlockSpec((count, CAP, half), lambda j, idx: (0, j, 0))
    saved_spec = pl.BlockSpec((1, 1, count, CAP, 2 * width), lambda j, idx: (0, idx[2] ^ j, 0, 0, 0))
    keep, send = call(
        "act",
        functools.partial(act_kernel, half),
        (sources,),
        [saved_spec],
        [act_spec, act_spec],
        [act_shape, act_shape],
    )(idx, saved_acts)

    pieces = call(
        "pack",
        functools.partial(pack_kernel, rows, part),
        (1,),
        [whole((rows, model)), whole((rows, top)), whole((rows, top))],
        [whole((rows + META, part))] * nz,
        [jax.ShapeDtypeStruct((rows + META, part), BF)] * nz,
    )(idx, out_grad, expert_ids, gate_weights)

    bits = []
    bit = sources // 2
    while bit:
        bits.append(bit)
        bit //= 2
    def order_of(steps):
        seen = [(0, 0)]
        for bit in steps:
            seen = seen + [(jx ^ (bit == 0), jm ^ bit) for jx, jm in seen]
        return seen

    steps = {k: [0, *bits] if k else [bits[0], 0, *bits[1:]] for k in range(nz)}
    places = {k: order_of(steps[k]) for k in range(nz)}
    nb = 2 * sources
    parts, weighted = {}, {}
    near, far = {}, {}

    def route(k):
        blocks = pl.BlockSpec((nb // 2, rows + META, part), lambda e, idx: (0, 0, 0))
        quarter = pl.BlockSpec((nb // 4, rows + META, part), lambda e, idx: (0, 0, 0))
        wire = k and (k == nz - 1 or not line)
        out = call(
            f"route{k}",
            functools.partial(route_kernel, rows, places[k], count, half, cut),
            (count,),
            [blocks, quarter, quarter, pl.BlockSpec((1, depth, width), lambda e, idx: (e, 0, 0))]
            + [
                pl.BlockSpec((1, depth, half), lambda e, idx, i=i: (jnp.clip(e - i * cut, 0, cut - 1), 0, 0))
                for i in range(cuts)
            ],
            [
                pl.BlockSpec((2, 1, size, half), lambda e, idx: (0, e, 0, 0)),
                pl.BlockSpec((1, 2 * size, part), lambda e, idx: (e, 0, 0)),
            ],
            [
                jax.ShapeDtypeStruct((2, count, size, half), BF if wire else F32),
                jax.ShapeDtypeStruct((count, 2 * size, part), BF),
            ],
            [pltpu.VMEM((2 * size, part), BF)],
        )(idx, near[k], *far[k], down_weight, *other_w)
        weighted[k] = out[1]
        return out[0]

    weights = [
        lax.dynamic_slice(down_weight, (h * cut, 0, (1 - x) * half), (cut, depth, half))
        for h in range(cuts)
    ]
    first = nz - 1
    come = {0: pieces[0], first: flip_z(pieces[first], first, f"rows{first}_z")}
    act_got = flip_x(send, "act_x")
    other_w = [flip_x(weights[0], "weight0_x")]
    flat_spec = pl.BlockSpec((1, size, half), lambda e: (e, 0, 0))
    pair_spec = pl.BlockSpec((1, half, 2 * size), lambda e: (e, 0, 0))
    own_act = pl.pallas_call(
        pair_kernel,
        name="pair",
        grid=(count,),
        in_specs=[flat_spec, flat_spec],
        out_specs=pair_spec,
        out_shape=jax.ShapeDtypeStruct((count, half, 2 * size), BF),
        compiler_params=params(32),
    )(keep, act_got)
    if line:
        r1 = flip_z(own_act, 1, "act_z_r1")
        i3 = move_z(after(own_act, come[3]), inner, "act_z_i3")
        come[1] = flip_z(after(pieces[1], r1), 1, "rows1_z")
    else:
        for k in range(first - 1, 0, -1):
            come[k] = flip_z(after(pieces[k], come[first]), k, f"rows{k}_z")
        acts = [[own_act]] + [[flip_z(own_act, k, f"act_z{k}")] for k in range(1, nz)]

    def plus(v, got):
        return (v.astype(F32) + got.astype(F32)).astype(BF)

    ties = {}

    chains = {"x": [], "y": []}

    def stage(k, at):
        bit = steps[k][at]
        link = "x" if bit == 0 else "y" if bit == bits[0] else "c"
        tied = [*chains.get(link, []), *ties.get((link, k), [])]
        if at == 0:
            v = after(come[k][None], *tied)
        else:
            v = jnp.concatenate([near[k], *(after(u, *tied) for u in far[k])], axis=0)
        sent = [v]
        if at == len(steps[k]) - 1:
            sent = [v[: v.shape[0] // 2], v[v.shape[0] // 2 :]]
        if bit == 0:
            far[k] = [flip_x(u, f"rows{k}_x") for u in sent]
        else:
            far[k] = [flip_m(u, bit, f"rows{k}_expert{bit}") for u in sent]
        near[k] = v
        if link in chains:
            chains[link] = [far[k][-1]]

    def rest(k, start):
        for at in range(start, len(steps[k])):
            stage(k, at)

    if line:
        stage(0, 0)
    stage(first, 0)
    come3_x = far[first][0]
    if line:
        come[2] = flip_z(after(pieces[2], come3_x), 2, "rows2_z")
        ties["y", 3] = [other_w[0]]
        ties["c", 3] = [r1, i3]
    if cuts > 1:
        other_w.append(flip_x(after(weights[1], other_w[0], come3_x), "weight1_x"))
        chains["x"] = [other_w[-1]]
    rest(first, 1)
    parts[first, 0] = route(first)
    if line:
        s1 = [move_z(parts[3, 0], inward, "back_s1")]
        ties["x", 2] = [parts[3, 0]]
        stage(2, 0)
        o2 = move_z(i3, outward, "act_z_o2")
        i2 = move_z(r1, inner, "act_z_i2")
        stage(1, 0)
        stage(0, 1)
        come1_x, come0_x = far[1][0], far[0][0]
        stage(2, 1)
        ties["c", 2] = [come1_x, come0_x, *s1, o2, i2]
        rest(2, 2)
        parts[2, 0] = route(2)
        v2 = [plus(parts[2, 0], s1[0])]
        s2_in = [move_z(v2[0], inward, "back_s2_in")]
        s2_mid = [move_z(v2[0], inner, "back_s2_mid")]
        stage(1, 1)
        o3 = move_z(after(i2, *s1), outward, "act_z_o3")
        ties["c", 1] = [parts[2, 0]]
        rest(1, 2)
        acts = [[own_act], [r1], [o2, i2], [o3, i3]]
        parts[1, 0] = route(1)
        ties["c", 0] = [*far[1]]
        rest(0, 2)
        near[0] = after(near[0], o3)
        parts[0, 0] = route(0)
    else:
        for k in range(first - 1, -1, -1):
            rest(k, 0)
            parts[k, 0] = route(k)

    flat = [weighted[k] for k in range(nz)]
    specs = [pl.BlockSpec((1, 2 * size, part), lambda e, idx: (e, 0, 0))] * nz
    for act in acts:
        flat += act
        specs += [pl.BlockSpec((1, half, 2 * size), lambda e, idx: (e, 0, 0))] * len(act)
    g_spec = pl.BlockSpec((1, depth, half), lambda e, idx: (e, 0, 0))
    g_shape = jax.ShapeDtypeStruct((count, depth, half), BF)
    g_keep, g_send = call(
        "down_grad",
        functools.partial(grad_kernel, [len(a) for a in acts]),
        (count,),
        specs,
        [g_spec, g_spec],
        [g_shape, g_shape],
        [pltpu.VMEM((part, half), BF)],
        mib=60,
        flops=2 * count * nz * 2 * size * part * half,
        moved=sum(v.size * 2 for v in flat),
    )(idx, *flat)
    if line:
        v3 = [plus(parts[1, h], s2_mid[h]) for h in range(lots)]
        v4 = [plus(parts[3, h], s2_in[h]) for h in range(lots)]
        v3[0] = after(v3[0], g_send)
        v4[0] = after(v4[0], g_send)
        got = [
            [flip_z(v3[h], 1, f"back{h}_s3_flip"), move_z(v4[h], inner, f"back{h}_s3_mid")]
            for h in range(lots)
        ]
    else:
        got = [[flip_z(parts[k, h], k, f"back{h}_{k}") for k in range(1, nz)] for h in range(lots)]
    owns = [[parts[0, h]] + got[h] for h in range(lots)]

    g_got = flip_x(g_send, "grad_x")
    down_grad = call(
        "join",
        functools.partial(join_kernel, half),
        (count,),
        [g_spec, g_spec],
        pl.BlockSpec((1, depth, width), lambda e, idx: (e, 0, 0)),
        jax.ShapeDtypeStruct((count, depth, width), BF),
    )(idx, g_keep, g_got)

    outgoing = [sum(o[1].astype(F32) for o in own).astype(BF) for own in owns]
    outgoing[0] = after(outgoing[0], g_send)
    other = [flip_x(outgoing[h], f"back{h}_x") for h in range(lots)]

    order = {jm: at for at, (jx, jm) in enumerate(places[0]) if jx == 0}
    blocks = [(v, i) for v in (near[0], *far[0]) for i in range(v.shape[0])]

    def meta_of(jm):
        ref, i = blocks[order[jm]]
        return ref[i, rows:, 0 : 2 * rows]

    meta = jnp.stack([meta_of(jm) for jm in range(sources)])
    own_spec = pl.BlockSpec((1, per, CAP, half), lambda j, idx: (0, 0, j, 0))
    pre_grads = None
    scores = []
    for h in range(lots):
        piece = pl.BlockSpec(
            (1, 1, per, CAP, 2 * width), lambda j, idx, h=h: (0, idx[2] ^ j, h, 0, 0)
        )
        pre_grads, score = call(
            f"owner{h}",
            functools.partial(last_kernel, rows, half, len(owns[h]), h * per, count, h > 0),
            (sources,),
            [piece, pl.BlockSpec((1, META, 2 * rows), lambda j, idx: (j, 0, 0))]
            + [own_spec] * len(owns[h])
            + [pl.BlockSpec((per, CAP, half), lambda j, idx: (0, j, 0))]
            + [pl.BlockSpec(memory_space=pl.ANY)] * (h > 0),
            [piece, pl.BlockSpec((1, per, 128), lambda j, idx: (j, 0, 0))],
            [
                jax.ShapeDtypeStruct(saved_acts.shape, BF),
                jax.ShapeDtypeStruct((sources, per, 128), F32),
            ],
            alias={len(owns[h]) + 4: 0} if h else {},
        )(idx, saved_acts, meta, *owns[h], other[h], *([pre_grads] if h else []))
        scores.append(score)
    scores = jnp.concatenate(scores, axis=1)
    returned = [scores[0]] + [flip_m(scores[j], j, f"score{j}") for j in range(1, sources)]
    gate_grad = call(
        "gate_grad",
        functools.partial(gate_kernel, rows),
        (1,),
        [whole((rows, top))] + [whole((count, 128))] * sources,
        whole((rows, top)),
        jax.ShapeDtypeStruct((rows, top), F32),
    )(idx, expert_ids, *returned)
    return (pre_grads, down_grad, gate_grad)


def solution(mesh):
    placed = (
        P(("dp", "expert"), None),
        P(("dp", "expert"), None),
        P(("dp", "expert"), None),
        P("dp", None, "expert", None, None),
        P("expert", "dp", None),
    )
    return jax.shard_map(
        shards,
        mesh=mesh,
        in_specs=placed,
        out_specs=(
            P("dp", None, "expert", None, None),
            P("expert", "dp", None),
            P(("dp", "expert"), None),
        ),
        check_vma=False,
    )
```

time: 288 us -> 232 us (0.81)
  starting transfers between devices: 92.7 us -> 56 us
  waiting for transfers between devices: 121 us -> 108 us
  other arithmetic: 12.3 us -> 5.66 us
    ppermute x13, starting transfers between devices: 75.2 us -> 37 us  [move_z(): lax.ppermute(v, 'dp', [(2 * a + i, 2 * b + i) for a, b in pairs for i in...]
    ppermute x8 -> x9, waiting for transfers between devices: 78.2 us -> 41.3 us  [flip_x(): return lax.ppermute(v, 'dp', [(i, i ^ 1) for i in range(n_dp)])]
    ppermute x11 -> x15, waiting for transfers between devices: 8 us -> 28.4 us  [flip_m(): return lax.ppermute(v, 'expert', [(i, i ^ k) for i in range(sources)])]
    select_n x1 -> x0, other arithmetic: 3.91 us -> none  [shards(): jnp.where(x == 0, jnp.concatenate([g_keep, g_got], axis=2), jnp.concatena...]
    ppermute x13, waiting for transfers between devices: 35.1 us -> 38.4 us  [move_z(): lax.ppermute(v, 'dp', [(2 * a + i, 2 * b + i) for a, b in pairs for i in...]
    ppermute x11 -> x15, starting transfers between devices: 6.37 us -> 9.21 us  [flip_m(): return lax.ppermute(v, 'expert', [(i, i ^ k) for i in range(sources)])]
    pallas_call x9 -> x11, Pallas kernels: 44 us -> 46.1 us  [the longest x4 20.6 us: route(): call(f'route{k}', functools.partial(route_kernel, rows, places[k], count,...]
    unnamed x49 -> x59, local copies, waits for them, and re-layouts: 12.1 us -> 10.4 us
  transfers between devices with their start and end apart: 32 -> 37, of which waited for: 13 -> 14; matrix products, arithmetic and copies ran while one was open for 5% -> 4% of each run, Pallas kernels for 14% -> 18%
where the time goes in v2:
time: 232 us
  waiting for transfers between devices  108 us (47%)
  starting transfers between devices  56 us (24%)
  Pallas kernels  46.1 us (20%)
  local copies, waits for them, and re-layouts  14.6 us (6%)
  other arithmetic  5.66 us (2%)
    ppermute x9, waiting for transfers between devices, flip_x(): return lax.ppermute(v, 'dp', [(i, i ^ 1) for i in range(n_dp)])  41.3 us
    ppermute x13, waiting for transfers between devices, move_z(): lax.ppermute(v, 'dp', [(2 * a + i, 2 * b + i) for a, b in pairs for i in...  38.4 us
    ppermute x13, starting transfers between devices, move_z(): lax.ppermute(v, 'dp', [(2 * a + i, 2 * b + i) for a, b in pairs for i in...  37 us
    ppermute x15, waiting for transfers between devices, flip_m(): return lax.ppermute(v, 'expert', [(i, i ^ k) for i in range(sources)])  28.4 us
    pallas_call x4, Pallas kernels, route(): call(f'route{k}', functools.partial(route_kernel, rows, places[k], count,...  20.6 us
    pallas_call x1, Pallas kernels, shards(): call('down_grad', functools.partial(grad_kernel, [len(a) for a in acts]),...  12.7 us
    unnamed x59, local copies, waits for them, and re-layouts  10.4 us
    ppermute x9, starting transfers between devices, flip_x(): return lax.ppermute(v, 'dp', [(i, i ^ 1) for i in range(n_dp)])  9.79 us
  transfers between devices with their start and end apart: 37, of which 14 were waited for; matrix products, arithmetic and copies ran while one was open for 4% of the time, Pallas kernels for 18%

profile of v2, /device:TPU:0, one launch (start us, length us, event | category | flops | bytes accessed | tf_op | source)
XLA Modules:
  0.0 231.5 jit_solution(380263716326207600)
XLA Ops:
  4.8 2.9 %collective-permute-start.1 = (bf16[4,192,384]{2,1,0:T(8,128)(2,1)}, bf16[4,192,384]{2,1,0:T(8,128)(2,1)S(1)}, u32[]{:S(2)}, u32[]{:S(2)}) collective-permute-start(bf16[4,192,384]{2,1,0:T(8,128)(2,1)} %get-tuple-element.43), channel_id=1, source_target_pairs={{0,4},{4,0},{8,12},{12,8},{16,20},{20,16},{24,28},{28,24},{1,5},{5... | collective-permute-start | bytes 1769480 | tf_op jit(solution)/shard_map/act_x/ppermute | solution.py:246
  7.7 2.8 %constant_dynamic-slice_fusion = (bf16[2,512,384]{2,1,0:T(8,128)(2,1)}, bf16[2,512,384]{2,1,0:T(8,128)(2,1)}) fusion(bf16[4,512,768]{2,1,0:T(8,128)(2,1)} %own_ref.7, s32[]{:T(128)S(6)} %select_n.17), kind=kLoop, calls=%fused_computation.21 | loop fusion | bytes 3145732 | tf_op jit(solution)/shard_map/dynamic_slice | solution.py:321
  11.6 4.1 %collective-permute-start.4 = (bf16[144,1024]{1,0:T(8,128)(2,1)S(1)}, bf16[144,1024]{1,0:T(8,128)(2,1)S(1)}, u32[]{:S(2)}, u32[]{:S(2)}) collective-permute-start(bf16[144,1024]{1,0:T(8,128)(2,1)S(1)} %get-tuple-element.46), channel_id=1, source_target_pairs={{0,24},{4,28},{8,16},{12,20},{16,8},{20,12},{24,0},{28,4},{1,25},{... | collective-permute-start | bytes 884744 | tf_op jit(solution)/shard_map/rows3_z/ppermute | solution.py:239
  15.8 6.3 %collective-permute-done.1.got_ref = bf16[4,192,384]{2,1,0:T(8,128)(2,1)S(1)} collective-permute-done((bf16[4,192,384]{2,1,0:T(8,128)(2,1)}, bf16[4,192,384]{2,1,0:T(8,128)(2,1)S(1)}, u32[]{:S(2)}, u32[]{:S(2)}) %collective-permute-start.1) | collective-permute-done | bytes 589856 | tf_op jit(solution)/shard_map/act_x/ppermute | solution.py:246
  23.6 8.2 %collective-permute-start.2 = (bf16[4,384,384]{2,1,0:T(8,128)(2,1)S(1)}, bf16[4,384,384]{2,1,0:T(8,128)(2,1)S(1)}, u32[]{:S(2)}, u32[]{:S(2)}) collective-permute-start(bf16[4,384,384]{2,1,0:T(8,128)(2,1)S(1)} %pair.1.refs_4_), channel_id=1, source_target_pairs={{0,8},{4,12},{8,0},{12,4},{16,24},{20,28},{24,16},{28,20},{1,9},{5... | collective-permute-start | bytes 3538952 | tf_op jit(solution)/shard_map/act_z_r1/ppermute | solution.py:239
  34.8 3.7 %collective-permute-done = bf16[1,144,1024]{2,1,0:T(8,128)(2,1)S(1)} collective-permute-done((bf16[1,144,1024]{2,1,0:T(8,128)(2,1)S(1)}, bf16[1,144,1024]{2,1,0:T(8,128)(2,1)S(1)}, u32[]{:S(2)}, u32[]{:S(2)}) %collective-permute-start) | collective-permute-done | bytes 294944 | tf_op jit(solution)/shard_map/rows0_expert2/ppermute | solution.py:250
  38.5 5.9 %collective-permute-done.5 = bf16[1,144,1024]{2,1,0:T(8,128)(2,1)S(1)} collective-permute-done((bf16[1,144,1024]{2,1,0:T(8,128)(2,1)S(1)}, bf16[1,144,1024]{2,1,0:T(8,128)(2,1)S(1)}, u32[]{:S(2)}, u32[]{:S(2)}) %collective-permute-start.5) | collective-permute-done | bytes 294944 | tf_op jit(solution)/shard_map/rows3_x/ppermute | solution.py:246
  47.8 11.2 %collective-permute-done.9 = bf16[2,144,1024]{2,1,0:T(8,128)(2,1)S(1)} collective-permute-done((bf16[2,144,1024]{2,1,0:T(8,128)(2,1)S(1)}, bf16[2,144,1024]{2,1,0:T(8,128)(2,1)S(1)}, u32[]{:S(2)}, u32[]{:S(2)}) %collective-permute-start.9) | collective-permute-done | bytes 589856 | tf_op jit(solution)/shard_map/rows3_expert2/ppermute | solution.py:250
  64.5 5.1 %route3.1 = (bf16[2,4,192,384]{3,2,1,0:T(8,128)(2,1)S(1)}, bf16[4,384,1024]{2,1,0:T(8,128)(2,1)S(1)}) custom-call(s32[3]{0:T(128)S(1)} %pad_add_fusion.idx, bf16[4,144,1024]{2,1,0:T(8,128)(2,1)S(1)} %pad_maximum_fusion.a_ref, bf16[2,144,1024]{2,1,0:T(8,128)(2,1)S(1)} %collective-permute-done.11.b_ref, ...), custom_call_target="tpu_custom_call" | custom-call | tf_op jit(solution)/shard_map/route3/pallas_call | solution.py:298
  71.3 4.7 %collective-permute-done.6 = bf16[144,1024]{1,0:T(8,128)(2,1)S(1)} collective-permute-done((bf16[144,1024]{1,0:T(8,128)(2,1)S(1)}, bf16[144,1024]{1,0:T(8,128)(2,1)S(1)}, u32[]{:S(2)}, u32[]{:S(2)}) %collective-permute-start.6) | collective-permute-done | bytes 294944 | tf_op jit(solution)/shard_map/rows2_z/ppermute | solution.py:239
  79.4 8.3 %collective-permute-start.19 = (bf16[2,4,192,384]{3,2,1,0:T(8,128)(2,1)S(1)}, bf16[2,4,192,384]{3,2,1,0:T(8,128)(2,1)S(1)}, u32[]{:S(2)}, u32[]{:S(2)}) collective-permute-start(bf16[2,4,192,384]{3,2,1,0:T(8,128)(2,1)S(1)} %get-tuple-element.52), channel_id=1, source_target_pairs={{0,8},{4,12},{24,16},{28,20},{1,9},{5,13},{25,17},{29,21},{2,10},{... | collective-permute-start | bytes 3538952 | tf_op jit(solution)/shard_map/back_s1/ppermute | solution.py:239
  90.0 5.7 %collective-permute-done.14 = bf16[1,144,1024]{2,1,0:T(8,128)(2,1)S(1)} collective-permute-done((bf16[1,144,1024]{2,1,0:T(8,128)(2,1)S(1)}, bf16[1,144,1024]{2,1,0:T(8,128)(2,1)S(1)}, u32[]{:S(2)}, u32[]{:S(2)}) %collective-permute-start.14) | collective-permute-done | bytes 294944 | tf_op jit(solution)/shard_map/rows1_x/ppermute | solution.py:246
  96.4 6.0 %collective-permute-done.16 = bf16[2,144,1024]{2,1,0:T(8,128)(2,1)S(1)} collective-permute-done((bf16[2,144,1024]{2,1,0:T(8,128)(2,1)S(1)}, bf16[2,144,1024]{2,1,0:T(8,128)(2,1)S(1)}, u32[]{:S(2)}, u32[]{:S(2)}) %collective-permute-start.16) | collective-permute-done | bytes 589856 | tf_op jit(solution)/shard_map/rows2_expert2/ppermute | solution.py:250
  102.4 4.0 %collective-permute-done.20.refs_6_ = bf16[4,384,384]{2,1,0:T(8,128)(2,1)S(1)} collective-permute-done((bf16[4,384,384]{2,1,0:T(8,128)(2,1)S(1)}, bf16[4,384,384]{2,1,0:T(8,128)(2,1)S(1)}, u32[]{:S(2)}, u32[]{:S(2)}) %collective-permute-start.20) | collective-permute-done | bytes 1179680 | tf_op jit(solution)/shard_map/act_z_o2/ppermute | solution.py:239
  109.1 3.2 %collective-permute-done.19 = bf16[2,4,192,384]{3,2,1,0:T(8,128)(2,1)S(1)} collective-permute-done((bf16[2,4,192,384]{3,2,1,0:T(8,128)(2,1)S(1)}, bf16[2,4,192,384]{3,2,1,0:T(8,128)(2,1)S(1)}, u32[]{:S(2)}, u32[]{:S(2)}) %collective-permute-start.19) | collective-permute-done | bytes 1179680 | tf_op jit(solution)/shard_map/back_s1/ppermute | solution.py:239
  115.6 5.1 %route2.1 = (f32[2,4,192,384]{3,2,1,0:T(8,128)S(1)}, bf16[4,384,1024]{2,1,0:T(8,128)(2,1)S(1)}) custom-call(s32[3]{0:T(128)S(1)} %pad_add_fusion.idx, bf16[4,144,1024]{2,1,0:T(8,128)(2,1)S(1)} %pad_maximum_fusion.1.a_ref, bf16[2,144,1024]{2,1,0:T(8,128)(2,1)S(1)} %collective-permute-done.22.b_ref, bf16[2,144,1024]{2,1,0:T(8,128)(2,1)S(1)} %collective-permute-done.23.c_ref, ...), custom_call_target="tpu_custom_call" | custom-call | tf_op jit(solution)/shard_map/route2/pallas_call | solution.py:298
  120.7 7.4 %collective-permute-done.18 = bf16[2,144,1024]{2,1,0:T(8,128)(2,1)S(1)} collective-permute-done((bf16[2,144,1024]{2,1,0:T(8,128)(2,1)S(1)}, bf16[2,144,1024]{2,1,0:T(8,128)(2,1)S(1)}, u32[]{:S(2)}, u32[]{:S(2)}) %collective-permute-start.18) | collective-permute-done | bytes 589856 | tf_op jit(solution)/shard_map/rows1_expert2/ppermute | solution.py:250
  129.4 5.4 %collective-permute-start.30 = (bf16[2,4,192,384]{3,2,1,0:T(8,128)(2,1)}, bf16[2,4,192,384]{3,2,1,0:T(8,128)(2,1)}, u32[]{:S(2)}, u32[]{:S(2)}) collective-permute-start(bf16[2,4,192,384]{3,2,1,0:T(8,128)(2,1)} %add_convert_fusion.2), channel_id=1, source_target_pairs={{0,8},{4,12},{24,16},{28,20},{1,9},{5,13},{25,17},{29,21},{2,10},{... | collective-permute-start | bytes 3538952 | tf_op jit(solution)/shard_map/back_s2_in/ppermute | solution.py:239
  137.2 5.1 %route1.1 = (f32[2,4,192,384]{3,2,1,0:T(8,128)S(1)}, bf16[4,384,1024]{2,1,0:T(8,128)(2,1)S(1)}) custom-call(s32[3]{0:T(128)S(1)} %pad_add_fusion.idx, bf16[4,144,1024]{2,1,0:T(8,128)(2,1)S(1)} %pad_maximum_fusion.3.a_ref, bf16[2,144,1024]{2,1,0:T(8,128)(2,1)S(1)} %collective-permute-done.17.b_ref, bf16[2,144,1024]{2,1,0:T(8,128)(2,1)S(1)} %collective-permute-done.24.c_ref, ...), custom_call_target="tpu_custom_call" | custom-call | tf_op jit(solution)/shard_map/route1/pallas_call | solution.py:298
  146.6 5.1 %route0.1 = (f32[2,4,192,384]{3,2,1,0:T(8,128)S(1)}, bf16[4,384,1024]{2,1,0:T(8,128)(2,1)S(1)}) custom-call(s32[3]{0:T(128)S(1)} %pad_add_fusion.idx, bf16[4,144,1024]{2,1,0:T(8,128)(2,1)S(1)} %pad_maximum_fusion.2.a_ref, bf16[2,144,1024]{2,1,0:T(8,128)(2,1)S(1)} %collective-permute-done.26.b_ref, bf16[2,144,1024]{2,1,0:T(8,128)(2,1)S(1)} %collective-permute-done.27.c_ref, ...), custom_call_target="tpu_custom_call" | custom-call | tf_op jit(solution)/shard_map/route0/pallas_call | solution.py:298
  153.4 12.7 %down_grad.1 = (bf16[4,512,384]{2,1,0:T(8,128)(2,1)}, bf16[4,512,384]{2,1,0:T(8,128)(2,1)}) custom-call(s32[3]{0:T(128)} %copy-done.16, bf16[4,384,1024]{2,1,0:T(8,128)(2,1)} %copy-done.8, bf16[4,384,1024]{2,1,0:T(8,128)(2,1)} %copy-done.7, bf16[4,384,1024]{2,1,0:T(8,128)(2,1)} %copy-done.6, bf16[4,384,1024]{2,1,0:T(8,128)(2,1)} %copy-done.5, ...), custom_call_target="tpu_custom_call" | custom-call | flops 4831838208 | bytes 19660800 | tf_op jit(solution)/shard_map/down_grad/pallas_call | solution.py:429
  171.5 26.5 %collective-permute-done.29.refs_1_ = bf16[2,4,192,384]{3,2,1,0:T(8,128)(2,1)S(1)} collective-permute-done((bf16[2,4,192,384]{3,2,1,0:T(8,128)(2,1)S(1)}, bf16[2,4,192,384]{3,2,1,0:T(8,128)(2,1)S(1)}, u32[]{:S(2)}, u32[]{:S(2)}) %collective-permute-start.29) | collective-permute-done | bytes 1179680 | tf_op jit(solution)/shard_map/back0_s3_flip/ppermute | solution.py:239
  200.4 19.8 %collective-permute-done.32.refs_3_ = bf16[4,192,384]{2,1,0:T(8,128)(2,1)S(1)} collective-permute-done((bf16[4,192,384]{2,1,0:T(8,128)(2,1)S(1)}, bf16[4,192,384]{2,1,0:T(8,128)(2,1)S(1)}, u32[]{:S(2)}, u32[]{:S(2)}) %collective-permute-start.32) | collective-permute-done | bytes 589856 | tf_op jit(solution)/shard_map/back0_x/ppermute | solution.py:246
  220.2 4.0 %owner0.1 = (bf16[1,4,4,48,1536]{4,3,2,1,0:T(8,128)(2,1)}, f32[4,4,128]{2,1,0:T(4,128)S(1)}) custom-call(s32[3]{0:T(128)S(1)} %copy-done.17, bf16[1,4,4,48,1536]{4,3,2,1,0:T(8,128)(2,1)S(1)} %copy-done.2, bf16[4,16,256]{2,1,0:T(8,128)(2,1)S(1)} %pad_maximum_fusion.6.meta_ref, f32[2,4,192,384]{3,2,1,0:T(8,128)S(1)} %get-tuple-element.64.refs_0_, ...), custom_call_target="tpu_custom_call" | custom-call | tf_op jit(solution)/shard_map/owner0/pallas_call | solution.py:483
  (138 shorter events, 57.0 us)
Async XLA Ops:
  4.8 17.3 %collective-permute-start.1 = (bf16[4,192,384]{2,1,0:T(8,128)(2,1)}, bf16[4,192,384]{2,1,0:T(8,128)(2,1)S(1)}, u32[]{:S(2)}, u32[]{:S(2)}) collective-permute-start(bf16[4,192,384]{2,1,0:T(8,128)(2,1)} %get-tuple-element.43), channel_id=1, source_target_pairs={{0,4},{4,0},{8,12},{12,8},{16,20},{20,16},{24,28},{28,24},{1,5},{5... | collective-permute-start | bytes 1769480 | tf_op jit(solution)/shard_map/act_x/ppermute | solution.py:246
  10.5 33.9 %collective-permute-start.7 = (bf16[2,512,384]{2,1,0:T(8,128)(2,1)}, bf16[2,512,384]{2,1,0:T(8,128)(2,1)S(1)}, u32[]{:S(2)}, u32[]{:S(2)}) collective-permute-start(bf16[2,512,384]{2,1,0:T(8,128)(2,1)} %get-tuple-element.80), channel_id=1, source_target_pairs={{0,4},{4,0},{8,12},{12,8},{16,20},{20,16},{24,28},{28,24},{1,5},{5... | collective-permute-start | bytes 2359304 | tf_op jit(solution)/shard_map/weight0_x/ppermute | solution.py:246
  22.8 36.3 %collective-permute-start.10 = (bf16[4,384,384]{2,1,0:T(8,128)(2,1)S(1)}, bf16[4,384,384]{2,1,0:T(8,128)(2,1)S(1)}, u32[]{:S(2)}, u32[]{:S(2)}) collective-permute-start(bf16[4,384,384]{2,1,0:T(8,128)(2,1)S(1)} %pair.1.refs_4_), channel_id=1, source_target_pairs={{8,16},{12,20},{16,8},{20,12},{9,17},{13,21},{17,9},{21,13},{10,18... | collective-permute-start | bytes 3538952 | tf_op jit(solution)/shard_map/act_z_i3/ppermute | solution.py:239
  23.6 35.5 %collective-permute-start.2 = (bf16[4,384,384]{2,1,0:T(8,128)(2,1)S(1)}, bf16[4,384,384]{2,1,0:T(8,128)(2,1)S(1)}, u32[]{:S(2)}, u32[]{:S(2)}) collective-permute-start(bf16[4,384,384]{2,1,0:T(8,128)(2,1)S(1)} %pair.1.refs_4_), channel_id=1, source_target_pairs={{0,8},{4,12},{8,0},{12,4},{16,24},{20,28},{24,16},{28,20},{1,9},{5... | collective-permute-start | bytes 3538952 | tf_op jit(solution)/shard_map/act_z_r1/ppermute | solution.py:239
  44.5 14.6 %collective-permute-start.9 = (bf16[2,144,1024]{2,1,0:T(8,128)(2,1)S(1)}, bf16[2,144,1024]{2,1,0:T(8,128)(2,1)S(1)}, u32[]{:S(2)}, u32[]{:S(2)}) collective-permute-start(bf16[2,144,1024]{2,1,0:T(8,128)(2,1)S(1)} %pad_maximum_fusion.4), channel_id=1, source_target_pairs={{0,2},{1,3},{2,0},{3,1},{4,6},{5,7},{6,4},{7,5},{8,10},{9,11},{10,... | collective-permute-start | bytes 1769480 | tf_op jit(solution)/shard_map/rows3_expert2/ppermute | solution.py:250
  46.3 18.1 %collective-permute-start.8 = (bf16[2,512,384]{2,1,0:T(8,128)(2,1)S(1)}, bf16[2,512,384]{2,1,0:T(8,128)(2,1)S(1)}, u32[]{:S(2)}, u32[]{:S(2)}) collective-permute-start(bf16[2,512,384]{2,1,0:T(8,128)(2,1)S(1)} %copy-done.23), channel_id=1, source_target_pairs={{0,4},{4,0},{8,12},{12,8},{16,20},{20,16},{24,28},{28,24},{1,5},{5... | collective-permute-start | bytes 2359304 | tf_op jit(solution)/shard_map/weight1_x/ppermute | solution.py:246
  47.8 15.6 %collective-permute-start.11 = (bf16[2,144,1024]{2,1,0:T(8,128)(2,1)S(1)}, bf16[2,144,1024]{2,1,0:T(8,128)(2,1)S(1)}, u32[]{:S(2)}, u32[]{:S(2)}) collective-permute-start(bf16[2,144,1024]{2,1,0:T(8,128)(2,1)S(1)} %pad_maximum_fusion.4), channel_id=1, source_target_pairs={{0,1},{1,0},{2,3},{3,2},{4,5},{5,4},{6,7},{7,6},{8,9},{9,8},{10,11... | collective-permute-start | bytes 1769480 | tf_op jit(solution)/shard_map/rows3_expert1/ppermute | solution.py:250
  59.2 16.7 %collective-permute-start.6 = (bf16[144,1024]{1,0:T(8,128)(2,1)S(1)}, bf16[144,1024]{1,0:T(8,128)(2,1)S(1)}, u32[]{:S(2)}, u32[]{:S(2)}) collective-permute-start(bf16[144,1024]{1,0:T(8,128)(2,1)S(1)} %get-tuple-element.47), channel_id=1, source_target_pairs={{0,16},{4,20},{8,24},{12,28},{16,0},{20,4},{24,8},{28,12},{1,17},{... | collective-permute-start | bytes 884744 | tf_op jit(solution)/shard_map/rows2_z/ppermute | solution.py:239
  61.8 26.0 %collective-permute-start.3 = (bf16[144,1024]{1,0:T(8,128)(2,1)S(1)}, bf16[144,1024]{1,0:T(8,128)(2,1)S(1)}, u32[]{:S(2)}, u32[]{:S(2)}) collective-permute-start(bf16[144,1024]{1,0:T(8,128)(2,1)S(1)} %get-tuple-element.44), channel_id=1, source_target_pairs={{0,8},{4,12},{8,0},{12,4},{16,24},{20,28},{24,16},{28,20},{1,9},{5... | collective-permute-start | bytes 884744 | tf_op jit(solution)/shard_map/rows1_z/ppermute | solution.py:239
  77.3 29.1 %collective-permute-start.20 = (bf16[4,384,384]{2,1,0:T(8,128)(2,1)S(1)}, bf16[4,384,384]{2,1,0:T(8,128)(2,1)S(1)}, u32[]{:S(2)}, u32[]{:S(2)}) collective-permute-start(bf16[4,384,384]{2,1,0:T(8,128)(2,1)S(1)} %collective-permute-done.10.refs_9_), channel_id=1, source_target_pairs={{8,0},{12,4},{16,24},{20,28},{9,1},{13,5},{17,25},{21,29},{10,2},{... | collective-permute-start | bytes 3538952 | tf_op jit(solution)/shard_map/act_z_o2/ppermute | solution.py:239
  78.6 27.8 %collective-permute-start.21 = (bf16[4,384,384]{2,1,0:T(8,128)(2,1)S(1)}, bf16[4,384,384]{2,1,0:T(8,128)(2,1)S(1)}, u32[]{:S(2)}, u32[]{:S(2)}) collective-permute-start(bf16[4,384,384]{2,1,0:T(8,128)(2,1)S(1)} %collective-permute-done.2.refs_5_), channel_id=1, source_target_pairs={{8,16},{12,20},{16,8},{20,12},{9,17},{13,21},{17,9},{21,13},{10,18... | collective-permute-start | bytes 3538952 | tf_op jit(solution)/shard_map/act_z_i2/ppermute | solution.py:239
  79.4 32.9 %collective-permute-start.19 = (bf16[2,4,192,384]{3,2,1,0:T(8,128)(2,1)S(1)}, bf16[2,4,192,384]{3,2,1,0:T(8,128)(2,1)S(1)}, u32[]{:S(2)}, u32[]{:S(2)}) collective-permute-start(bf16[2,4,192,384]{3,2,1,0:T(8,128)(2,1)S(1)} %get-tuple-element.52), channel_id=1, source_target_pairs={{0,8},{4,12},{24,16},{28,20},{1,9},{5,13},{25,17},{29,21},{2,10},{... | collective-permute-start | bytes 3538952 | tf_op jit(solution)/shard_map/back_s1/ppermute | solution.py:239
  88.4 14.0 %collective-permute-start.16 = (bf16[2,144,1024]{2,1,0:T(8,128)(2,1)S(1)}, bf16[2,144,1024]{2,1,0:T(8,128)(2,1)S(1)}, u32[]{:S(2)}, u32[]{:S(2)}) collective-permute-start(bf16[2,144,1024]{2,1,0:T(8,128)(2,1)S(1)} %constant_dynamic-update-slice_fusion), channel_id=1, source_target_pairs={{0,2},{1,3},{2,0},{3,1},{4,6},{5,7},{6,4},{7,5},{8,10},{9,11},{10,... | collective-permute-start | bytes 1769480 | tf_op jit(solution)/shard_map/rows2_expert2/ppermute | solution.py:250
  95.8 13.3 %collective-permute-start.15 = (bf16[2,144,1024]{2,1,0:T(8,128)(2,1)S(1)}, bf16[2,144,1024]{2,1,0:T(8,128)(2,1)S(1)}, u32[]{:S(2)}, u32[]{:S(2)}) collective-permute-start(bf16[2,144,1024]{2,1,0:T(8,128)(2,1)S(1)} %pad_maximum_fusion.5), channel_id=1, source_target_pairs={{0,4},{4,0},{8,12},{12,8},{16,20},{20,16},{24,28},{28,24},{1,5},{5... | collective-permute-start | bytes 1769480 | tf_op jit(solution)/shard_map/rows0_x/ppermute | solution.py:246
  102.4 13.2 %collective-permute-start.22 = (bf16[2,144,1024]{2,1,0:T(8,128)(2,1)S(1)}, bf16[2,144,1024]{2,1,0:T(8,128)(2,1)S(1)}, u32[]{:S(2)}, u32[]{:S(2)}) collective-permute-start(bf16[2,144,1024]{2,1,0:T(8,128)(2,1)S(1)} %constant_dynamic-update-slice_fusion), channel_id=1, source_target_pairs={{0,1},{1,0},{2,3},{3,2},{4,5},{5,4},{6,7},{7,6},{8,9},{9,8},{10,11... | collective-permute-start | bytes 1769480 | tf_op jit(solution)/shard_map/rows2_expert1/ppermute | solution.py:250
  112.3 15.8 %collective-permute-start.18 = (bf16[2,144,1024]{2,1,0:T(8,128)(2,1)S(1)}, bf16[2,144,1024]{2,1,0:T(8,128)(2,1)S(1)}, u32[]{:S(2)}, u32[]{:S(2)}) collective-permute-start(bf16[2,144,1024]{2,1,0:T(8,128)(2,1)S(1)} %constant_dynamic-update-slice_fusion.2), channel_id=1, source_target_pairs={{0,2},{1,3},{2,0},{3,1},{4,6},{5,7},{6,4},{7,5},{8,10},{9,11},{10,... | collective-permute-start | bytes 1769480 | tf_op jit(solution)/shard_map/rows1_expert2/ppermute | solution.py:250
  113.9 21.2 %collective-permute-start.17 = (bf16[2,144,1024]{2,1,0:T(8,128)(2,1)S(1)}, bf16[2,144,1024]{2,1,0:T(8,128)(2,1)S(1)}, u32[]{:S(2)}, u32[]{:S(2)}) collective-permute-start(bf16[2,144,1024]{2,1,0:T(8,128)(2,1)S(1)} %constant_dynamic-update-slice_fusion.2), channel_id=1, source_target_pairs={{0,1},{1,0},{2,3},{3,2},{4,5},{5,4},{6,7},{7,6},{8,9},{9,8},{10,11... | collective-permute-start | bytes 1769480 | tf_op jit(solution)/shard_map/rows1_expert1/ppermute | solution.py:250
  114.1 31.3 %collective-permute-start.25 = (bf16[4,384,384]{2,1,0:T(8,128)(2,1)S(1)}, bf16[4,384,384]{2,1,0:T(8,128)(2,1)S(1)}, u32[]{:S(2)}, u32[]{:S(2)}) collective-permute-start(bf16[4,384,384]{2,1,0:T(8,128)(2,1)S(1)} %collective-permute-done.21.refs_7_), channel_id=1, source_target_pairs={{8,0},{12,4},{16,24},{20,28},{9,1},{13,5},{17,25},{21,29},{10,2},{... | collective-permute-start | bytes 3538952 | tf_op jit(solution)/shard_map/act_z_o3/ppermute | solution.py:239
  129.4 36.7 %collective-permute-start.30 = (bf16[2,4,192,384]{3,2,1,0:T(8,128)(2,1)}, bf16[2,4,192,384]{3,2,1,0:T(8,128)(2,1)}, u32[]{:S(2)}, u32[]{:S(2)}) collective-permute-start(bf16[2,4,192,384]{3,2,1,0:T(8,128)(2,1)} %add_convert_fusion.2), channel_id=1, source_target_pairs={{0,8},{4,12},{24,16},{28,20},{1,9},{5,13},{25,17},{29,21},{2,10},{... | collective-permute-start | bytes 3538952 | tf_op jit(solution)/shard_map/back_s2_in/ppermute | solution.py:239
  135.4 32.5 %collective-permute-start.28 = (bf16[2,4,192,384]{3,2,1,0:T(8,128)(2,1)}, bf16[2,4,192,384]{3,2,1,0:T(8,128)(2,1)}, u32[]{:S(2)}, u32[]{:S(2)}) collective-permute-start(bf16[2,4,192,384]{3,2,1,0:T(8,128)(2,1)} %add_convert_fusion.2), channel_id=1, source_target_pairs={{8,16},{12,20},{16,8},{20,12},{9,17},{13,21},{17,9},{21,13},{10,18... | collective-permute-start | bytes 3538952 | tf_op jit(solution)/shard_map/back_s2_mid/ppermute | solution.py:239
  169.9 28.2 %collective-permute-start.29 = (bf16[2,4,192,384]{3,2,1,0:T(8,128)(2,1)S(1)}, bf16[2,4,192,384]{3,2,1,0:T(8,128)(2,1)S(1)}, u32[]{:S(2)}, u32[]{:S(2)}) collective-permute-start(bf16[2,4,192,384]{3,2,1,0:T(8,128)(2,1)S(1)} %add_convert_fusion.1), channel_id=1, source_target_pairs={{0,8},{4,12},{8,0},{12,4},{16,24},{20,28},{24,16},{28,20},{1,9},{5... | collective-permute-start | bytes 3538952 | tf_op jit(solution)/shard_map/back0_s3_flip/ppermute | solution.py:239
  170.0 28.1 %collective-permute-start.31 = (bf16[2,4,192,384]{3,2,1,0:T(8,128)(2,1)S(1)}, bf16[2,4,192,384]{3,2,1,0:T(8,128)(2,1)S(1)}, u32[]{:S(2)}, u32[]{:S(2)}) collective-permute-start(bf16[2,4,192,384]{3,2,1,0:T(8,128)(2,1)S(1)} %add_convert_fusion), channel_id=1, source_target_pairs={{8,16},{12,20},{16,8},{20,12},{9,17},{13,21},{17,9},{21,13},{10,18... | collective-permute-start | bytes 3538952 | tf_op jit(solution)/shard_map/back0_s3_mid/ppermute | solution.py:239
  170.9 55.1 %collective-permute-start.33 = (bf16[4,512,384]{2,1,0:T(8,128)(2,1)S(1)}, bf16[4,512,384]{2,1,0:T(8,128)(2,1)S(1)}, u32[]{:S(2)}, u32[]{:S(2)}) collective-permute-start(bf16[4,512,384]{2,1,0:T(8,128)(2,1)S(1)} %copy-done.26), channel_id=1, source_target_pairs={{0,4},{4,0},{8,12},{12,8},{16,20},{20,16},{24,28},{28,24},{1,5},{5... | collective-permute-start | bytes 4718600 | tf_op jit(solution)/shard_map/grad_x/ppermute | solution.py:246
  198.3 21.8 %collective-permute-start.32 = (bf16[4,192,384]{2,1,0:T(8,128)(2,1)S(1)}, bf16[4,192,384]{2,1,0:T(8,128)(2,1)S(1)}, u32[]{:S(2)}, u32[]{:S(2)}) collective-permute-start(bf16[4,192,384]{2,1,0:T(8,128)(2,1)S(1)} %fusion), channel_id=1, source_target_pairs={{0,4},{4,0},{8,12},{12,8},{16,20},{20,16},{24,28},{28,24},{1,5},{5... | collective-permute-start | bytes 1769480 | tf_op jit(solution)/shard_map/back0_x/ppermute | solution.py:246
  (40 other events, 526.9 us)

commit v3 on v2

--- a/solution.py
+++ b/solution.py
@@ -190,7 +190,7 @@
         out_ref[:, k : k + 1] = o
 
 
-def call(name, kernel, grid, in_specs, out_specs, out_shape, scratch=(), mib=32, alias=None, flops=0, moved=0):
+def call(name, kernel, grid, in_specs, out_specs, out_shape, scratch=(), mib=20, alias=None, flops=0, moved=0):
     return pl.pallas_call(
         kernel,
         name=name,
@@ -313,6 +313,7 @@
                 jax.ShapeDtypeStruct((count, 2 * size, part), BF),
             ],
             [pltpu.VMEM((2 * size, part), BF)],
+            mib=20 if line else 48,
         )(idx, near[k], *far[k], down_weight, *other_w)
         weighted[k] = out[1]
         return out[0]
@@ -334,7 +335,7 @@
         in_specs=[flat_spec, flat_spec],
         out_specs=pair_spec,
         out_shape=jax.ShapeDtypeStruct((count, half, 2 * size), BF),
-        compiler_params=params(32),
+        compiler_params=params(16),
     )(keep, act_got)
     if line:
         r1 = flip_z(own_act, 1, "act_z_r1")
@@ -434,7 +435,7 @@
         [g_spec, g_spec],
         [g_shape, g_shape],
         [pltpu.VMEM((part, half), BF)],
-        mib=60,
+        mib=22 if line else 60,
         flops=2 * count * nz * 2 * size * part * half,
         moved=sum(v.size * 2 for v in flat),
     )(idx, *flat)
@@ -462,7 +463,7 @@
     )(idx, g_keep, g_got)
 
     outgoing = [sum(o[1].astype(F32) for o in own).astype(BF) for own in owns]
-    outgoing[0] = after(outgoing[0], g_send)
+    outgoing[0] = after(outgoing[0], g_got)
     other = [flip_x(outgoing[h], f"back{h}_x") for h in range(lots)]
 
     order = {jm: at for at, (jx, jm) in enumerate(places[0]) if jx == 0}

time: 232 us -> 219 us (0.944)
  local copies, waits for them, and re-layouts: 14.6 us -> 5.43 us
  Pallas kernels: 46.1 us -> 41.8 us
  other arithmetic: 5.66 us -> 1.83 us
  waiting for transfers between devices: 108 us -> 111 us
    unnamed x59 -> x19, local copies, waits for them, and re-layouts: 10.4 us -> 2.63 us
    ppermute x13, waiting for transfers between devices: 38.4 us -> 43.7 us  [move_z(): lax.ppermute(v, 'dp', [(2 * a + i, 2 * b + i) for a, b in pairs for i in...]
    pallas_call x1, Pallas kernels: 12.7 us -> 8.45 us  [shards(): call('down_grad', functools.partial(grad_kernel, [len(a) for a in acts]),...]
    convert_element_type x3, other arithmetic: 4.75 us -> 0.96 us  [plus(): return (v.astype(F32) + got.astype(F32)).astype(BF)]
  transfers between devices with their start and end apart: 37 -> 37, of which waited for: 14 -> 18; matrix products, arithmetic and copies ran while one was open for 4% -> 2% of each run, Pallas kernels for 18% -> 15%
where the time goes in v3:
time: 219 us
  waiting for transfers between devices  111 us (51%)
  starting transfers between devices  57.6 us (26%)
  Pallas kernels  41.8 us (19%)
  local copies, waits for them, and re-layouts  5.43 us (2%)
    ppermute x13, waiting for transfers between devices, move_z(): lax.ppermute(v, 'dp', [(2 * a + i, 2 * b + i) for a, b in pairs for i in...  43.7 us
    ppermute x9, waiting for transfers between devices, flip_x(): return lax.ppermute(v, 'dp', [(i, i ^ 1) for i in range(n_dp)])  39 us
    ppermute x13, starting transfers between devices, move_z(): lax.ppermute(v, 'dp', [(2 * a + i, 2 * b + i) for a, b in pairs for i in...  38.6 us
    ppermute x15, waiting for transfers between devices, flip_m(): return lax.ppermute(v, 'expert', [(i, i ^ k) for i in range(sources)])  28.7 us
    pallas_call x4, Pallas kernels, route(): call(f'route{k}', functools.partial(route_kernel, rows, places[k], count,...  20.6 us
    ppermute x9, starting transfers between devices, flip_x(): return lax.ppermute(v, 'dp', [(i, i ^ 1) for i in range(n_dp)])  9.71 us
    ppermute x15, starting transfers between devices, flip_m(): return lax.ppermute(v, 'expert', [(i, i ^ k) for i in range(sources)])  9.34 us
    pallas_call x1, Pallas kernels, shards(): call('down_grad', functools.partial(grad_kernel, [len(a) for a in acts]),...  8.45 us
  transfers between devices with their start and end apart: 37, of which 18 were waited for; matrix products, arithmetic and copies ran while one was open for 2% of the time, Pallas kernels for 15%

profile of v3, /device:TPU:0, one launch (start us, length us, event | category | flops | bytes accessed | tf_op | source)
XLA Modules:
  0.0 219.0 jit_solution(15592849993489243862)
XLA Ops:
  11.6 4.1 %collective-permute-start.4 = (bf16[144,1024]{1,0:T(8,128)(2,1)S(1)}, bf16[144,1024]{1,0:T(8,128)(2,1)S(1)}, u32[]{:S(2)}, u32[]{:S(2)}) collective-permute-start(bf16[144,1024]{1,0:T(8,128)(2,1)S(1)} %get-tuple-element.46), channel_id=1, source_target_pairs={{0,24},{4,28},{8,16},{12,20},{16,8},{20,12},{24,0},{28,4},{1,25},{... | collective-permute-start | bytes 884744 | tf_op jit(solution)/shard_map/rows3_z/ppermute | solution.py:239
  15.8 6.3 %collective-permute-done.1.got_ref = bf16[4,192,384]{2,1,0:T(8,128)(2,1)S(1)} collective-permute-done((bf16[4,192,384]{2,1,0:T(8,128)(2,1)}, bf16[4,192,384]{2,1,0:T(8,128)(2,1)S(1)}, u32[]{:S(2)}, u32[]{:S(2)}) %collective-permute-start.1) | collective-permute-done | bytes 589856 | tf_op jit(solution)/shard_map/act_x/ppermute | solution.py:246
  23.5 8.2 %collective-permute-start.2 = (bf16[4,384,384]{2,1,0:T(8,128)(2,1)S(1)}, bf16[4,384,384]{2,1,0:T(8,128)(2,1)S(1)}, u32[]{:S(2)}, u32[]{:S(2)}) collective-permute-start(bf16[4,384,384]{2,1,0:T(8,128)(2,1)S(1)} %pair.1.refs_4_), channel_id=1, source_target_pairs={{0,8},{4,12},{8,0},{12,4},{16,24},{20,28},{24,16},{28,20},{1,9},{5... | collective-permute-start | bytes 3538952 | tf_op jit(solution)/shard_map/act_z_r1/ppermute | solution.py:239
  34.8 3.7 %collective-permute-done = bf16[1,144,1024]{2,1,0:T(8,128)(2,1)S(1)} collective-permute-done((bf16[1,144,1024]{2,1,0:T(8,128)(2,1)S(1)}, bf16[1,144,1024]{2,1,0:T(8,128)(2,1)S(1)}, u32[]{:S(2)}, u32[]{:S(2)}) %collective-permute-start) | collective-permute-done | bytes 294944 | tf_op jit(solution)/shard_map/rows0_expert2/ppermute | solution.py:250
  38.5 5.9 %collective-permute-done.5 = bf16[1,144,1024]{2,1,0:T(8,128)(2,1)S(1)} collective-permute-done((bf16[1,144,1024]{2,1,0:T(8,128)(2,1)S(1)}, bf16[1,144,1024]{2,1,0:T(8,128)(2,1)S(1)}, u32[]{:S(2)}, u32[]{:S(2)}) %collective-permute-start.5) | collective-permute-done | bytes 294944 | tf_op jit(solution)/shard_map/rows3_x/ppermute | solution.py:246
  47.8 11.2 %collective-permute-done.9 = bf16[2,144,1024]{2,1,0:T(8,128)(2,1)S(1)} collective-permute-done((bf16[2,144,1024]{2,1,0:T(8,128)(2,1)S(1)}, bf16[2,144,1024]{2,1,0:T(8,128)(2,1)S(1)}, u32[]{:S(2)}, u32[]{:S(2)}) %collective-permute-start.9) | collective-permute-done | bytes 589856 | tf_op jit(solution)/shard_map/rows3_expert2/ppermute | solution.py:250
  64.5 5.1 %route3.1 = (bf16[2,4,192,384]{3,2,1,0:T(8,128)(2,1)S(1)}, bf16[4,384,1024]{2,1,0:T(8,128)(2,1)S(1)}) custom-call(s32[3]{0:T(128)S(1)} %pad_add_fusion.idx, bf16[4,144,1024]{2,1,0:T(8,128)(2,1)S(1)} %pad_maximum_fusion.a_ref, bf16[2,144,1024]{2,1,0:T(8,128)(2,1)S(1)} %collective-permute-done.11.b_ref, ...), custom_call_target="tpu_custom_call" | custom-call | tf_op jit(solution)/shard_map/route3/pallas_call | solution.py:298
  69.6 6.2 %collective-permute-done.6 = bf16[144,1024]{1,0:T(8,128)(2,1)S(1)} collective-permute-done((bf16[144,1024]{1,0:T(8,128)(2,1)S(1)}, bf16[144,1024]{1,0:T(8,128)(2,1)S(1)}, u32[]{:S(2)}, u32[]{:S(2)}) %collective-permute-start.6) | collective-permute-done | bytes 294944 | tf_op jit(solution)/shard_map/rows2_z/ppermute | solution.py:239
  79.3 8.3 %collective-permute-start.19 = (bf16[2,4,192,384]{3,2,1,0:T(8,128)(2,1)S(1)}, bf16[2,4,192,384]{3,2,1,0:T(8,128)(2,1)S(1)}, u32[]{:S(2)}, u32[]{:S(2)}) collective-permute-start(bf16[2,4,192,384]{3,2,1,0:T(8,128)(2,1)S(1)} %get-tuple-element.52), channel_id=1, source_target_pairs={{0,8},{4,12},{24,16},{28,20},{1,9},{5,13},{25,17},{29,21},{2,10},{... | collective-permute-start | bytes 3538952 | tf_op jit(solution)/shard_map/back_s1/ppermute | solution.py:239
  89.9 5.7 %collective-permute-done.14 = bf16[1,144,1024]{2,1,0:T(8,128)(2,1)S(1)} collective-permute-done((bf16[1,144,1024]{2,1,0:T(8,128)(2,1)S(1)}, bf16[1,144,1024]{2,1,0:T(8,128)(2,1)S(1)}, u32[]{:S(2)}, u32[]{:S(2)}) %collective-permute-start.14) | collective-permute-done | bytes 294944 | tf_op jit(solution)/shard_map/rows1_x/ppermute | solution.py:246
  96.3 6.0 %collective-permute-done.16 = bf16[2,144,1024]{2,1,0:T(8,128)(2,1)S(1)} collective-permute-done((bf16[2,144,1024]{2,1,0:T(8,128)(2,1)S(1)}, bf16[2,144,1024]{2,1,0:T(8,128)(2,1)S(1)}, u32[]{:S(2)}, u32[]{:S(2)}) %collective-permute-start.16) | collective-permute-done | bytes 589856 | tf_op jit(solution)/shard_map/rows2_expert2/ppermute | solution.py:250
  102.3 4.0 %collective-permute-done.20.refs_6_ = bf16[4,384,384]{2,1,0:T(8,128)(2,1)S(1)} collective-permute-done((bf16[4,384,384]{2,1,0:T(8,128)(2,1)S(1)}, bf16[4,384,384]{2,1,0:T(8,128)(2,1)S(1)}, u32[]{:S(2)}, u32[]{:S(2)}) %collective-permute-start.20) | collective-permute-done | bytes 1179680 | tf_op jit(solution)/shard_map/act_z_o2/ppermute | solution.py:239
  109.0 3.2 %collective-permute-done.19 = bf16[2,4,192,384]{3,2,1,0:T(8,128)(2,1)S(1)} collective-permute-done((bf16[2,4,192,384]{3,2,1,0:T(8,128)(2,1)S(1)}, bf16[2,4,192,384]{3,2,1,0:T(8,128)(2,1)S(1)}, u32[]{:S(2)}, u32[]{:S(2)}) %collective-permute-start.19) | collective-permute-done | bytes 1179680 | tf_op jit(solution)/shard_map/back_s1/ppermute | solution.py:239
  115.4 5.1 %route2.1 = (f32[2,4,192,384]{3,2,1,0:T(8,128)S(1)}, bf16[4,384,1024]{2,1,0:T(8,128)(2,1)S(1)}) custom-call(s32[3]{0:T(128)S(1)} %pad_add_fusion.idx, bf16[4,144,1024]{2,1,0:T(8,128)(2,1)S(1)} %pad_maximum_fusion.1.a_ref, bf16[2,144,1024]{2,1,0:T(8,128)(2,1)S(1)} %collective-permute-done.22.b_ref, bf16[2,144,1024]{2,1,0:T(8,128)(2,1)S(1)} %collective-permute-done.23.c_ref, ...), custom_call_target="tpu_custom_call" | custom-call | tf_op jit(solution)/shard_map/route2/pallas_call | solution.py:298
  120.6 7.4 %collective-permute-done.18 = bf16[2,144,1024]{2,1,0:T(8,128)(2,1)S(1)} collective-permute-done((bf16[2,144,1024]{2,1,0:T(8,128)(2,1)S(1)}, bf16[2,144,1024]{2,1,0:T(8,128)(2,1)S(1)}, u32[]{:S(2)}, u32[]{:S(2)}) %collective-permute-start.18) | collective-permute-done | bytes 589856 | tf_op jit(solution)/shard_map/rows1_expert2/ppermute | solution.py:250
  130.1 5.5 %collective-permute-start.30 = (bf16[2,4,192,384]{3,2,1,0:T(8,128)(2,1)S(1)}, bf16[2,4,192,384]{3,2,1,0:T(8,128)(2,1)S(1)}, u32[]{:S(2)}, u32[]{:S(2)}) collective-permute-start(bf16[2,4,192,384]{3,2,1,0:T(8,128)(2,1)S(1)} %add_convert_fusion.2), channel_id=1, source_target_pairs={{0,8},{4,12},{24,16},{28,20},{1,9},{5,13},{25,17},{29,21},{2,10},{... | collective-permute-start | bytes 3538952 | tf_op jit(solution)/shard_map/back_s2_in/ppermute | solution.py:239
  135.7 5.1 %route1.1 = (f32[2,4,192,384]{3,2,1,0:T(8,128)S(1)}, bf16[4,384,1024]{2,1,0:T(8,128)(2,1)S(1)}) custom-call(s32[3]{0:T(128)S(1)} %pad_add_fusion.idx, bf16[4,144,1024]{2,1,0:T(8,128)(2,1)S(1)} %pad_maximum_fusion.3.a_ref, bf16[2,144,1024]{2,1,0:T(8,128)(2,1)S(1)} %collective-permute-done.17.b_ref, bf16[2,144,1024]{2,1,0:T(8,128)(2,1)S(1)} %collective-permute-done.24.c_ref, ...), custom_call_target="tpu_custom_call" | custom-call | tf_op jit(solution)/shard_map/route1/pallas_call | solution.py:298
  141.0 3.2 %collective-permute-done.25.refs_8_ = bf16[4,384,384]{2,1,0:T(8,128)(2,1)S(1)} collective-permute-done((bf16[4,384,384]{2,1,0:T(8,128)(2,1)S(1)}, bf16[4,384,384]{2,1,0:T(8,128)(2,1)S(1)}, u32[]{:S(2)}, u32[]{:S(2)}) %collective-permute-start.25) | collective-permute-done | bytes 1179680 | tf_op jit(solution)/shard_map/act_z_o3/ppermute | solution.py:239
  144.2 5.1 %route0.1 = (f32[2,4,192,384]{3,2,1,0:T(8,128)S(1)}, bf16[4,384,1024]{2,1,0:T(8,128)(2,1)S(1)}) custom-call(s32[3]{0:T(128)S(1)} %pad_add_fusion.idx, bf16[4,144,1024]{2,1,0:T(8,128)(2,1)S(1)} %pad_maximum_fusion.2.a_ref, bf16[2,144,1024]{2,1,0:T(8,128)(2,1)S(1)} %collective-permute-done.26.b_ref, bf16[2,144,1024]{2,1,0:T(8,128)(2,1)S(1)} %collective-permute-done.27.c_ref, ...), custom_call_target="tpu_custom_call" | custom-call | tf_op jit(solution)/shard_map/route0/pallas_call | solution.py:298
  149.3 8.4 %down_grad.1 = (bf16[4,512,384]{2,1,0:T(8,128)(2,1)S(1)}, bf16[4,512,384]{2,1,0:T(8,128)(2,1)S(1)}) custom-call(s32[3]{0:T(128)S(1)} %pad_add_fusion.idx, bf16[4,384,1024]{2,1,0:T(8,128)(2,1)S(1)} %get-tuple-element.66.refs_0_, bf16[4,384,1024]{2,1,0:T(8,128)(2,1)S(1)} %get-tuple-element.67.refs_1_, bf16[4,384,1024]{2,1,0:T(8,128)(2,1)S(1)} %get-tuple-element.68.refs_2_, ...), custom_call_target="tpu_custom_call" | custom-call | flops 4831838208 | bytes 19660800 | tf_op jit(solution)/shard_map/down_grad/pallas_call | solution.py:430
  164.9 24.6 %collective-permute-done.29.refs_1_ = bf16[2,4,192,384]{3,2,1,0:T(8,128)(2,1)S(1)} collective-permute-done((bf16[2,4,192,384]{3,2,1,0:T(8,128)(2,1)S(1)}, bf16[2,4,192,384]{3,2,1,0:T(8,128)(2,1)S(1)}, u32[]{:S(2)}, u32[]{:S(2)}) %collective-permute-start.29) | collective-permute-done | bytes 1179680 | tf_op jit(solution)/shard_map/back0_s3_flip/ppermute | solution.py:239
  189.7 4.0 %collective-permute-done.32.got_ref = bf16[4,512,384]{2,1,0:T(8,128)(2,1)S(1)} collective-permute-done((bf16[4,512,384]{2,1,0:T(8,128)(2,1)S(1)}, bf16[4,512,384]{2,1,0:T(8,128)(2,1)S(1)}, u32[]{:S(2)}, u32[]{:S(2)}) %collective-permute-start.32) | collective-permute-done | bytes 1572896 | tf_op jit(solution)/shard_map/grad_x/ppermute | solution.py:246
  194.3 13.4 %collective-permute-done.33.refs_3_ = bf16[4,192,384]{2,1,0:T(8,128)(2,1)S(1)} collective-permute-done((bf16[4,192,384]{2,1,0:T(8,128)(2,1)S(1)}, bf16[4,192,384]{2,1,0:T(8,128)(2,1)S(1)}, u32[]{:S(2)}, u32[]{:S(2)}) %collective-permute-start.33) | collective-permute-done | bytes 589856 | tf_op jit(solution)/shard_map/back0_x/ppermute | solution.py:246
  207.7 4.0 %owner0.1 = (bf16[1,4,4,48,1536]{4,3,2,1,0:T(8,128)(2,1)}, f32[4,4,128]{2,1,0:T(4,128)S(1)}) custom-call(s32[3]{0:T(128)S(1)} %pad_add_fusion.idx, bf16[1,4,4,48,1536]{4,3,2,1,0:T(8,128)(2,1)S(1)} %copy-done.2, bf16[4,16,256]{2,1,0:T(8,128)(2,1)S(1)} %pad_maximum_fusion.6.meta_ref, f32[2,4,192,384]{3,2,1,0:T(8,128)S(1)} %get-tuple-element.64.refs_0_, ...), custom_call_target="tpu_custom_call" | custom-call | tf_op jit(solution)/shard_map/owner0/pallas_call | solution.py:484
  (98 shorter events, 54.0 us)
Async XLA Ops:
  4.8 17.3 %collective-permute-start.1 = (bf16[4,192,384]{2,1,0:T(8,128)(2,1)}, bf16[4,192,384]{2,1,0:T(8,128)(2,1)S(1)}, u32[]{:S(2)}, u32[]{:S(2)}) collective-permute-start(bf16[4,192,384]{2,1,0:T(8,128)(2,1)} %get-tuple-element.43), channel_id=1, source_target_pairs={{0,4},{4,0},{8,12},{12,8},{16,20},{20,16},{24,28},{28,24},{1,5},{5... | collective-permute-start | bytes 1769480 | tf_op jit(solution)/shard_map/act_x/ppermute | solution.py:246
  10.5 33.9 %collective-permute-start.7 = (bf16[2,512,384]{2,1,0:T(8,128)(2,1)}, bf16[2,512,384]{2,1,0:T(8,128)(2,1)S(1)}, u32[]{:S(2)}, u32[]{:S(2)}) collective-permute-start(bf16[2,512,384]{2,1,0:T(8,128)(2,1)} %get-tuple-element.80), channel_id=1, source_target_pairs={{0,4},{4,0},{8,12},{12,8},{16,20},{20,16},{24,28},{28,24},{1,5},{5... | collective-permute-start | bytes 2359304 | tf_op jit(solution)/shard_map/weight0_x/ppermute | solution.py:246
  22.8 36.3 %collective-permute-start.10 = (bf16[4,384,384]{2,1,0:T(8,128)(2,1)S(1)}, bf16[4,384,384]{2,1,0:T(8,128)(2,1)S(1)}, u32[]{:S(2)}, u32[]{:S(2)}) collective-permute-start(bf16[4,384,384]{2,1,0:T(8,128)(2,1)S(1)} %pair.1.refs_4_), channel_id=1, source_target_pairs={{8,16},{12,20},{16,8},{20,12},{9,17},{13,21},{17,9},{21,13},{10,18... | collective-permute-start | bytes 3538952 | tf_op jit(solution)/shard_map/act_z_i3/ppermute | solution.py:239
  23.5 35.5 %collective-permute-start.2 = (bf16[4,384,384]{2,1,0:T(8,128)(2,1)S(1)}, bf16[4,384,384]{2,1,0:T(8,128)(2,1)S(1)}, u32[]{:S(2)}, u32[]{:S(2)}) collective-permute-start(bf16[4,384,384]{2,1,0:T(8,128)(2,1)S(1)} %pair.1.refs_4_), channel_id=1, source_target_pairs={{0,8},{4,12},{8,0},{12,4},{16,24},{20,28},{24,16},{28,20},{1,9},{5... | collective-permute-start | bytes 3538952 | tf_op jit(solution)/shard_map/act_z_r1/ppermute | solution.py:239
  44.5 14.6 %collective-permute-start.9 = (bf16[2,144,1024]{2,1,0:T(8,128)(2,1)S(1)}, bf16[2,144,1024]{2,1,0:T(8,128)(2,1)S(1)}, u32[]{:S(2)}, u32[]{:S(2)}) collective-permute-start(bf16[2,144,1024]{2,1,0:T(8,128)(2,1)S(1)} %pad_maximum_fusion.4), channel_id=1, source_target_pairs={{0,2},{1,3},{2,0},{3,1},{4,6},{5,7},{6,4},{7,5},{8,10},{9,11},{10,... | collective-permute-start | bytes 1769480 | tf_op jit(solution)/shard_map/rows3_expert2/ppermute | solution.py:250
  46.3 18.1 %collective-permute-start.8 = (bf16[2,512,384]{2,1,0:T(8,128)(2,1)S(1)}, bf16[2,512,384]{2,1,0:T(8,128)(2,1)S(1)}, u32[]{:S(2)}, u32[]{:S(2)}) collective-permute-start(bf16[2,512,384]{2,1,0:T(8,128)(2,1)S(1)} %copy-done.4), channel_id=1, source_target_pairs={{0,4},{4,0},{8,12},{12,8},{16,20},{20,16},{24,28},{28,24},{1,5},{5... | collective-permute-start | bytes 2359304 | tf_op jit(solution)/shard_map/weight1_x/ppermute | solution.py:246
  47.8 15.6 %collective-permute-start.11 = (bf16[2,144,1024]{2,1,0:T(8,128)(2,1)S(1)}, bf16[2,144,1024]{2,1,0:T(8,128)(2,1)S(1)}, u32[]{:S(2)}, u32[]{:S(2)}) collective-permute-start(bf16[2,144,1024]{2,1,0:T(8,128)(2,1)S(1)} %pad_maximum_fusion.4), channel_id=1, source_target_pairs={{0,1},{1,0},{2,3},{3,2},{4,5},{5,4},{6,7},{7,6},{8,9},{9,8},{10,11... | collective-permute-start | bytes 1769480 | tf_op jit(solution)/shard_map/rows3_expert1/ppermute | solution.py:250
  59.1 16.7 %collective-permute-start.6 = (bf16[144,1024]{1,0:T(8,128)(2,1)S(1)}, bf16[144,1024]{1,0:T(8,128)(2,1)S(1)}, u32[]{:S(2)}, u32[]{:S(2)}) collective-permute-start(bf16[144,1024]{1,0:T(8,128)(2,1)S(1)} %get-tuple-element.47), channel_id=1, source_target_pairs={{0,16},{4,20},{8,24},{12,28},{16,0},{20,4},{24,8},{28,12},{1,17},{... | collective-permute-start | bytes 884744 | tf_op jit(solution)/shard_map/rows2_z/ppermute | solution.py:239
  61.7 26.0 %collective-permute-start.3 = (bf16[144,1024]{1,0:T(8,128)(2,1)S(1)}, bf16[144,1024]{1,0:T(8,128)(2,1)S(1)}, u32[]{:S(2)}, u32[]{:S(2)}) collective-permute-start(bf16[144,1024]{1,0:T(8,128)(2,1)S(1)} %get-tuple-element.44), channel_id=1, source_target_pairs={{0,8},{4,12},{8,0},{12,4},{16,24},{20,28},{24,16},{28,20},{1,9},{5... | collective-permute-start | bytes 884744 | tf_op jit(solution)/shard_map/rows1_z/ppermute | solution.py:239
  77.2 29.1 %collective-permute-start.20 = (bf16[4,384,384]{2,1,0:T(8,128)(2,1)S(1)}, bf16[4,384,384]{2,1,0:T(8,128)(2,1)S(1)}, u32[]{:S(2)}, u32[]{:S(2)}) collective-permute-start(bf16[4,384,384]{2,1,0:T(8,128)(2,1)S(1)} %collective-permute-done.10.refs_9_), channel_id=1, source_target_pairs={{8,0},{12,4},{16,24},{20,28},{9,1},{13,5},{17,25},{21,29},{10,2},{... | collective-permute-start | bytes 3538952 | tf_op jit(solution)/shard_map/act_z_o2/ppermute | solution.py:239
  78.5 27.8 %collective-permute-start.21 = (bf16[4,384,384]{2,1,0:T(8,128)(2,1)S(1)}, bf16[4,384,384]{2,1,0:T(8,128)(2,1)S(1)}, u32[]{:S(2)}, u32[]{:S(2)}) collective-permute-start(bf16[4,384,384]{2,1,0:T(8,128)(2,1)S(1)} %collective-permute-done.2.refs_5_), channel_id=1, source_target_pairs={{8,16},{12,20},{16,8},{20,12},{9,17},{13,21},{17,9},{21,13},{10,18... | collective-permute-start | bytes 3538952 | tf_op jit(solution)/shard_map/act_z_i2/ppermute | solution.py:239
  79.3 32.9 %collective-permute-start.19 = (bf16[2,4,192,384]{3,2,1,0:T(8,128)(2,1)S(1)}, bf16[2,4,192,384]{3,2,1,0:T(8,128)(2,1)S(1)}, u32[]{:S(2)}, u32[]{:S(2)}) collective-permute-start(bf16[2,4,192,384]{3,2,1,0:T(8,128)(2,1)S(1)} %get-tuple-element.52), channel_id=1, source_target_pairs={{0,8},{4,12},{24,16},{28,20},{1,9},{5,13},{25,17},{29,21},{2,10},{... | collective-permute-start | bytes 3538952 | tf_op jit(solution)/shard_map/back_s1/ppermute | solution.py:239
  88.3 14.0 %collective-permute-start.16 = (bf16[2,144,1024]{2,1,0:T(8,128)(2,1)S(1)}, bf16[2,144,1024]{2,1,0:T(8,128)(2,1)S(1)}, u32[]{:S(2)}, u32[]{:S(2)}) collective-permute-start(bf16[2,144,1024]{2,1,0:T(8,128)(2,1)S(1)} %constant_dynamic-update-slice_fusion), channel_id=1, source_target_pairs={{0,2},{1,3},{2,0},{3,1},{4,6},{5,7},{6,4},{7,5},{8,10},{9,11},{10,... | collective-permute-start | bytes 1769480 | tf_op jit(solution)/shard_map/rows2_expert2/ppermute | solution.py:250
  112.2 15.8 %collective-permute-start.18 = (bf16[2,144,1024]{2,1,0:T(8,128)(2,1)S(1)}, bf16[2,144,1024]{2,1,0:T(8,128)(2,1)S(1)}, u32[]{:S(2)}, u32[]{:S(2)}) collective-permute-start(bf16[2,144,1024]{2,1,0:T(8,128)(2,1)S(1)} %constant_dynamic-update-slice_fusion.2), channel_id=1, source_target_pairs={{0,2},{1,3},{2,0},{3,1},{4,6},{5,7},{6,4},{7,5},{8,10},{9,11},{10,... | collective-permute-start | bytes 1769480 | tf_op jit(solution)/shard_map/rows1_expert2/ppermute | solution.py:250
  113.8 15.9 %collective-permute-start.17 = (bf16[2,144,1024]{2,1,0:T(8,128)(2,1)S(1)}, bf16[2,144,1024]{2,1,0:T(8,128)(2,1)S(1)}, u32[]{:S(2)}, u32[]{:S(2)}) collective-permute-start(bf16[2,144,1024]{2,1,0:T(8,128)(2,1)S(1)} %constant_dynamic-update-slice_fusion.2), channel_id=1, source_target_pairs={{0,1},{1,0},{2,3},{3,2},{4,5},{5,4},{6,7},{7,6},{8,9},{9,8},{10,11... | collective-permute-start | bytes 1769480 | tf_op jit(solution)/shard_map/rows1_expert1/ppermute | solution.py:250
  114.0 30.2 %collective-permute-start.25 = (bf16[4,384,384]{2,1,0:T(8,128)(2,1)S(1)}, bf16[4,384,384]{2,1,0:T(8,128)(2,1)S(1)}, u32[]{:S(2)}, u32[]{:S(2)}) collective-permute-start(bf16[4,384,384]{2,1,0:T(8,128)(2,1)S(1)} %collective-permute-done.21.refs_7_), channel_id=1, source_target_pairs={{8,0},{12,4},{16,24},{20,28},{9,1},{13,5},{17,25},{21,29},{10,2},{... | collective-permute-start | bytes 3538952 | tf_op jit(solution)/shard_map/act_z_o3/ppermute | solution.py:239
  128.3 30.0 %collective-permute-start.28 = (bf16[2,4,192,384]{3,2,1,0:T(8,128)(2,1)S(1)}, bf16[2,4,192,384]{3,2,1,0:T(8,128)(2,1)S(1)}, u32[]{:S(2)}, u32[]{:S(2)}) collective-permute-start(bf16[2,4,192,384]{3,2,1,0:T(8,128)(2,1)S(1)} %add_convert_fusion.2), channel_id=1, source_target_pairs={{8,16},{12,20},{16,8},{20,12},{9,17},{13,21},{17,9},{21,13},{10,18... | collective-permute-start | bytes 3538952 | tf_op jit(solution)/shard_map/back_s2_mid/ppermute | solution.py:239
  129.1 15.1 %collective-permute-start.26 = (bf16[2,144,1024]{2,1,0:T(8,128)(2,1)S(1)}, bf16[2,144,1024]{2,1,0:T(8,128)(2,1)S(1)}, u32[]{:S(2)}, u32[]{:S(2)}) collective-permute-start(bf16[2,144,1024]{2,1,0:T(8,128)(2,1)S(1)} %pad_maximum_fusion.5), channel_id=1, source_target_pairs={{0,1},{1,0},{2,3},{3,2},{4,5},{5,4},{6,7},{7,6},{8,9},{9,8},{10,11... | collective-permute-start | bytes 1769480 | tf_op jit(solution)/shard_map/rows0_expert1/ppermute | solution.py:250
  130.0 14.2 %collective-permute-start.27 = (bf16[2,144,1024]{2,1,0:T(8,128)(2,1)S(1)}, bf16[2,144,1024]{2,1,0:T(8,128)(2,1)S(1)}, u32[]{:S(2)}, u32[]{:S(2)}) collective-permute-start(bf16[2,144,1024]{2,1,0:T(8,128)(2,1)S(1)} %collective-permute-done.15), channel_id=1, source_target_pairs={{0,1},{1,0},{2,3},{3,2},{4,5},{5,4},{6,7},{7,6},{8,9},{9,8},{10,11... | collective-permute-start | bytes 1769480 | tf_op jit(solution)/shard_map/rows0_expert1/ppermute | solution.py:250
  130.1 31.0 %collective-permute-start.30 = (bf16[2,4,192,384]{3,2,1,0:T(8,128)(2,1)S(1)}, bf16[2,4,192,384]{3,2,1,0:T(8,128)(2,1)S(1)}, u32[]{:S(2)}, u32[]{:S(2)}) collective-permute-start(bf16[2,4,192,384]{3,2,1,0:T(8,128)(2,1)S(1)} %add_convert_fusion.2), channel_id=1, source_target_pairs={{0,8},{4,12},{24,16},{28,20},{1,9},{5,13},{25,17},{29,21},{2,10},{... | collective-permute-start | bytes 3538952 | tf_op jit(solution)/shard_map/back_s2_in/ppermute | solution.py:239
  157.8 36.0 %collective-permute-start.32 = (bf16[4,512,384]{2,1,0:T(8,128)(2,1)S(1)}, bf16[4,512,384]{2,1,0:T(8,128)(2,1)S(1)}, u32[]{:S(2)}, u32[]{:S(2)}) collective-permute-start(bf16[4,512,384]{2,1,0:T(8,128)(2,1)S(1)} %get-tuple-element.70), channel_id=1, source_target_pairs={{0,4},{4,0},{8,12},{12,8},{16,20},{20,16},{24,28},{28,24},{1,5},{5... | collective-permute-start | bytes 4718600 | tf_op jit(solution)/shard_map/grad_x/ppermute | solution.py:246
  161.4 28.1 %collective-permute-start.29 = (bf16[2,4,192,384]{3,2,1,0:T(8,128)(2,1)S(1)}, bf16[2,4,192,384]{3,2,1,0:T(8,128)(2,1)S(1)}, u32[]{:S(2)}, u32[]{:S(2)}) collective-permute-start(bf16[2,4,192,384]{3,2,1,0:T(8,128)(2,1)S(1)} %add_convert_fusion.1), channel_id=1, source_target_pairs={{0,8},{4,12},{8,0},{12,4},{16,24},{20,28},{24,16},{28,20},{1,9},{5... | collective-permute-start | bytes 3538952 | tf_op jit(solution)/shard_map/back0_s3_flip/ppermute | solution.py:239
  164.0 25.5 %collective-permute-start.31 = (bf16[2,4,192,384]{3,2,1,0:T(8,128)(2,1)S(1)}, bf16[2,4,192,384]{3,2,1,0:T(8,128)(2,1)S(1)}, u32[]{:S(2)}, u32[]{:S(2)}) collective-permute-start(bf16[2,4,192,384]{3,2,1,0:T(8,128)(2,1)S(1)} %add_convert_fusion), channel_id=1, source_target_pairs={{8,16},{12,20},{16,8},{20,12},{9,17},{13,21},{17,9},{21,13},{10,18... | collective-permute-start | bytes 3538952 | tf_op jit(solution)/shard_map/back0_s3_mid/ppermute | solution.py:239
  193.7 13.9 %collective-permute-start.33 = (bf16[4,192,384]{2,1,0:T(8,128)(2,1)S(1)}, bf16[4,192,384]{2,1,0:T(8,128)(2,1)S(1)}, u32[]{:S(2)}, u32[]{:S(2)}) collective-permute-start(bf16[4,192,384]{2,1,0:T(8,128)(2,1)S(1)} %fusion), channel_id=1, source_target_pairs={{0,4},{4,0},{8,12},{12,8},{16,20},{20,16},{24,28},{28,24},{1,5},{5... | collective-permute-start | bytes 1769480 | tf_op jit(solution)/shard_map/back0_x/ppermute | solution.py:246
  (20 other events, 171.9 us)

commit v4 on v3

--- a/solution.py
+++ b/solution.py
@@ -399,7 +399,7 @@
         stage(0, 1)
         come1_x, come0_x = far[1][0], far[0][0]
         stage(2, 1)
-        ties["c", 2] = [come1_x, come0_x, *s1, o2, i2]
+        ties["c", 2] = [come1_x, come0_x, *s1]
         rest(2, 2)
         parts[2, 0] = route(2)
         v2 = [plus(parts[2, 0], s1[0])]
@@ -407,7 +407,7 @@
         s2_mid = [move_z(v2[0], inner, "back_s2_mid")]
         stage(1, 1)
         o3 = move_z(after(i2, *s1), outward, "act_z_o3")
-        ties["c", 1] = [parts[2, 0]]
+        ties["c", 1] = [parts[2, 0], o2, i2]
         rest(1, 2)
         acts = [[own_act], [r1], [o2, i2], [o3, i3]]
         parts[1, 0] = route(1)

time: 219 us -> 218 us (level)
  starting transfers between devices: 57.6 us -> 52.5 us
  waiting for transfers between devices: 111 us -> 115 us
    ppermute x15, waiting for transfers between devices: 28.7 us -> 20.8 us  [flip_m(): return lax.ppermute(v, 'expert', [(i, i ^ k) for i in range(sources)])]
    ppermute x13, starting transfers between devices: 38.6 us -> 31.7 us  [move_z(): lax.ppermute(v, 'dp', [(2 * a + i, 2 * b + i) for a, b in pairs for i in...]
    ppermute x9, waiting for transfers between devices: 39 us -> 45.6 us  [flip_x(): return lax.ppermute(v, 'dp', [(i, i ^ 1) for i in range(n_dp)])]
    ppermute x13, waiting for transfers between devices: 43.7 us -> 48.7 us  [move_z(): lax.ppermute(v, 'dp', [(2 * a + i, 2 * b + i) for a, b in pairs for i in...]
  transfers between devices with their start and end apart: 37 -> 37, of which waited for: 18 -> 16; matrix products, arithmetic and copies ran while one was open for 2% -> 2% of each run, Pallas kernels for 15% -> 15%
where the time goes in v4:
time: 218 us
  waiting for transfers between devices  115 us (53%)
  starting transfers between devices  52.5 us (24%)
  Pallas kernels  41.8 us (19%)
  local copies, waits for them, and re-layouts  5.44 us (2%)
    ppermute x13, waiting for transfers between devices, move_z(): lax.ppermute(v, 'dp', [(2 * a + i, 2 * b + i) for a, b in pairs for i in...  48.7 us
    ppermute x9, waiting for transfers between devices, flip_x(): return lax.ppermute(v, 'dp', [(i, i ^ 1) for i in range(n_dp)])  45.6 us
    ppermute x13, starting transfers between devices, move_z(): lax.ppermute(v, 'dp', [(2 * a + i, 2 * b + i) for a, b in pairs for i in...  31.7 us
    ppermute x15, waiting for transfers between devices, flip_m(): return lax.ppermute(v, 'expert', [(i, i ^ k) for i in range(sources)])  20.8 us
    pallas_call x4, Pallas kernels, route(): call(f'route{k}', functools.partial(route_kernel, rows, places[k], count,...  20.6 us
    ppermute x9, starting transfers between devices, flip_x(): return lax.ppermute(v, 'dp', [(i, i ^ 1) for i in range(n_dp)])  11.5 us
    ppermute x15, starting transfers between devices, flip_m(): return lax.ppermute(v, 'expert', [(i, i ^ k) for i in range(sources)])  9.27 us
    pallas_call x1, Pallas kernels, shards(): call('down_grad', functools.partial(grad_kernel, [len(a) for a in acts]),...  8.45 us
  transfers between devices with their start and end apart: 37, of which 16 were waited for; matrix products, arithmetic and copies ran while one was open for 2% of the time, Pallas kernels for 15%

profile of v4, /device:TPU:0, one launch (start us, length us, event | category | flops | bytes accessed | tf_op | source)
XLA Modules:
  0.0 217.7 jit_solution(9002406525482716328)
XLA Ops:
  4.8 2.9 %collective-permute-start.1 = (bf16[4,192,384]{2,1,0:T(8,128)(2,1)}, bf16[4,192,384]{2,1,0:T(8,128)(2,1)S(1)}, u32[]{:S(2)}, u32[]{:S(2)}) collective-permute-start(bf16[4,192,384]{2,1,0:T(8,128)(2,1)} %get-tuple-element.43), channel_id=1, source_target_pairs={{0,4},{4,0},{8,12},{12,8},{16,20},{20,16},{24,28},{28,24},{1,5},{5... | collective-permute-start | bytes 1769480 | tf_op jit(solution)/shard_map/act_x/ppermute | solution.py:246
  11.6 4.1 %collective-permute-start.4 = (bf16[144,1024]{1,0:T(8,128)(2,1)S(1)}, bf16[144,1024]{1,0:T(8,128)(2,1)S(1)}, u32[]{:S(2)}, u32[]{:S(2)}) collective-permute-start(bf16[144,1024]{1,0:T(8,128)(2,1)S(1)} %get-tuple-element.46), channel_id=1, source_target_pairs={{0,24},{4,28},{8,16},{12,20},{16,8},{20,12},{24,0},{28,4},{1,25},{... | collective-permute-start | bytes 884744 | tf_op jit(solution)/shard_map/rows3_z/ppermute | solution.py:239
  15.8 6.3 %collective-permute-done.1.got_ref = bf16[4,192,384]{2,1,0:T(8,128)(2,1)S(1)} collective-permute-done((bf16[4,192,384]{2,1,0:T(8,128)(2,1)}, bf16[4,192,384]{2,1,0:T(8,128)(2,1)S(1)}, u32[]{:S(2)}, u32[]{:S(2)}) %collective-permute-start.1) | collective-permute-done | bytes 589856 | tf_op jit(solution)/shard_map/act_x/ppermute | solution.py:246
  23.5 8.2 %collective-permute-start.2 = (bf16[4,384,384]{2,1,0:T(8,128)(2,1)S(1)}, bf16[4,384,384]{2,1,0:T(8,128)(2,1)S(1)}, u32[]{:S(2)}, u32[]{:S(2)}) collective-permute-start(bf16[4,384,384]{2,1,0:T(8,128)(2,1)S(1)} %pair.1.refs_4_), channel_id=1, source_target_pairs={{0,8},{4,12},{8,0},{12,4},{16,24},{20,28},{24,16},{28,20},{1,9},{5... | collective-permute-start | bytes 3538952 | tf_op jit(solution)/shard_map/act_z_r1/ppermute | solution.py:239
  34.8 3.7 %collective-permute-done = bf16[1,144,1024]{2,1,0:T(8,128)(2,1)S(1)} collective-permute-done((bf16[1,144,1024]{2,1,0:T(8,128)(2,1)S(1)}, bf16[1,144,1024]{2,1,0:T(8,128)(2,1)S(1)}, u32[]{:S(2)}, u32[]{:S(2)}) %collective-permute-start) | collective-permute-done | bytes 294944 | tf_op jit(solution)/shard_map/rows0_expert2/ppermute | solution.py:250
  38.5 5.9 %collective-permute-done.5 = bf16[1,144,1024]{2,1,0:T(8,128)(2,1)S(1)} collective-permute-done((bf16[1,144,1024]{2,1,0:T(8,128)(2,1)S(1)}, bf16[1,144,1024]{2,1,0:T(8,128)(2,1)S(1)}, u32[]{:S(2)}, u32[]{:S(2)}) %collective-permute-start.5) | collective-permute-done | bytes 294944 | tf_op jit(solution)/shard_map/rows3_x/ppermute | solution.py:246
  47.8 11.2 %collective-permute-done.9 = bf16[2,144,1024]{2,1,0:T(8,128)(2,1)S(1)} collective-permute-done((bf16[2,144,1024]{2,1,0:T(8,128)(2,1)S(1)}, bf16[2,144,1024]{2,1,0:T(8,128)(2,1)S(1)}, u32[]{:S(2)}, u32[]{:S(2)}) %collective-permute-start.9) | collective-permute-done | bytes 589856 | tf_op jit(solution)/shard_map/rows3_expert2/ppermute | solution.py:250
  64.5 5.1 %route3.1 = (bf16[2,4,192,384]{3,2,1,0:T(8,128)(2,1)S(1)}, bf16[4,384,1024]{2,1,0:T(8,128)(2,1)S(1)}) custom-call(s32[3]{0:T(128)S(1)} %pad_add_fusion.idx, bf16[4,144,1024]{2,1,0:T(8,128)(2,1)S(1)} %pad_maximum_fusion.a_ref, bf16[2,144,1024]{2,1,0:T(8,128)(2,1)S(1)} %collective-permute-done.11.b_ref, ...), custom_call_target="tpu_custom_call" | custom-call | tf_op jit(solution)/shard_map/route3/pallas_call | solution.py:298
  69.6 6.2 %collective-permute-done.6 = bf16[144,1024]{1,0:T(8,128)(2,1)S(1)} collective-permute-done((bf16[144,1024]{1,0:T(8,128)(2,1)S(1)}, bf16[144,1024]{1,0:T(8,128)(2,1)S(1)}, u32[]{:S(2)}, u32[]{:S(2)}) %collective-permute-start.6) | collective-permute-done | bytes 294944 | tf_op jit(solution)/shard_map/rows2_z/ppermute | solution.py:239
  79.8 4.5 %collective-permute-done.13 = bf16[1,144,1024]{2,1,0:T(8,128)(2,1)S(1)} collective-permute-done((bf16[1,144,1024]{2,1,0:T(8,128)(2,1)S(1)}, bf16[1,144,1024]{2,1,0:T(8,128)(2,1)S(1)}, u32[]{:S(2)}, u32[]{:S(2)}) %collective-permute-start.13) | collective-permute-done | bytes 294944 | tf_op jit(solution)/shard_map/rows2_x/ppermute | solution.py:246
  88.1 3.8 %collective-permute-done.14 = bf16[1,144,1024]{2,1,0:T(8,128)(2,1)S(1)} collective-permute-done((bf16[1,144,1024]{2,1,0:T(8,128)(2,1)S(1)}, bf16[1,144,1024]{2,1,0:T(8,128)(2,1)S(1)}, u32[]{:S(2)}, u32[]{:S(2)}) %collective-permute-start.14) | collective-permute-done | bytes 294944 | tf_op jit(solution)/shard_map/rows1_x/ppermute | solution.py:246
  94.8 5.5 %collective-permute-done.16 = bf16[2,144,1024]{2,1,0:T(8,128)(2,1)S(1)} collective-permute-done((bf16[2,144,1024]{2,1,0:T(8,128)(2,1)S(1)}, bf16[2,144,1024]{2,1,0:T(8,128)(2,1)S(1)}, u32[]{:S(2)}, u32[]{:S(2)}) %collective-permute-start.16) | collective-permute-done | bytes 589856 | tf_op jit(solution)/shard_map/rows2_expert2/ppermute | solution.py:250
  100.2 4.8 %collective-permute-done.15 = bf16[2,144,1024]{2,1,0:T(8,128)(2,1)S(1)} collective-permute-done((bf16[2,144,1024]{2,1,0:T(8,128)(2,1)S(1)}, bf16[2,144,1024]{2,1,0:T(8,128)(2,1)S(1)}, u32[]{:S(2)}, u32[]{:S(2)}) %collective-permute-start.15) | collective-permute-done | bytes 589856 | tf_op jit(solution)/shard_map/rows0_x/ppermute | solution.py:246
  108.3 5.1 %route2.1 = (f32[2,4,192,384]{3,2,1,0:T(8,128)S(1)}, bf16[4,384,1024]{2,1,0:T(8,128)(2,1)S(1)}) custom-call(s32[3]{0:T(128)S(1)} %pad_add_fusion.idx, bf16[4,144,1024]{2,1,0:T(8,128)(2,1)S(1)} %pad_maximum_fusion.1.a_ref, bf16[2,144,1024]{2,1,0:T(8,128)(2,1)S(1)} %collective-permute-done.20.b_ref, bf16[2,144,1024]{2,1,0:T(8,128)(2,1)S(1)} %collective-permute-done.21.c_ref, ...), custom_call_target="tpu_custom_call" | custom-call | tf_op jit(solution)/shard_map/route2/pallas_call | solution.py:298
  113.4 9.7 %collective-permute-done.22.refs_6_ = bf16[4,384,384]{2,1,0:T(8,128)(2,1)S(1)} collective-permute-done((bf16[4,384,384]{2,1,0:T(8,128)(2,1)S(1)}, bf16[4,384,384]{2,1,0:T(8,128)(2,1)S(1)}, u32[]{:S(2)}, u32[]{:S(2)}) %collective-permute-start.22) | collective-permute-done | bytes 1179680 | tf_op jit(solution)/shard_map/act_z_o2/ppermute | solution.py:239
  125.2 6.9 %collective-permute-start.30 = (bf16[2,4,192,384]{3,2,1,0:T(8,128)(2,1)S(1)}, bf16[2,4,192,384]{3,2,1,0:T(8,128)(2,1)S(1)}, u32[]{:S(2)}, u32[]{:S(2)}) collective-permute-start(bf16[2,4,192,384]{3,2,1,0:T(8,128)(2,1)S(1)} %add_convert_fusion.2), channel_id=1, source_target_pairs={{0,8},{4,12},{24,16},{28,20},{1,9},{5,13},{25,17},{29,21},{2,10},{... | collective-permute-start | bytes 3538952 | tf_op jit(solution)/shard_map/back_s2_in/ppermute | solution.py:239
  132.3 5.1 %route1.1 = (f32[2,4,192,384]{3,2,1,0:T(8,128)S(1)}, bf16[4,384,1024]{2,1,0:T(8,128)(2,1)S(1)}) custom-call(s32[3]{0:T(128)S(1)} %pad_add_fusion.idx, bf16[4,144,1024]{2,1,0:T(8,128)(2,1)S(1)} %pad_maximum_fusion.3.a_ref, bf16[2,144,1024]{2,1,0:T(8,128)(2,1)S(1)} %collective-permute-done.17.b_ref, bf16[2,144,1024]{2,1,0:T(8,128)(2,1)S(1)} %collective-permute-done.24.c_ref, ...), custom_call_target="tpu_custom_call" | custom-call | tf_op jit(solution)/shard_map/route1/pallas_call | solution.py:298
  137.5 8.4 %collective-permute-done.25.refs_8_ = bf16[4,384,384]{2,1,0:T(8,128)(2,1)S(1)} collective-permute-done((bf16[4,384,384]{2,1,0:T(8,128)(2,1)S(1)}, bf16[4,384,384]{2,1,0:T(8,128)(2,1)S(1)}, u32[]{:S(2)}, u32[]{:S(2)}) %collective-permute-start.25) | collective-permute-done | bytes 1179680 | tf_op jit(solution)/shard_map/act_z_o3/ppermute | solution.py:239
  146.0 5.1 %route0.1 = (f32[2,4,192,384]{3,2,1,0:T(8,128)S(1)}, bf16[4,384,1024]{2,1,0:T(8,128)(2,1)S(1)}) custom-call(s32[3]{0:T(128)S(1)} %pad_add_fusion.idx, bf16[4,144,1024]{2,1,0:T(8,128)(2,1)S(1)} %pad_maximum_fusion.2.a_ref, bf16[2,144,1024]{2,1,0:T(8,128)(2,1)S(1)} %collective-permute-done.26.b_ref, bf16[2,144,1024]{2,1,0:T(8,128)(2,1)S(1)} %collective-permute-done.27.c_ref, ...), custom_call_target="tpu_custom_call" | custom-call | tf_op jit(solution)/shard_map/route0/pallas_call | solution.py:298
  151.1 8.4 %down_grad.1 = (bf16[4,512,384]{2,1,0:T(8,128)(2,1)S(1)}, bf16[4,512,384]{2,1,0:T(8,128)(2,1)S(1)}) custom-call(s32[3]{0:T(128)S(1)} %pad_add_fusion.idx, bf16[4,384,1024]{2,1,0:T(8,128)(2,1)S(1)} %get-tuple-element.66.refs_0_, bf16[4,384,1024]{2,1,0:T(8,128)(2,1)S(1)} %get-tuple-element.67.refs_1_, bf16[4,384,1024]{2,1,0:T(8,128)(2,1)S(1)} %get-tuple-element.68.refs_2_, ...), custom_call_target="tpu_custom_call" | custom-call | flops 4831838208 | bytes 19660800 | tf_op jit(solution)/shard_map/down_grad/pallas_call | solution.py:430
  161.9 24.3 %collective-permute-done.29.refs_1_ = bf16[2,4,192,384]{3,2,1,0:T(8,128)(2,1)S(1)} collective-permute-done((bf16[2,4,192,384]{3,2,1,0:T(8,128)(2,1)S(1)}, bf16[2,4,192,384]{3,2,1,0:T(8,128)(2,1)S(1)}, u32[]{:S(2)}, u32[]{:S(2)}) %collective-permute-start.29) | collective-permute-done | bytes 1179680 | tf_op jit(solution)/shard_map/back0_s3_flip/ppermute | solution.py:239
  186.4 7.8 %collective-permute-done.32.got_ref = bf16[4,512,384]{2,1,0:T(8,128)(2,1)S(1)} collective-permute-done((bf16[4,512,384]{2,1,0:T(8,128)(2,1)S(1)}, bf16[4,512,384]{2,1,0:T(8,128)(2,1)S(1)}, u32[]{:S(2)}, u32[]{:S(2)}) %collective-permute-start.32) | collective-permute-done | bytes 1572896 | tf_op jit(solution)/shard_map/grad_x/ppermute | solution.py:246
  194.8 11.5 %collective-permute-done.33.refs_3_ = bf16[4,192,384]{2,1,0:T(8,128)(2,1)S(1)} collective-permute-done((bf16[4,192,384]{2,1,0:T(8,128)(2,1)S(1)}, bf16[4,192,384]{2,1,0:T(8,128)(2,1)S(1)}, u32[]{:S(2)}, u32[]{:S(2)}) %collective-permute-start.33) | collective-permute-done | bytes 589856 | tf_op jit(solution)/shard_map/back0_x/ppermute | solution.py:246
  206.3 4.0 %owner0.1 = (bf16[1,4,4,48,1536]{4,3,2,1,0:T(8,128)(2,1)}, f32[4,4,128]{2,1,0:T(4,128)S(1)}) custom-call(s32[3]{0:T(128)S(1)} %pad_add_fusion.idx, bf16[1,4,4,48,1536]{4,3,2,1,0:T(8,128)(2,1)S(1)} %copy-done.2, bf16[4,16,256]{2,1,0:T(8,128)(2,1)S(1)} %pad_maximum_fusion.6.meta_ref, f32[2,4,192,384]{3,2,1,0:T(8,128)S(1)} %get-tuple-element.64.refs_0_, ...), custom_call_target="tpu_custom_call" | custom-call | tf_op jit(solution)/shard_map/owner0/pallas_call | solution.py:484
  (98 shorter events, 47.9 us)
Async XLA Ops:
  4.8 17.3 %collective-permute-start.1 = (bf16[4,192,384]{2,1,0:T(8,128)(2,1)}, bf16[4,192,384]{2,1,0:T(8,128)(2,1)S(1)}, u32[]{:S(2)}, u32[]{:S(2)}) collective-permute-start(bf16[4,192,384]{2,1,0:T(8,128)(2,1)} %get-tuple-element.43), channel_id=1, source_target_pairs={{0,4},{4,0},{8,12},{12,8},{16,20},{20,16},{24,28},{28,24},{1,5},{5... | collective-permute-start | bytes 1769480 | tf_op jit(solution)/shard_map/act_x/ppermute | solution.py:246
  10.5 33.9 %collective-permute-start.7 = (bf16[2,512,384]{2,1,0:T(8,128)(2,1)}, bf16[2,512,384]{2,1,0:T(8,128)(2,1)S(1)}, u32[]{:S(2)}, u32[]{:S(2)}) collective-permute-start(bf16[2,512,384]{2,1,0:T(8,128)(2,1)} %get-tuple-element.80), channel_id=1, source_target_pairs={{0,4},{4,0},{8,12},{12,8},{16,20},{20,16},{24,28},{28,24},{1,5},{5... | collective-permute-start | bytes 2359304 | tf_op jit(solution)/shard_map/weight0_x/ppermute | solution.py:246
  22.8 36.3 %collective-permute-start.10 = (bf16[4,384,384]{2,1,0:T(8,128)(2,1)S(1)}, bf16[4,384,384]{2,1,0:T(8,128)(2,1)S(1)}, u32[]{:S(2)}, u32[]{:S(2)}) collective-permute-start(bf16[4,384,384]{2,1,0:T(8,128)(2,1)S(1)} %pair.1.refs_4_), channel_id=1, source_target_pairs={{8,16},{12,20},{16,8},{20,12},{9,17},{13,21},{17,9},{21,13},{10,18... | collective-permute-start | bytes 3538952 | tf_op jit(solution)/shard_map/act_z_i3/ppermute | solution.py:239
  23.5 35.5 %collective-permute-start.2 = (bf16[4,384,384]{2,1,0:T(8,128)(2,1)S(1)}, bf16[4,384,384]{2,1,0:T(8,128)(2,1)S(1)}, u32[]{:S(2)}, u32[]{:S(2)}) collective-permute-start(bf16[4,384,384]{2,1,0:T(8,128)(2,1)S(1)} %pair.1.refs_4_), channel_id=1, source_target_pairs={{0,8},{4,12},{8,0},{12,4},{16,24},{20,28},{24,16},{28,20},{1,9},{5... | collective-permute-start | bytes 3538952 | tf_op jit(solution)/shard_map/act_z_r1/ppermute | solution.py:239
  44.5 14.6 %collective-permute-start.9 = (bf16[2,144,1024]{2,1,0:T(8,128)(2,1)S(1)}, bf16[2,144,1024]{2,1,0:T(8,128)(2,1)S(1)}, u32[]{:S(2)}, u32[]{:S(2)}) collective-permute-start(bf16[2,144,1024]{2,1,0:T(8,128)(2,1)S(1)} %pad_maximum_fusion.4), channel_id=1, source_target_pairs={{0,2},{1,3},{2,0},{3,1},{4,6},{5,7},{6,4},{7,5},{8,10},{9,11},{10,... | collective-permute-start | bytes 1769480 | tf_op jit(solution)/shard_map/rows3_expert2/ppermute | solution.py:250
  46.3 18.1 %collective-permute-start.8 = (bf16[2,512,384]{2,1,0:T(8,128)(2,1)S(1)}, bf16[2,512,384]{2,1,0:T(8,128)(2,1)S(1)}, u32[]{:S(2)}, u32[]{:S(2)}) collective-permute-start(bf16[2,512,384]{2,1,0:T(8,128)(2,1)S(1)} %copy-done.4), channel_id=1, source_target_pairs={{0,4},{4,0},{8,12},{12,8},{16,20},{20,16},{24,28},{28,24},{1,5},{5... | collective-permute-start | bytes 2359304 | tf_op jit(solution)/shard_map/weight1_x/ppermute | solution.py:246
  47.8 15.6 %collective-permute-start.11 = (bf16[2,144,1024]{2,1,0:T(8,128)(2,1)S(1)}, bf16[2,144,1024]{2,1,0:T(8,128)(2,1)S(1)}, u32[]{:S(2)}, u32[]{:S(2)}) collective-permute-start(bf16[2,144,1024]{2,1,0:T(8,128)(2,1)S(1)} %pad_maximum_fusion.4), channel_id=1, source_target_pairs={{0,1},{1,0},{2,3},{3,2},{4,5},{5,4},{6,7},{7,6},{8,9},{9,8},{10,11... | collective-permute-start | bytes 1769480 | tf_op jit(solution)/shard_map/rows3_expert1/ppermute | solution.py:250
  59.1 16.7 %collective-permute-start.6 = (bf16[144,1024]{1,0:T(8,128)(2,1)S(1)}, bf16[144,1024]{1,0:T(8,128)(2,1)S(1)}, u32[]{:S(2)}, u32[]{:S(2)}) collective-permute-start(bf16[144,1024]{1,0:T(8,128)(2,1)S(1)} %get-tuple-element.47), channel_id=1, source_target_pairs={{0,16},{4,20},{8,24},{12,28},{16,0},{20,4},{24,8},{28,12},{1,17},{... | collective-permute-start | bytes 884744 | tf_op jit(solution)/shard_map/rows2_z/ppermute | solution.py:239
  61.7 18.1 %collective-permute-start.3 = (bf16[144,1024]{1,0:T(8,128)(2,1)S(1)}, bf16[144,1024]{1,0:T(8,128)(2,1)S(1)}, u32[]{:S(2)}, u32[]{:S(2)}) collective-permute-start(bf16[144,1024]{1,0:T(8,128)(2,1)S(1)} %get-tuple-element.44), channel_id=1, source_target_pairs={{0,8},{4,12},{8,0},{12,4},{16,24},{20,28},{24,16},{28,20},{1,9},{5... | collective-permute-start | bytes 884744 | tf_op jit(solution)/shard_map/rows1_z/ppermute | solution.py:239
  77.2 27.8 %collective-permute-start.19 = (bf16[2,4,192,384]{3,2,1,0:T(8,128)(2,1)S(1)}, bf16[2,4,192,384]{3,2,1,0:T(8,128)(2,1)S(1)}, u32[]{:S(2)}, u32[]{:S(2)}) collective-permute-start(bf16[2,4,192,384]{3,2,1,0:T(8,128)(2,1)S(1)} %get-tuple-element.52), channel_id=1, source_target_pairs={{0,8},{4,12},{24,16},{28,20},{1,9},{5,13},{25,17},{29,21},{2,10},{... | collective-permute-start | bytes 3538952 | tf_op jit(solution)/shard_map/back_s1/ppermute | solution.py:239
  85.7 20.8 %collective-permute-start.23 = (bf16[4,384,384]{2,1,0:T(8,128)(2,1)S(1)}, bf16[4,384,384]{2,1,0:T(8,128)(2,1)S(1)}, u32[]{:S(2)}, u32[]{:S(2)}) collective-permute-start(bf16[4,384,384]{2,1,0:T(8,128)(2,1)S(1)} %collective-permute-done.2.refs_5_), channel_id=1, source_target_pairs={{8,16},{12,20},{16,8},{20,12},{9,17},{13,21},{17,9},{21,13},{10,18... | collective-permute-start | bytes 3538952 | tf_op jit(solution)/shard_map/act_z_i2/ppermute | solution.py:239
  86.5 13.7 %collective-permute-start.16 = (bf16[2,144,1024]{2,1,0:T(8,128)(2,1)S(1)}, bf16[2,144,1024]{2,1,0:T(8,128)(2,1)S(1)}, u32[]{:S(2)}, u32[]{:S(2)}) collective-permute-start(bf16[2,144,1024]{2,1,0:T(8,128)(2,1)S(1)} %constant_dynamic-update-slice_fusion), channel_id=1, source_target_pairs={{0,2},{1,3},{2,0},{3,1},{4,6},{5,7},{6,4},{7,5},{8,10},{9,11},{10,... | collective-permute-start | bytes 1769480 | tf_op jit(solution)/shard_map/rows2_expert2/ppermute | solution.py:250
  92.0 13.1 %collective-permute-start.15 = (bf16[2,144,1024]{2,1,0:T(8,128)(2,1)S(1)}, bf16[2,144,1024]{2,1,0:T(8,128)(2,1)S(1)}, u32[]{:S(2)}, u32[]{:S(2)}) collective-permute-start(bf16[2,144,1024]{2,1,0:T(8,128)(2,1)S(1)} %pad_maximum_fusion.5), channel_id=1, source_target_pairs={{0,4},{4,0},{8,12},{12,8},{16,20},{20,16},{24,28},{28,24},{1,5},{5... | collective-permute-start | bytes 1769480 | tf_op jit(solution)/shard_map/rows0_x/ppermute | solution.py:246
  93.5 29.6 %collective-permute-start.22 = (bf16[4,384,384]{2,1,0:T(8,128)(2,1)S(1)}, bf16[4,384,384]{2,1,0:T(8,128)(2,1)S(1)}, u32[]{:S(2)}, u32[]{:S(2)}) collective-permute-start(bf16[4,384,384]{2,1,0:T(8,128)(2,1)S(1)} %collective-permute-done.10.refs_9_), channel_id=1, source_target_pairs={{8,0},{12,4},{16,24},{20,28},{9,1},{13,5},{17,25},{21,29},{10,2},{... | collective-permute-start | bytes 3538952 | tf_op jit(solution)/shard_map/act_z_o2/ppermute | solution.py:239
  105.1 18.0 %collective-permute-start.18 = (bf16[2,144,1024]{2,1,0:T(8,128)(2,1)S(1)}, bf16[2,144,1024]{2,1,0:T(8,128)(2,1)S(1)}, u32[]{:S(2)}, u32[]{:S(2)}) collective-permute-start(bf16[2,144,1024]{2,1,0:T(8,128)(2,1)S(1)} %constant_dynamic-update-slice_fusion.2), channel_id=1, source_target_pairs={{0,2},{1,3},{2,0},{3,1},{4,6},{5,7},{6,4},{7,5},{8,10},{9,11},{10,... | collective-permute-start | bytes 1769480 | tf_op jit(solution)/shard_map/rows1_expert2/ppermute | solution.py:250
  106.6 18.2 %collective-permute-start.17 = (bf16[2,144,1024]{2,1,0:T(8,128)(2,1)S(1)}, bf16[2,144,1024]{2,1,0:T(8,128)(2,1)S(1)}, u32[]{:S(2)}, u32[]{:S(2)}) collective-permute-start(bf16[2,144,1024]{2,1,0:T(8,128)(2,1)S(1)} %constant_dynamic-update-slice_fusion.2), channel_id=1, source_target_pairs={{0,1},{1,0},{2,3},{3,2},{4,5},{5,4},{6,7},{7,6},{8,9},{9,8},{10,11... | collective-permute-start | bytes 1769480 | tf_op jit(solution)/shard_map/rows1_expert1/ppermute | solution.py:250
  106.9 39.0 %collective-permute-start.25 = (bf16[4,384,384]{2,1,0:T(8,128)(2,1)S(1)}, bf16[4,384,384]{2,1,0:T(8,128)(2,1)S(1)}, u32[]{:S(2)}, u32[]{:S(2)}) collective-permute-start(bf16[4,384,384]{2,1,0:T(8,128)(2,1)S(1)} %collective-permute-done.23.refs_7_), channel_id=1, source_target_pairs={{8,0},{12,4},{16,24},{20,28},{9,1},{13,5},{17,25},{21,29},{10,2},{... | collective-permute-start | bytes 3538952 | tf_op jit(solution)/shard_map/act_z_o3/ppermute | solution.py:239
  123.5 36.8 %collective-permute-start.28 = (bf16[2,4,192,384]{3,2,1,0:T(8,128)(2,1)S(1)}, bf16[2,4,192,384]{3,2,1,0:T(8,128)(2,1)S(1)}, u32[]{:S(2)}, u32[]{:S(2)}) collective-permute-start(bf16[2,4,192,384]{3,2,1,0:T(8,128)(2,1)S(1)} %add_convert_fusion.2), channel_id=1, source_target_pairs={{8,16},{12,20},{16,8},{20,12},{9,17},{13,21},{17,9},{21,13},{10,18... | collective-permute-start | bytes 3538952 | tf_op jit(solution)/shard_map/back_s2_mid/ppermute | solution.py:239
  124.2 21.8 %collective-permute-start.26 = (bf16[2,144,1024]{2,1,0:T(8,128)(2,1)S(1)}, bf16[2,144,1024]{2,1,0:T(8,128)(2,1)S(1)}, u32[]{:S(2)}, u32[]{:S(2)}) collective-permute-start(bf16[2,144,1024]{2,1,0:T(8,128)(2,1)S(1)} %pad_maximum_fusion.5), channel_id=1, source_target_pairs={{0,1},{1,0},{2,3},{3,2},{4,5},{5,4},{6,7},{7,6},{8,9},{9,8},{10,11... | collective-permute-start | bytes 1769480 | tf_op jit(solution)/shard_map/rows0_expert1/ppermute | solution.py:250
  125.1 20.9 %collective-permute-start.27 = (bf16[2,144,1024]{2,1,0:T(8,128)(2,1)S(1)}, bf16[2,144,1024]{2,1,0:T(8,128)(2,1)S(1)}, u32[]{:S(2)}, u32[]{:S(2)}) collective-permute-start(bf16[2,144,1024]{2,1,0:T(8,128)(2,1)S(1)} %collective-permute-done.15), channel_id=1, source_target_pairs={{0,1},{1,0},{2,3},{3,2},{4,5},{5,4},{6,7},{7,6},{8,9},{9,8},{10,11... | collective-permute-start | bytes 1769480 | tf_op jit(solution)/shard_map/rows0_expert1/ppermute | solution.py:250
  125.2 35.3 %collective-permute-start.30 = (bf16[2,4,192,384]{3,2,1,0:T(8,128)(2,1)S(1)}, bf16[2,4,192,384]{3,2,1,0:T(8,128)(2,1)S(1)}, u32[]{:S(2)}, u32[]{:S(2)}) collective-permute-start(bf16[2,4,192,384]{3,2,1,0:T(8,128)(2,1)S(1)} %add_convert_fusion.2), channel_id=1, source_target_pairs={{0,8},{4,12},{24,16},{28,20},{1,9},{5,13},{25,17},{29,21},{2,10},{... | collective-permute-start | bytes 3538952 | tf_op jit(solution)/shard_map/back_s2_in/ppermute | solution.py:239
  159.6 34.6 %collective-permute-start.32 = (bf16[4,512,384]{2,1,0:T(8,128)(2,1)S(1)}, bf16[4,512,384]{2,1,0:T(8,128)(2,1)S(1)}, u32[]{:S(2)}, u32[]{:S(2)}) collective-permute-start(bf16[4,512,384]{2,1,0:T(8,128)(2,1)S(1)} %get-tuple-element.70), channel_id=1, source_target_pairs={{0,4},{4,0},{8,12},{12,8},{16,20},{20,16},{24,28},{28,24},{1,5},{5... | collective-permute-start | bytes 4718600 | tf_op jit(solution)/shard_map/grad_x/ppermute | solution.py:246
  160.9 25.3 %collective-permute-start.29 = (bf16[2,4,192,384]{3,2,1,0:T(8,128)(2,1)S(1)}, bf16[2,4,192,384]{3,2,1,0:T(8,128)(2,1)S(1)}, u32[]{:S(2)}, u32[]{:S(2)}) collective-permute-start(bf16[2,4,192,384]{3,2,1,0:T(8,128)(2,1)S(1)} %add_convert_fusion.1), channel_id=1, source_target_pairs={{0,8},{4,12},{8,0},{12,4},{16,24},{20,28},{24,16},{28,20},{1,9},{5... | collective-permute-start | bytes 3538952 | tf_op jit(solution)/shard_map/back0_s3_flip/ppermute | solution.py:239
  161.0 25.2 %collective-permute-start.31 = (bf16[2,4,192,384]{3,2,1,0:T(8,128)(2,1)S(1)}, bf16[2,4,192,384]{3,2,1,0:T(8,128)(2,1)S(1)}, u32[]{:S(2)}, u32[]{:S(2)}) collective-permute-start(bf16[2,4,192,384]{3,2,1,0:T(8,128)(2,1)S(1)} %add_convert_fusion), channel_id=1, source_target_pairs={{8,16},{12,20},{16,8},{20,12},{9,17},{13,21},{17,9},{21,13},{10,18... | collective-permute-start | bytes 3538952 | tf_op jit(solution)/shard_map/back0_s3_mid/ppermute | solution.py:239
  (20 other events, 161.4 us)

commit v5 on v4

--- a/solution.py
+++ b/solution.py
@@ -137,34 +137,39 @@
     out_ref[0, :, pl.ds(pl.multiple_of((1 - x) * half, 128), half)] = got_ref[0]
 
 
-def last_kernel(rows, half, n_own, first, total, more, idx, saved_ref, meta_ref, *refs):
-    owns, other_ref, (pre_ref, score_ref) = refs[:n_own], refs[n_own], refs[n_own + 1 + more :]
-    x, m = idx[1], idx[2]
-    count = saved_ref.shape[2]
-    width = 2 * half
-    meta = meta_ref[0].astype(F32)
-    r = lax.broadcasted_iota(jnp.int32, (CAP, 128), 0)
-    c = lax.broadcasted_iota(jnp.int32, (CAP, 128), 1)
-    for e in range(count):
-        _, gated = spread(meta, m * total + first + e, rows)
-        gate = jnp.sum(gated, axis=1, keepdims=True)
-        score = jnp.zeros((CAP, 1), F32)
-        for mine in (True, False):
-            at = pl.multiple_of((x if mine else 1 - x) * half, 128)
-            up_at = pl.multiple_of(width + at, 128)
-            if mine:
-                back = sum(o[0, e].astype(F32) for o in owns)
-            else:
-                back = other_ref[e].astype(F32)
-            g = saved_ref[0, 0, e, :, pl.ds(at, half)].astype(F32)
-            u = saved_ref[0, 0, e, :, pl.ds(up_at, half)].astype(F32)
-            sig = lax.logistic(g)
-            silu = g * sig
-            score = score + jnp.sum(back * (silu * u), axis=1, keepdims=True)
-            grad = gate * back
-            pre_ref[0, 0, e, :, pl.ds(at, half)] = (grad * u * sig * (1.0 + g * (1.0 - sig))).astype(BF)
-            pre_ref[0, 0, e, :, pl.ds(up_at, half)] = (grad * silu).astype(BF)
-        score_ref[0, e : e + 1, :] = jnp.sum(jnp.where(r == c, score, 0.0), axis=0, keepdims=True)
+def last_kernel(rows, n_in, again, idx, gate_ref, up_ref, meta_ref, *refs):
+    ins, (pre_ref, score_ref, late) = refs[:n_in], refs[-3:]
+    count = gate_ref.shape[2]
+    m = idx[2]
+
+    @pl.when(pl.program_id(1) == 0)
+    def _():
+        r = lax.broadcasted_iota(jnp.int32, (CAP, 128), 0)
+        c = lax.broadcasted_iota(jnp.int32, (CAP, 128), 1)
+        for i in range(2):
+            meta = meta_ref[i].astype(F32)
+            at = i ^ (m % 2)
+            span = slice(i * CAP, (i + 1) * CAP)
+            for e in range(count):
+                _, gated = spread(meta, m * count + e, rows)
+                if again:
+                    back = ins[0][e, span].astype(F32)
+                else:
+                    back = sum(o[0, e, span].astype(F32) for o in ins)
+                g = gate_ref[0, at, e].astype(F32)
+                u = up_ref[0, at, e].astype(F32)
+                sig = lax.logistic(g)
+                silu = g * sig
+                score = jnp.sum(back * (silu * u), axis=1, keepdims=True)
+                grad = jnp.sum(gated, axis=1, keepdims=True) * back
+                pre_ref[0, at, e] = (grad * u * sig * (1.0 + g * (1.0 - sig))).astype(BF)
+                late[at, e] = (grad * silu).astype(BF)
+                line = jnp.sum(jnp.where(r == c, score, 0.0), axis=0, keepdims=True)
+                score_ref[i, e : e + 1, :] = line + ins[1][i, e : e + 1, :] if again else line
+
+    @pl.when(pl.program_id(1) == 1)
+    def _():
+        pre_ref[0] = late[...]
 
 
 def gate_kernel(rows, idx, ids_ref, *refs):
@@ -474,30 +479,43 @@
         return ref[i, rows:, 0 : 2 * rows]
 
     meta = jnp.stack([meta_of(jm) for jm in range(sources)])
-    own_spec = pl.BlockSpec((1, per, CAP, half), lambda j, idx: (0, 0, j, 0))
-    pre_grads = None
-    scores = []
-    for h in range(lots):
-        piece = pl.BlockSpec(
-            (1, 1, per, CAP, 2 * width), lambda j, idx, h=h: (0, idx[2] ^ j, h, 0, 0)
-        )
-        pre_grads, score = call(
-            f"owner{h}",
-            functools.partial(last_kernel, rows, half, len(owns[h]), h * per, count, h > 0),
-            (sources,),
-            [piece, pl.BlockSpec((1, META, 2 * rows), lambda j, idx: (j, 0, 0))]
-            + [own_spec] * len(owns[h])
-            + [pl.BlockSpec((per, CAP, half), lambda j, idx: (0, j, 0))]
-            + [pl.BlockSpec(memory_space=pl.ANY)] * (h > 0),
-            [piece, pl.BlockSpec((1, per, 128), lambda j, idx: (j, 0, 0))],
+    score_spec = pl.BlockSpec((2, count, 128), lambda j, p, idx: (j, 0, 0))
+
+    def owner(ins, in_specs, again, before):
+        def side(idx):
+            return 1 - idx[1] if again else idx[1]
+
+        def lanes(up):
+            return pl.BlockSpec(
+                (1, 2, count, CAP, half), lambda j, p, idx: (0, (idx[2] // 2) ^ j, 0, 0, side(idx) + 2 * up)
+            )
+
+        return call(
+            "owner_other" if again else "owner_own",
+            functools.partial(last_kernel, rows, len(ins), again),
+            (sources // 2, 2),
+            [lanes(0), lanes(1), pl.BlockSpec((2, META, 2 * rows), lambda j, p, idx: (j, 0, 0))]
+            + in_specs
+            + [pl.BlockSpec(memory_space=pl.ANY)] * len(before),
+            [
+                pl.BlockSpec(
+                    (1, 2, count, CAP, half), lambda j, p, idx: (0, (idx[2] // 2) ^ j, 0, 0, side(idx) + 2 * p)
+                ),
+                score_spec,
+            ],
             [
                 jax.ShapeDtypeStruct(saved_acts.shape, BF),
-                jax.ShapeDtypeStruct((sources, per, 128), F32),
+                jax.ShapeDtypeStruct((sources, count, 128), F32),
             ],
-            alias={len(owns[h]) + 4: 0} if h else {},
-        )(idx, saved_acts, meta, *owns[h], other[h], *([pre_grads] if h else []))
-        scores.append(score)
-    scores = jnp.concatenate(scores, axis=1)
+            [pltpu.VMEM((2, count, CAP, half), BF)],
+            alias={4 + len(ins): 0} if again else {},
+        )(idx, saved_acts, saved_acts, meta, *ins, *before)
+
+    own_spec = pl.BlockSpec((1, count, 2 * CAP, half), lambda j, p, idx: (0, 0, j, 0))
+    early, partial_scores = owner(owns[0], [own_spec] * len(owns[0]), False, [])
+    other_spec = pl.BlockSpec((count, 2 * CAP, half), lambda j, p, idx: (0, j, 0))
+    late = after(other[0], down_grad, partial_scores)
+    pre_grads, scores = owner([late, partial_scores], [other_spec, score_spec], True, [early])
     returned = [scores[0]] + [flip_m(scores[j], j, f"score{j}") for j in range(1, sources)]
     gate_grad = call(
         "gate_grad",

time: 218 us -> 217 us (level)
  waiting for transfers between devices: 115 us -> 112 us
  Pallas kernels: 41.8 us -> 44.5 us
    ppermute x9, waiting for transfers between devices: 45.6 us -> 39.8 us  [flip_x(): return lax.ppermute(v, 'dp', [(i, i ^ 1) for i in range(n_dp)])]
    pallas_call x1 -> x2, Pallas kernels: 3.99 us -> 6.72 us  [owner(): call('owner_other' if again else 'owner_own', functools.partial(last_kern...]
    ppermute x15, waiting for transfers between devices: 20.8 us -> 23.4 us  [flip_m(): return lax.ppermute(v, 'expert', [(i, i ^ k) for i in range(sources)])]
  transfers between devices with their start and end apart: 37 -> 37, of which waited for: 16 -> 18; matrix products, arithmetic and copies ran while one was open for 2% -> 2% of each run, Pallas kernels for 15% -> 17%
where the time goes in v5:
time: 217 us
  waiting for transfers between devices  112 us (52%)
  starting transfers between devices  52.5 us (24%)
  Pallas kernels  44.5 us (21%)
  local copies, waits for them, and re-layouts  5.44 us (3%)
    ppermute x13, waiting for transfers between devices, move_z(): lax.ppermute(v, 'dp', [(2 * a + i, 2 * b + i) for a, b in pairs for i in...  48.3 us
    ppermute x9, waiting for transfers between devices, flip_x(): return lax.ppermute(v, 'dp', [(i, i ^ 1) for i in range(n_dp)])  39.8 us
    ppermute x13, starting transfers between devices, move_z(): lax.ppermute(v, 'dp', [(2 * a + i, 2 * b + i) for a, b in pairs for i in...  31.7 us
    ppermute x15, waiting for transfers between devices, flip_m(): return lax.ppermute(v, 'expert', [(i, i ^ k) for i in range(sources)])  23.4 us
    pallas_call x4, Pallas kernels, route(): call(f'route{k}', functools.partial(route_kernel, rows, places[k], count,...  20.6 us
    ppermute x9, starting transfers between devices, flip_x(): return lax.ppermute(v, 'dp', [(i, i ^ 1) for i in range(n_dp)])  11.5 us
    ppermute x15, starting transfers between devices, flip_m(): return lax.ppermute(v, 'expert', [(i, i ^ k) for i in range(sources)])  9.27 us
    pallas_call x1, Pallas kernels, shards(): call('down_grad', functools.partial(grad_kernel, [len(a) for a in acts]),...  8.45 us
  transfers between devices with their start and end apart: 37, of which 18 were waited for; matrix products, arithmetic and copies ran while one was open for 2% of the time, Pallas kernels for 17%

profile of v5, /device:TPU:0, one launch (start us, length us, event | category | flops | bytes accessed | tf_op | source)
XLA Modules:
  0.0 216.9 jit_solution(1454340312541500658)
XLA Ops:
  11.6 4.1 %collective-permute-start.4 = (bf16[144,1024]{1,0:T(8,128)(2,1)S(1)}, bf16[144,1024]{1,0:T(8,128)(2,1)S(1)}, u32[]{:S(2)}, u32[]{:S(2)}) collective-permute-start(bf16[144,1024]{1,0:T(8,128)(2,1)S(1)} %get-tuple-element.49), channel_id=1, source_target_pairs={{0,24},{4,28},{8,16},{12,20},{16,8},{20,12},{24,0},{28,4},{1,25},{... | collective-permute-start | bytes 884744 | tf_op jit(solution)/shard_map/rows3_z/ppermute | solution.py:244
  15.7 6.3 %collective-permute-done.1.got_ref = bf16[4,192,384]{2,1,0:T(8,128)(2,1)S(1)} collective-permute-done((bf16[4,192,384]{2,1,0:T(8,128)(2,1)}, bf16[4,192,384]{2,1,0:T(8,128)(2,1)S(1)}, u32[]{:S(2)}, u32[]{:S(2)}) %collective-permute-start.1) | collective-permute-done | bytes 589856 | tf_op jit(solution)/shard_map/act_x/ppermute | solution.py:251
  23.5 8.2 %collective-permute-start.2 = (bf16[4,384,384]{2,1,0:T(8,128)(2,1)S(1)}, bf16[4,384,384]{2,1,0:T(8,128)(2,1)S(1)}, u32[]{:S(2)}, u32[]{:S(2)}) collective-permute-start(bf16[4,384,384]{2,1,0:T(8,128)(2,1)S(1)} %pair.1.refs_4_), channel_id=1, source_target_pairs={{0,8},{4,12},{8,0},{12,4},{16,24},{20,28},{24,16},{28,20},{1,9},{5... | collective-permute-start | bytes 3538952 | tf_op jit(solution)/shard_map/act_z_r1/ppermute | solution.py:244
  34.8 3.7 %collective-permute-done = bf16[1,144,1024]{2,1,0:T(8,128)(2,1)S(1)} collective-permute-done((bf16[1,144,1024]{2,1,0:T(8,128)(2,1)S(1)}, bf16[1,144,1024]{2,1,0:T(8,128)(2,1)S(1)}, u32[]{:S(2)}, u32[]{:S(2)}) %collective-permute-start) | collective-permute-done | bytes 294944 | tf_op jit(solution)/shard_map/rows0_expert2/ppermute | solution.py:255
  38.5 5.9 %collective-permute-done.5 = bf16[1,144,1024]{2,1,0:T(8,128)(2,1)S(1)} collective-permute-done((bf16[1,144,1024]{2,1,0:T(8,128)(2,1)S(1)}, bf16[1,144,1024]{2,1,0:T(8,128)(2,1)S(1)}, u32[]{:S(2)}, u32[]{:S(2)}) %collective-permute-start.5) | collective-permute-done | bytes 294944 | tf_op jit(solution)/shard_map/rows3_x/ppermute | solution.py:251
  47.8 11.2 %collective-permute-done.9 = bf16[2,144,1024]{2,1,0:T(8,128)(2,1)S(1)} collective-permute-done((bf16[2,144,1024]{2,1,0:T(8,128)(2,1)S(1)}, bf16[2,144,1024]{2,1,0:T(8,128)(2,1)S(1)}, u32[]{:S(2)}, u32[]{:S(2)}) %collective-permute-start.9) | collective-permute-done | bytes 589856 | tf_op jit(solution)/shard_map/rows3_expert2/ppermute | solution.py:255
  64.4 5.1 %route3.1 = (bf16[2,4,192,384]{3,2,1,0:T(8,128)(2,1)S(1)}, bf16[4,384,1024]{2,1,0:T(8,128)(2,1)S(1)}) custom-call(s32[3]{0:T(128)S(1)} %pad_add_fusion.idx, bf16[4,144,1024]{2,1,0:T(8,128)(2,1)S(1)} %pad_maximum_fusion.a_ref, bf16[2,144,1024]{2,1,0:T(8,128)(2,1)S(1)} %collective-permute-done.11.b_ref, ...), custom_call_target="tpu_custom_call" | custom-call | tf_op jit(solution)/shard_map/route3/pallas_call | solution.py:303
  69.6 6.2 %collective-permute-done.6 = bf16[144,1024]{1,0:T(8,128)(2,1)S(1)} collective-permute-done((bf16[144,1024]{1,0:T(8,128)(2,1)S(1)}, bf16[144,1024]{1,0:T(8,128)(2,1)S(1)}, u32[]{:S(2)}, u32[]{:S(2)}) %collective-permute-start.6) | collective-permute-done | bytes 294944 | tf_op jit(solution)/shard_map/rows2_z/ppermute | solution.py:244
  79.8 4.5 %collective-permute-done.13 = bf16[1,144,1024]{2,1,0:T(8,128)(2,1)S(1)} collective-permute-done((bf16[1,144,1024]{2,1,0:T(8,128)(2,1)S(1)}, bf16[1,144,1024]{2,1,0:T(8,128)(2,1)S(1)}, u32[]{:S(2)}, u32[]{:S(2)}) %collective-permute-start.13) | collective-permute-done | bytes 294944 | tf_op jit(solution)/shard_map/rows2_x/ppermute | solution.py:251
  88.1 3.8 %collective-permute-done.14 = bf16[1,144,1024]{2,1,0:T(8,128)(2,1)S(1)} collective-permute-done((bf16[1,144,1024]{2,1,0:T(8,128)(2,1)S(1)}, bf16[1,144,1024]{2,1,0:T(8,128)(2,1)S(1)}, u32[]{:S(2)}, u32[]{:S(2)}) %collective-permute-start.14) | collective-permute-done | bytes 294944 | tf_op jit(solution)/shard_map/rows1_x/ppermute | solution.py:251
  94.8 5.5 %collective-permute-done.16 = bf16[2,144,1024]{2,1,0:T(8,128)(2,1)S(1)} collective-permute-done((bf16[2,144,1024]{2,1,0:T(8,128)(2,1)S(1)}, bf16[2,144,1024]{2,1,0:T(8,128)(2,1)S(1)}, u32[]{:S(2)}, u32[]{:S(2)}) %collective-permute-start.16) | collective-permute-done | bytes 589856 | tf_op jit(solution)/shard_map/rows2_expert2/ppermute | solution.py:255
  100.2 4.8 %collective-permute-done.15 = bf16[2,144,1024]{2,1,0:T(8,128)(2,1)S(1)} collective-permute-done((bf16[2,144,1024]{2,1,0:T(8,128)(2,1)S(1)}, bf16[2,144,1024]{2,1,0:T(8,128)(2,1)S(1)}, u32[]{:S(2)}, u32[]{:S(2)}) %collective-permute-start.15) | collective-permute-done | bytes 589856 | tf_op jit(solution)/shard_map/rows0_x/ppermute | solution.py:251
  108.2 5.1 %route2.1 = (f32[2,4,192,384]{3,2,1,0:T(8,128)S(1)}, bf16[4,384,1024]{2,1,0:T(8,128)(2,1)S(1)}) custom-call(s32[3]{0:T(128)S(1)} %pad_add_fusion.idx, bf16[4,144,1024]{2,1,0:T(8,128)(2,1)S(1)} %pad_maximum_fusion.1.a_ref, bf16[2,144,1024]{2,1,0:T(8,128)(2,1)S(1)} %collective-permute-done.20.b_ref, bf16[2,144,1024]{2,1,0:T(8,128)(2,1)S(1)} %collective-permute-done.21.c_ref, ...), custom_call_target="tpu_custom_call" | custom-call | tf_op jit(solution)/shard_map/route2/pallas_call | solution.py:303
  113.4 9.7 %collective-permute-done.22.refs_6_ = bf16[4,384,384]{2,1,0:T(8,128)(2,1)S(1)} collective-permute-done((bf16[4,384,384]{2,1,0:T(8,128)(2,1)S(1)}, bf16[4,384,384]{2,1,0:T(8,128)(2,1)S(1)}, u32[]{:S(2)}, u32[]{:S(2)}) %collective-permute-start.22) | collective-permute-done | bytes 1179680 | tf_op jit(solution)/shard_map/act_z_o2/ppermute | solution.py:244
  125.2 6.9 %collective-permute-start.30 = (bf16[2,4,192,384]{3,2,1,0:T(8,128)(2,1)S(1)}, bf16[2,4,192,384]{3,2,1,0:T(8,128)(2,1)S(1)}, u32[]{:S(2)}, u32[]{:S(2)}) collective-permute-start(bf16[2,4,192,384]{3,2,1,0:T(8,128)(2,1)S(1)} %add_convert_fusion.2), channel_id=1, source_target_pairs={{0,8},{4,12},{24,16},{28,20},{1,9},{5,13},{25,17},{29,21},{2,10},{... | collective-permute-start | bytes 3538952 | tf_op jit(solution)/shard_map/back_s2_in/ppermute | solution.py:244
  132.2 5.1 %route1.1 = (f32[2,4,192,384]{3,2,1,0:T(8,128)S(1)}, bf16[4,384,1024]{2,1,0:T(8,128)(2,1)S(1)}) custom-call(s32[3]{0:T(128)S(1)} %pad_add_fusion.idx, bf16[4,144,1024]{2,1,0:T(8,128)(2,1)S(1)} %pad_maximum_fusion.3.a_ref, bf16[2,144,1024]{2,1,0:T(8,128)(2,1)S(1)} %collective-permute-done.17.b_ref, bf16[2,144,1024]{2,1,0:T(8,128)(2,1)S(1)} %collective-permute-done.24.c_ref, ...), custom_call_target="tpu_custom_call" | custom-call | tf_op jit(solution)/shard_map/route1/pallas_call | solution.py:303
  137.5 8.5 %collective-permute-done.25.refs_8_ = bf16[4,384,384]{2,1,0:T(8,128)(2,1)S(1)} collective-permute-done((bf16[4,384,384]{2,1,0:T(8,128)(2,1)S(1)}, bf16[4,384,384]{2,1,0:T(8,128)(2,1)S(1)}, u32[]{:S(2)}, u32[]{:S(2)}) %collective-permute-start.25) | collective-permute-done | bytes 1179680 | tf_op jit(solution)/shard_map/act_z_o3/ppermute | solution.py:244
  146.0 5.1 %route0.1 = (f32[2,4,192,384]{3,2,1,0:T(8,128)S(1)}, bf16[4,384,1024]{2,1,0:T(8,128)(2,1)S(1)}) custom-call(s32[3]{0:T(128)S(1)} %pad_add_fusion.idx, bf16[4,144,1024]{2,1,0:T(8,128)(2,1)S(1)} %pad_maximum_fusion.2.a_ref, bf16[2,144,1024]{2,1,0:T(8,128)(2,1)S(1)} %collective-permute-done.26.b_ref, bf16[2,144,1024]{2,1,0:T(8,128)(2,1)S(1)} %collective-permute-done.27.c_ref, ...), custom_call_target="tpu_custom_call" | custom-call | tf_op jit(solution)/shard_map/route0/pallas_call | solution.py:303
  151.1 8.4 %down_grad.1 = (bf16[4,512,384]{2,1,0:T(8,128)(2,1)S(1)}, bf16[4,512,384]{2,1,0:T(8,128)(2,1)S(1)}) custom-call(s32[3]{0:T(128)S(1)} %pad_add_fusion.idx, bf16[4,384,1024]{2,1,0:T(8,128)(2,1)S(1)} %get-tuple-element.69.refs_0_, bf16[4,384,1024]{2,1,0:T(8,128)(2,1)S(1)} %get-tuple-element.70.refs_1_, bf16[4,384,1024]{2,1,0:T(8,128)(2,1)S(1)} %get-tuple-element.71.refs_2_, ...), custom_call_target="tpu_custom_call" | custom-call | flops 4831838208 | bytes 19660800 | tf_op jit(solution)/shard_map/down_grad/pallas_call | solution.py:435
  161.9 24.0 %collective-permute-done.29.refs_1_ = bf16[2,4,192,384]{3,2,1,0:T(8,128)(2,1)S(1)} collective-permute-done((bf16[2,4,192,384]{3,2,1,0:T(8,128)(2,1)S(1)}, bf16[2,4,192,384]{3,2,1,0:T(8,128)(2,1)S(1)}, u32[]{:S(2)}, u32[]{:S(2)}) %collective-permute-start.29) | collective-permute-done | bytes 1179680 | tf_op jit(solution)/shard_map/back0_s3_flip/ppermute | solution.py:244
  186.1 8.1 %collective-permute-done.32.got_ref = bf16[4,512,384]{2,1,0:T(8,128)(2,1)S(1)} collective-permute-done((bf16[4,512,384]{2,1,0:T(8,128)(2,1)S(1)}, bf16[4,512,384]{2,1,0:T(8,128)(2,1)S(1)}, u32[]{:S(2)}, u32[]{:S(2)}) %collective-permute-start.32) | collective-permute-done | bytes 1572896 | tf_op jit(solution)/shard_map/grad_x/ppermute | solution.py:251
  194.8 3.4 %owner_own.1 = (bf16[1,4,4,48,1536]{4,3,2,1,0:T(8,128)(2,1)}, f32[4,4,128]{2,1,0:T(4,128)S(1)}) custom-call(s32[3]{0:T(128)S(1)} %pad_add_fusion.idx, bf16[1,4,4,48,1536]{4,3,2,1,0:T(8,128)(2,1)S(1)} %copy-done.2, bf16[1,4,4,48,1536]{4,3,2,1,0:T(8,128)(2,1)S(1)} %copy-done.2, bf16[4,16,256]{2,1,0:T(8,128)(2,1)S(1)} %pad_maximum_fusion.6.meta_ref, ...), custom_call_target="tpu_custom_call" | custom-call | tf_op jit(solution)/shard_map/owner_own/pallas_call | solution.py:493
  201.0 5.3 %collective-permute-done.33.refs_0_ = bf16[4,192,384]{2,1,0:T(8,128)(2,1)S(1)} collective-permute-done((bf16[4,192,384]{2,1,0:T(8,128)(2,1)S(1)}, bf16[4,192,384]{2,1,0:T(8,128)(2,1)S(1)}, u32[]{:S(2)}, u32[]{:S(2)}) %collective-permute-start.33) | collective-permute-done | bytes 589856 | tf_op jit(solution)/shard_map/back0_x/ppermute | solution.py:251
  206.3 3.3 %owner_other.1 = (bf16[1,4,4,48,1536]{4,3,2,1,0:T(8,128)(2,1)}, f32[4,4,128]{2,1,0:T(4,128)S(1)}) custom-call(s32[3]{0:T(128)S(1)} %pad_add_fusion.idx, bf16[1,4,4,48,1536]{4,3,2,1,0:T(8,128)(2,1)S(1)} %copy-done.2, bf16[1,4,4,48,1536]{4,3,2,1,0:T(8,128)(2,1)S(1)} %copy-done.2, ...), custom_call_target="tpu_custom_call", output_to_operand_aliasing={{0}: (6, {})} | custom-call | tf_op jit(solution)/shard_map/owner_other/pallas_call | solution.py:493
  (99 shorter events, 53.5 us)
Async XLA Ops:
  4.7 17.3 %collective-permute-start.1 = (bf16[4,192,384]{2,1,0:T(8,128)(2,1)}, bf16[4,192,384]{2,1,0:T(8,128)(2,1)S(1)}, u32[]{:S(2)}, u32[]{:S(2)}) collective-permute-start(bf16[4,192,384]{2,1,0:T(8,128)(2,1)} %get-tuple-element.46), channel_id=1, source_target_pairs={{0,4},{4,0},{8,12},{12,8},{16,20},{20,16},{24,28},{28,24},{1,5},{5... | collective-permute-start | bytes 1769480 | tf_op jit(solution)/shard_map/act_x/ppermute | solution.py:251
  10.4 33.9 %collective-permute-start.7 = (bf16[2,512,384]{2,1,0:T(8,128)(2,1)}, bf16[2,512,384]{2,1,0:T(8,128)(2,1)S(1)}, u32[]{:S(2)}, u32[]{:S(2)}) collective-permute-start(bf16[2,512,384]{2,1,0:T(8,128)(2,1)} %get-tuple-element.86), channel_id=1, source_target_pairs={{0,4},{4,0},{8,12},{12,8},{16,20},{20,16},{24,28},{28,24},{1,5},{5... | collective-permute-start | bytes 2359304 | tf_op jit(solution)/shard_map/weight0_x/ppermute | solution.py:251
  22.8 36.3 %collective-permute-start.10 = (bf16[4,384,384]{2,1,0:T(8,128)(2,1)S(1)}, bf16[4,384,384]{2,1,0:T(8,128)(2,1)S(1)}, u32[]{:S(2)}, u32[]{:S(2)}) collective-permute-start(bf16[4,384,384]{2,1,0:T(8,128)(2,1)S(1)} %pair.1.refs_4_), channel_id=1, source_target_pairs={{8,16},{12,20},{16,8},{20,12},{9,17},{13,21},{17,9},{21,13},{10,18... | collective-permute-start | bytes 3538952 | tf_op jit(solution)/shard_map/act_z_i3/ppermute | solution.py:244
  23.5 35.5 %collective-permute-start.2 = (bf16[4,384,384]{2,1,0:T(8,128)(2,1)S(1)}, bf16[4,384,384]{2,1,0:T(8,128)(2,1)S(1)}, u32[]{:S(2)}, u32[]{:S(2)}) collective-permute-start(bf16[4,384,384]{2,1,0:T(8,128)(2,1)S(1)} %pair.1.refs_4_), channel_id=1, source_target_pairs={{0,8},{4,12},{8,0},{12,4},{16,24},{20,28},{24,16},{28,20},{1,9},{5... | collective-permute-start | bytes 3538952 | tf_op jit(solution)/shard_map/act_z_r1/ppermute | solution.py:244
  44.5 14.6 %collective-permute-start.9 = (bf16[2,144,1024]{2,1,0:T(8,128)(2,1)S(1)}, bf16[2,144,1024]{2,1,0:T(8,128)(2,1)S(1)}, u32[]{:S(2)}, u32[]{:S(2)}) collective-permute-start(bf16[2,144,1024]{2,1,0:T(8,128)(2,1)S(1)} %pad_maximum_fusion.4), channel_id=1, source_target_pairs={{0,2},{1,3},{2,0},{3,1},{4,6},{5,7},{6,4},{7,5},{8,10},{9,11},{10,... | collective-permute-start | bytes 1769480 | tf_op jit(solution)/shard_map/rows3_expert2/ppermute | solution.py:255
  46.3 18.1 %collective-permute-start.8 = (bf16[2,512,384]{2,1,0:T(8,128)(2,1)S(1)}, bf16[2,512,384]{2,1,0:T(8,128)(2,1)S(1)}, u32[]{:S(2)}, u32[]{:S(2)}) collective-permute-start(bf16[2,512,384]{2,1,0:T(8,128)(2,1)S(1)} %copy-done.4), channel_id=1, source_target_pairs={{0,4},{4,0},{8,12},{12,8},{16,20},{20,16},{24,28},{28,24},{1,5},{5... | collective-permute-start | bytes 2359304 | tf_op jit(solution)/shard_map/weight1_x/ppermute | solution.py:251
  47.8 15.6 %collective-permute-start.11 = (bf16[2,144,1024]{2,1,0:T(8,128)(2,1)S(1)}, bf16[2,144,1024]{2,1,0:T(8,128)(2,1)S(1)}, u32[]{:S(2)}, u32[]{:S(2)}) collective-permute-start(bf16[2,144,1024]{2,1,0:T(8,128)(2,1)S(1)} %pad_maximum_fusion.4), channel_id=1, source_target_pairs={{0,1},{1,0},{2,3},{3,2},{4,5},{5,4},{6,7},{7,6},{8,9},{9,8},{10,11... | collective-permute-start | bytes 1769480 | tf_op jit(solution)/shard_map/rows3_expert1/ppermute | solution.py:255
  59.1 16.7 %collective-permute-start.6 = (bf16[144,1024]{1,0:T(8,128)(2,1)S(1)}, bf16[144,1024]{1,0:T(8,128)(2,1)S(1)}, u32[]{:S(2)}, u32[]{:S(2)}) collective-permute-start(bf16[144,1024]{1,0:T(8,128)(2,1)S(1)} %get-tuple-element.50), channel_id=1, source_target_pairs={{0,16},{4,20},{8,24},{12,28},{16,0},{20,4},{24,8},{28,12},{1,17},{... | collective-permute-start | bytes 884744 | tf_op jit(solution)/shard_map/rows2_z/ppermute | solution.py:244
  61.6 18.1 %collective-permute-start.3 = (bf16[144,1024]{1,0:T(8,128)(2,1)S(1)}, bf16[144,1024]{1,0:T(8,128)(2,1)S(1)}, u32[]{:S(2)}, u32[]{:S(2)}) collective-permute-start(bf16[144,1024]{1,0:T(8,128)(2,1)S(1)} %get-tuple-element.47), channel_id=1, source_target_pairs={{0,8},{4,12},{8,0},{12,4},{16,24},{20,28},{24,16},{28,20},{1,9},{5... | collective-permute-start | bytes 884744 | tf_op jit(solution)/shard_map/rows1_z/ppermute | solution.py:244
  77.2 27.8 %collective-permute-start.19 = (bf16[2,4,192,384]{3,2,1,0:T(8,128)(2,1)S(1)}, bf16[2,4,192,384]{3,2,1,0:T(8,128)(2,1)S(1)}, u32[]{:S(2)}, u32[]{:S(2)}) collective-permute-start(bf16[2,4,192,384]{3,2,1,0:T(8,128)(2,1)S(1)} %get-tuple-element.55), channel_id=1, source_target_pairs={{0,8},{4,12},{24,16},{28,20},{1,9},{5,13},{25,17},{29,21},{2,10},{... | collective-permute-start | bytes 3538952 | tf_op jit(solution)/shard_map/back_s1/ppermute | solution.py:244
  85.7 20.8 %collective-permute-start.23 = (bf16[4,384,384]{2,1,0:T(8,128)(2,1)S(1)}, bf16[4,384,384]{2,1,0:T(8,128)(2,1)S(1)}, u32[]{:S(2)}, u32[]{:S(2)}) collective-permute-start(bf16[4,384,384]{2,1,0:T(8,128)(2,1)S(1)} %collective-permute-done.2.refs_5_), channel_id=1, source_target_pairs={{8,16},{12,20},{16,8},{20,12},{9,17},{13,21},{17,9},{21,13},{10,18... | collective-permute-start | bytes 3538952 | tf_op jit(solution)/shard_map/act_z_i2/ppermute | solution.py:244
  86.5 13.7 %collective-permute-start.16 = (bf16[2,144,1024]{2,1,0:T(8,128)(2,1)S(1)}, bf16[2,144,1024]{2,1,0:T(8,128)(2,1)S(1)}, u32[]{:S(2)}, u32[]{:S(2)}) collective-permute-start(bf16[2,144,1024]{2,1,0:T(8,128)(2,1)S(1)} %constant_dynamic-update-slice_fusion), channel_id=1, source_target_pairs={{0,2},{1,3},{2,0},{3,1},{4,6},{5,7},{6,4},{7,5},{8,10},{9,11},{10,... | collective-permute-start | bytes 1769480 | tf_op jit(solution)/shard_map/rows2_expert2/ppermute | solution.py:255
  92.0 13.1 %collective-permute-start.15 = (bf16[2,144,1024]{2,1,0:T(8,128)(2,1)S(1)}, bf16[2,144,1024]{2,1,0:T(8,128)(2,1)S(1)}, u32[]{:S(2)}, u32[]{:S(2)}) collective-permute-start(bf16[2,144,1024]{2,1,0:T(8,128)(2,1)S(1)} %pad_maximum_fusion.5), channel_id=1, source_target_pairs={{0,4},{4,0},{8,12},{12,8},{16,20},{20,16},{24,28},{28,24},{1,5},{5... | collective-permute-start | bytes 1769480 | tf_op jit(solution)/shard_map/rows0_x/ppermute | solution.py:251
  93.4 29.6 %collective-permute-start.22 = (bf16[4,384,384]{2,1,0:T(8,128)(2,1)S(1)}, bf16[4,384,384]{2,1,0:T(8,128)(2,1)S(1)}, u32[]{:S(2)}, u32[]{:S(2)}) collective-permute-start(bf16[4,384,384]{2,1,0:T(8,128)(2,1)S(1)} %collective-permute-done.10.refs_9_), channel_id=1, source_target_pairs={{8,0},{12,4},{16,24},{20,28},{9,1},{13,5},{17,25},{21,29},{10,2},{... | collective-permute-start | bytes 3538952 | tf_op jit(solution)/shard_map/act_z_o2/ppermute | solution.py:244
  105.0 18.0 %collective-permute-start.18 = (bf16[2,144,1024]{2,1,0:T(8,128)(2,1)S(1)}, bf16[2,144,1024]{2,1,0:T(8,128)(2,1)S(1)}, u32[]{:S(2)}, u32[]{:S(2)}) collective-permute-start(bf16[2,144,1024]{2,1,0:T(8,128)(2,1)S(1)} %constant_dynamic-update-slice_fusion.2), channel_id=1, source_target_pairs={{0,2},{1,3},{2,0},{3,1},{4,6},{5,7},{6,4},{7,5},{8,10},{9,11},{10,... | collective-permute-start | bytes 1769480 | tf_op jit(solution)/shard_map/rows1_expert2/ppermute | solution.py:255
  106.6 18.2 %collective-permute-start.17 = (bf16[2,144,1024]{2,1,0:T(8,128)(2,1)S(1)}, bf16[2,144,1024]{2,1,0:T(8,128)(2,1)S(1)}, u32[]{:S(2)}, u32[]{:S(2)}) collective-permute-start(bf16[2,144,1024]{2,1,0:T(8,128)(2,1)S(1)} %constant_dynamic-update-slice_fusion.2), channel_id=1, source_target_pairs={{0,1},{1,0},{2,3},{3,2},{4,5},{5,4},{6,7},{7,6},{8,9},{9,8},{10,11... | collective-permute-start | bytes 1769480 | tf_op jit(solution)/shard_map/rows1_expert1/ppermute | solution.py:255
  106.9 39.0 %collective-permute-start.25 = (bf16[4,384,384]{2,1,0:T(8,128)(2,1)S(1)}, bf16[4,384,384]{2,1,0:T(8,128)(2,1)S(1)}, u32[]{:S(2)}, u32[]{:S(2)}) collective-permute-start(bf16[4,384,384]{2,1,0:T(8,128)(2,1)S(1)} %collective-permute-done.23.refs_7_), channel_id=1, source_target_pairs={{8,0},{12,4},{16,24},{20,28},{9,1},{13,5},{17,25},{21,29},{10,2},{... | collective-permute-start | bytes 3538952 | tf_op jit(solution)/shard_map/act_z_o3/ppermute | solution.py:244
  123.4 36.8 %collective-permute-start.28 = (bf16[2,4,192,384]{3,2,1,0:T(8,128)(2,1)S(1)}, bf16[2,4,192,384]{3,2,1,0:T(8,128)(2,1)S(1)}, u32[]{:S(2)}, u32[]{:S(2)}) collective-permute-start(bf16[2,4,192,384]{3,2,1,0:T(8,128)(2,1)S(1)} %add_convert_fusion.2), channel_id=1, source_target_pairs={{8,16},{12,20},{16,8},{20,12},{9,17},{13,21},{17,9},{21,13},{10,18... | collective-permute-start | bytes 3538952 | tf_op jit(solution)/shard_map/back_s2_mid/ppermute | solution.py:244
  124.2 21.8 %collective-permute-start.26 = (bf16[2,144,1024]{2,1,0:T(8,128)(2,1)S(1)}, bf16[2,144,1024]{2,1,0:T(8,128)(2,1)S(1)}, u32[]{:S(2)}, u32[]{:S(2)}) collective-permute-start(bf16[2,144,1024]{2,1,0:T(8,128)(2,1)S(1)} %pad_maximum_fusion.5), channel_id=1, source_target_pairs={{0,1},{1,0},{2,3},{3,2},{4,5},{5,4},{6,7},{7,6},{8,9},{9,8},{10,11... | collective-permute-start | bytes 1769480 | tf_op jit(solution)/shard_map/rows0_expert1/ppermute | solution.py:255
  125.1 20.9 %collective-permute-start.27 = (bf16[2,144,1024]{2,1,0:T(8,128)(2,1)S(1)}, bf16[2,144,1024]{2,1,0:T(8,128)(2,1)S(1)}, u32[]{:S(2)}, u32[]{:S(2)}) collective-permute-start(bf16[2,144,1024]{2,1,0:T(8,128)(2,1)S(1)} %collective-permute-done.15), channel_id=1, source_target_pairs={{0,1},{1,0},{2,3},{3,2},{4,5},{5,4},{6,7},{7,6},{8,9},{9,8},{10,11... | collective-permute-start | bytes 1769480 | tf_op jit(solution)/shard_map/rows0_expert1/ppermute | solution.py:255
  125.2 35.4 %collective-permute-start.30 = (bf16[2,4,192,384]{3,2,1,0:T(8,128)(2,1)S(1)}, bf16[2,4,192,384]{3,2,1,0:T(8,128)(2,1)S(1)}, u32[]{:S(2)}, u32[]{:S(2)}) collective-permute-start(bf16[2,4,192,384]{3,2,1,0:T(8,128)(2,1)S(1)} %add_convert_fusion.2), channel_id=1, source_target_pairs={{0,8},{4,12},{24,16},{28,20},{1,9},{5,13},{25,17},{29,21},{2,10},{... | collective-permute-start | bytes 3538952 | tf_op jit(solution)/shard_map/back_s2_in/ppermute | solution.py:244
  159.6 34.6 %collective-permute-start.32 = (bf16[4,512,384]{2,1,0:T(8,128)(2,1)S(1)}, bf16[4,512,384]{2,1,0:T(8,128)(2,1)S(1)}, u32[]{:S(2)}, u32[]{:S(2)}) collective-permute-start(bf16[4,512,384]{2,1,0:T(8,128)(2,1)S(1)} %get-tuple-element.73), channel_id=1, source_target_pairs={{0,4},{4,0},{8,12},{12,8},{16,20},{20,16},{24,28},{28,24},{1,5},{5... | collective-permute-start | bytes 4718600 | tf_op jit(solution)/shard_map/grad_x/ppermute | solution.py:251
  160.5 25.3 %collective-permute-start.29 = (bf16[2,4,192,384]{3,2,1,0:T(8,128)(2,1)S(1)}, bf16[2,4,192,384]{3,2,1,0:T(8,128)(2,1)S(1)}, u32[]{:S(2)}, u32[]{:S(2)}) collective-permute-start(bf16[2,4,192,384]{3,2,1,0:T(8,128)(2,1)S(1)} %add_convert_fusion.1), channel_id=1, source_target_pairs={{0,8},{4,12},{8,0},{12,4},{16,24},{20,28},{24,16},{28,20},{1,9},{5... | collective-permute-start | bytes 3538952 | tf_op jit(solution)/shard_map/back0_s3_flip/ppermute | solution.py:244
  161.0 24.9 %collective-permute-start.31 = (bf16[2,4,192,384]{3,2,1,0:T(8,128)(2,1)S(1)}, bf16[2,4,192,384]{3,2,1,0:T(8,128)(2,1)S(1)}, u32[]{:S(2)}, u32[]{:S(2)}) collective-permute-start(bf16[2,4,192,384]{3,2,1,0:T(8,128)(2,1)S(1)} %add_convert_fusion), channel_id=1, source_target_pairs={{8,16},{12,20},{16,8},{20,12},{9,17},{13,21},{17,9},{21,13},{10,18... | collective-permute-start | bytes 3538952 | tf_op jit(solution)/shard_map/back0_s3_mid/ppermute | solution.py:244
  (20 other events, 146.6 us)
